TPU v7x, 128 devices: a whole 4x4x4 slice. The times are simulated.
128 devices in a mesh: owner: 32 (over z, y, core), head: 4 (over x).
Axes of the slice: x: 4, y: 4, z: 4, core: 2. Of those that a mesh axis runs over, the one named last changes fastest.
Arguments:
- nodes: bfloat16 [65536, 768], P('owner'), may hold values from -6 to 6
- qkv_weight: bfloat16 [3, 768, 768], P(None, None, 'head'), may hold values from -12 to 12
- out_weight: bfloat16 [768, 768], replicated, may hold values from -0.6484375 to 0.6484375
- hop_bias: float32 [32, 24], P(None, 'head'), may hold values from -4 to 4
- up_weight: bfloat16 [768, 3072], replicated, may hold values from -0.21875 to 0.21875
- down_weight: bfloat16 [3072, 768], replicated, may hold values from -0.109375 to 0.109375
- key_owner: int32 [1024, 1], replicated, may hold values from 0 to 31; in each aligned block of 32 rows (0 to 31, 32 to 63, ...) at most 2 rows name the same one
- key_local: int32 [1024], replicated, may hold values from 0 to 7
- query_owner: int32 [1024, 1], replicated, may hold values from 0 to 31; in each aligned block of 32 rows (0 to 31, 32 to 63, ...) at most 2 rows name the same one
- query_local: int32 [1024], replicated, may hold values from 0 to 7
- hop_bucket: int32 [1024], P('owner'), may hold values from 0 to 31
Outputs:
- layer_out: bfloat16 [65536, 768], P('owner', 'head')
Inputs may be any that keep to these rules, and one draw needn't show every extreme that they name: `key_owner`: among the 32 tiles of one worker (rows w * 32 to (w + 1) * 32 - 1) no owner is named more than 2 times; every draw has workers that name some owner exactly 2 times. `query_owner`: among the 32 tiles of one worker no owner is named more than 2 times; every draw has workers that name some owner exactly 2 times.
All inputs are finite; a program needn't handle non-finite values.
Results may differ from a plain program's by a relative error of at most 0.0099.
Values may be sent and summed in bfloat16 or wider, within the bound.
A program may use at most 192 MiB of HBM per device.

v0:
```python
import math

import jax
import jax.numpy as jnp
from jax import lax
from jax.sharding import PartitionSpec as P

CSIZE = 256
KEY_CAP = 2
QUERY_CAP = 2


EPSILON = 1e-05


def norm_rows(values):
    center = values - jnp.mean(values, axis=-1, keepdims=True)
    spread = jnp.mean(center * center, axis=-1, keepdims=True)
    return center * lax.rsqrt(spread + EPSILON)


def tile_partial(query_block, pair_block, bias_rows):
    batch, length, feature_count = query_block.shape
    head_count = bias_rows.shape[1]
    head_size = feature_count // head_count
    scale = 1.0 / math.sqrt(head_size)
    queries = query_block.reshape(batch, length, head_count, head_size)
    keys = pair_block[..., :feature_count].reshape(batch, length, head_count, head_size)
    values = pair_block[..., feature_count:].reshape(batch, length, head_count, head_size)
    scores = (
        jnp.einsum("bqhd,bkhd->bhqk", queries, keys, preferred_element_type=jnp.float32) * scale
        + bias_rows[:, :, None, None]
    )
    highest = jnp.max(scores, axis=-1)
    expo = jnp.exp(scores - highest[..., None])
    totals = jnp.sum(expo, axis=-1)
    weights = expo.astype(jnp.bfloat16)
    mixed = jnp.einsum("bhqk,bkhd->bqhd", weights, values, preferred_element_type=jnp.float32)
    partial_value = mixed / jnp.transpose(totals, (0, 2, 1))[..., None]
    return (highest + jnp.log(totals), partial_value.reshape(batch, length, feature_count))


def slot_rank(owner_list, workers):
    owners = owner_list.reshape(workers, -1)
    places = jnp.arange(owners.shape[1], dtype=jnp.int32)
    matching = (owners[:, :, None] == owners[:, None, :]) & (
        places[None, None, :] < places[None, :, None]
    )
    return (owners, jnp.sum(matching.astype(jnp.int32), axis=2))


def slot_pick(owners, ranks, target, capacity, values):
    slots = jnp.arange(capacity, dtype=jnp.int32)
    chosen = ((owners == target)[:, :, None] & (ranks[:, :, None] == slots[None, None, :])).astype(
        jnp.int32
    )
    return (jnp.sum(chosen * values[:, :, None], axis=1), jnp.sum(chosen, axis=1) > 0)


def per_device(
    nodes,
    qkv_weight,
    out_weight,
    hop_bias,
    up_weight,
    down_weight,
    key_owner,
    key_local,
    query_owner,
    query_local,
    hop_bucket,
):
    workers = lax.axis_size("owner")
    myself = lax.axis_index("owner")
    row_count, model_width = nodes.shape
    feature_count = qkv_weight.shape[2]
    groups = hop_bias.shape[1]
    head_size = feature_count // groups
    clusters = row_count // CSIZE
    tile_count = hop_bucket.shape[0]
    normed = norm_rows(nodes.astype(jnp.float32)).astype(jnp.bfloat16)
    projected = jnp.einsum(
        "rd,sdf->srf", normed, qkv_weight, preferred_element_type=jnp.float32
    ).astype(jnp.bfloat16)
    query_blocks = projected[0].reshape(clusters, CSIZE, feature_count)
    pair_blocks = jnp.concatenate([projected[1], projected[2]], axis=-1).reshape(
        clusters, CSIZE, 2 * feature_count
    )
    key_owners, key_ranks = slot_rank(key_owner[:, 0], workers)
    query_owners, query_ranks = slot_rank(query_owner[:, 0], workers)
    key_cluster, key_fill = slot_pick(
        key_owners, key_ranks, myself, KEY_CAP, key_local.reshape(workers, -1)
    )
    query_cluster, query_fill = slot_pick(
        query_owners, query_ranks, myself, QUERY_CAP, query_local.reshape(workers, -1)
    )
    query_send = query_blocks[query_cluster]
    pair_send = pair_blocks[key_cluster]
    query_recv, pair_recv = (
        lax.all_to_all(query_send, "owner", split_axis=0, concat_axis=0, tiled=True),
        lax.all_to_all(pair_send, "owner", split_axis=0, concat_axis=0, tiled=True),
    )
    query_recv = query_recv.reshape(workers * QUERY_CAP, CSIZE, feature_count)
    pair_recv = pair_recv.reshape(workers * KEY_CAP, CSIZE, 2 * feature_count)
    my_key_owner = lax.dynamic_index_in_dim(key_owners, myself, 0, keepdims=False)
    my_key_rank = lax.dynamic_index_in_dim(key_ranks, myself, 0, keepdims=False)
    my_query_owner = lax.dynamic_index_in_dim(query_owners, myself, 0, keepdims=False)
    my_query_rank = lax.dynamic_index_in_dim(query_ranks, myself, 0, keepdims=False)
    tile_queries = query_recv[my_query_owner * QUERY_CAP + my_query_rank]
    tile_pairs = pair_recv[my_key_owner * KEY_CAP + my_key_rank]
    bucket_table = (
        hop_bucket[:, None] == jnp.arange(hop_bias.shape[0], dtype=jnp.int32)[None, :]
    ).astype(jnp.float32)
    tile_bias = jnp.dot(bucket_table, hop_bias, precision=lax.Precision.HIGHEST)
    self_bias = jnp.broadcast_to(hop_bias[0], (clusters, groups))
    all_queries = jnp.concatenate([tile_queries, query_blocks], 0)
    all_pairs = jnp.concatenate([tile_pairs, pair_blocks], 0)
    all_bias = jnp.concatenate([tile_bias, self_bias], 0)
    entries = tile_count + clusters

    def group_partial(inputs):
        return tile_partial(inputs[0], inputs[1], inputs[2])

    log_totals, partials = lax.map(
        group_partial,
        (
            all_queries.reshape(entries // 4, 4, CSIZE, feature_count),
            all_pairs.reshape(entries // 4, 4, CSIZE, 2 * feature_count),
            all_bias.reshape(entries // 4, 4, groups),
        ),
    )
    log_totals = log_totals.reshape(entries, groups, CSIZE)
    partials = partials.reshape(entries, CSIZE, feature_count)
    destinations = jnp.arange(workers, dtype=jnp.int32)
    slots = jnp.arange(QUERY_CAP, dtype=jnp.int32)
    chosen = (
        (my_query_owner[None, None, :] == destinations[:, None, None])
        & (my_query_rank[None, None, :] == slots[None, :, None])
    ).astype(jnp.int32)
    picks = jnp.sum(chosen * jnp.arange(tile_count, dtype=jnp.int32)[None, None, :], axis=2)
    send_log = log_totals[:tile_count][picks]
    send_part = partials[:tile_count][picks]
    back_log, back_part = (
        lax.all_to_all(send_log, "owner", split_axis=0, concat_axis=0, tiled=True),
        lax.all_to_all(send_part, "owner", split_axis=0, concat_axis=0, tiled=True),
    )
    all_log = jnp.concatenate(
        [log_totals[tile_count:], back_log.reshape(workers * QUERY_CAP, groups, CSIZE)], 0
    )
    all_part = jnp.concatenate(
        [partials[tile_count:], back_part.reshape(workers * QUERY_CAP, CSIZE, feature_count)], 0
    )
    cluster_ids = jnp.arange(clusters, dtype=jnp.int32)
    member = jnp.concatenate(
        [
            cluster_ids[:, None] == cluster_ids[None, :],
            query_fill.reshape(-1)[:, None]
            & (query_cluster.reshape(-1)[:, None] == cluster_ids[None, :]),
        ],
        0,
    )
    member_wide = member[:, :, None, None]
    masked = jnp.where(member_wide, all_log[:, None], -jnp.inf)
    peak_log = jnp.max(masked, axis=0)
    scaled = jnp.where(
        member_wide, jnp.exp(jnp.where(member_wide, all_log[:, None] - peak_log[None], 0.0)), 0.0
    )
    totals = jnp.sum(scaled, axis=0)
    shares = scaled / totals[None]
    attention = jnp.einsum(
        "ecgq,eqgd->cqgd",
        shares,
        all_part.reshape(-1, CSIZE, groups, head_size),
        precision=lax.Precision.HIGHEST,
    )
    attention = attention.reshape(row_count, feature_count).astype(jnp.bfloat16)
    head_rank = lax.axis_index("head")
    head_count = lax.axis_size("head")
    mixed = jnp.dot(
        lax.all_gather(attention, "head", axis=1, tiled=True),
        out_weight,
        preferred_element_type=jnp.float32,
    )
    resid = nodes.astype(jnp.float32) + mixed
    normed_again = norm_rows(resid).astype(jnp.bfloat16)
    unit_count = up_weight.shape[1] // head_count
    up_part = lax.dynamic_slice_in_dim(up_weight, head_rank * unit_count, unit_count, 1)
    down_part = lax.dynamic_slice_in_dim(down_weight, head_rank * unit_count, unit_count, 0)
    hidden = jax.nn.gelu(jnp.dot(normed_again, up_part, preferred_element_type=jnp.float32)).astype(
        jnp.bfloat16
    )
    terms = jnp.dot(hidden, down_part, preferred_element_type=jnp.float32)
    summed = lax.psum_scatter(
        terms.astype(jnp.bfloat16), "head", scatter_dimension=1, tiled=True
    ).astype(jnp.float32)
    column_count = model_width // head_count
    own_resid = lax.dynamic_slice_in_dim(resid, head_rank * column_count, column_count, 1)
    return (own_resid + summed).astype(jnp.bfloat16)


def solution(mesh):
    placed = (
        P("owner", None),
        P(None, None, "head"),
        P(),
        P(None, "head"),
        P(),
        P(),
        P(),
        P(),
        P(),
        P(),
        P("owner"),
    )
    return jax.shard_map(
        per_device, mesh=mesh, in_specs=placed, out_specs=P("owner", "head"), check_vma=False
    )
```

profile of v0, /device:TPU:0, one launch (start us, length us, event | category | flops | bytes accessed | tf_op | source)
XLA Modules:
  0.0 768.0 jit_solution(17093415510532091853)
XLA Ops:
  11.1 4.8 copy.106
  15.9 2.5 convert_reduce_fusion
  18.4 2.8 fusion.19
  25.2 2.8 convert_reduce_fusion.1
  35.5 3.7 gather_fusion
  39.2 8.5 %all-to-all-start = ((bf16[32,2,256,192]{2,3,1,0:T(8,128)(2,1)}), bf16[32,2,256,192]{2,3,1,0:T(8,128)(2,1)}, u32[]{:S(2)}, u32[]{:S(2)}) async-start(bf16[32,2,256,192]{2,3,1,0:T(8,128)(2,1)} %bitcast.113), calls=%async_computation | async-start | bytes 12582912 | tf_op jit(solution)/shard_map/all_to_all | solution.py:100
  58.7 2.1 pad_maximum_fusion.1
  60.8 7.5 gather_fusion.2
  68.3 57.3 %all-to-all-done = bf16[32,2,256,192]{2,3,1,0:T(8,128)(2,1)} async-done(((bf16[32,2,256,192]{2,3,1,0:T(8,128)(2,1)}), bf16[32,2,256,192]{2,3,1,0:T(8,128)(2,1)}, u32[]{:S(2)}, u32[]{:S(2)}) %all-to-all-start) | async-done | bytes 6291488 | tf_op jit(solution)/shard_map/all_to_all | solution.py:100
  125.6 5.7 all-to-all-start.1
  133.5 5.2 gather_fusion.1
  138.7 4.1 pad_maximum_fusion
  142.8 149.4 %all-to-all-done.1 = bf16[32,2,256,384]{3,2,1,0:T(8,128)(2,1)} async-done(((bf16[32,2,256,384]{3,2,1,0:T(8,128)(2,1)}), bf16[32,2,256,384]{3,2,1,0:T(8,128)(2,1)}, u32[]{:S(2)}, u32[]{:S(2)}) %all-to-all-start.1) | async-done | bytes 12582944 | tf_op jit(solution)/shard_map/all_to_all | solution.py:101
  292.2 8.9 %gather_fusion.3 = bf16[32,256,384]{2,1,0:T(8,128)(2,1)} fusion(bf16[64,256,384]{2,1,0:T(8,128)(2,1)} %bitcast.23, s32[1024]{0:T(1024)S(1)} %pad_clamp_fusion.1), kind=kCustom, calls=%fused_computation.3 | custom fusion | bytes 12583040 | tf_op jit(solution)/shard_map/gather | solution.py:110
  301.1 7.9 %maximum_maximum_fusion = bf16[40,256,384]{2,1,0:T(8,128)(2,1)} fusion(bf16[8,256,192]{2,1,0:T(8,128)(2,1)S(1)} %bitcast.120, bf16[8,256,192]{2,1,0:T(8,128)(2,1)S(1)} %bitcast.118, bf16[32,256,384]{2,1,0:T(8,128)(2,1)} %gather_fusion.3), kind=kLoop, calls=%fused_computation.29 | loop fusion | flops 23592960 | bytes 15728640 | tf_op jit(solution)/shard_map/concatenate | solution.py:117
  309.0 84.2 %while.12 = (s32[]{:T(128)}, f32[10,4,6,256]{3,2,1,0:T(8,128)}, f32[10,4,256,192]{2,3,1,0:T(8,128)}, bf16[10,4,256,192]{2,3,1,0:T(8,128)(2,1)}, bf16[10,4,256,38...) while((s32[]{:T(128)}, f32[10,4,6,256]{3,2,1,0:T(8,128)}, f32[10,4,256,192]{2,3,1,0:T(8,128)}, ...), condition=%wide.region_9.10_spmd, body=%wide.region_6.9_spmd.sunk | while | flops 218818560 | bytes 28124728 | solution.py:124
  395.8 3.9 all-to-all-start.3
  399.7 6.1 slice.45
  405.8 8.7 %gather_fusion.4 = f32[64,256,192]{1,2,0:T(8,128)} fusion(f32[32,256,192]{1,2,0:T(8,128)} %bitcast.107, s32[1024]{0:T(1024)S(1)} %pad_clamp_fusion), kind=kCustom, calls=%fused_computation.4 | custom fusion | bytes 25166080 | tf_op jit(solution)/shard_map/gather | solution.py:142
  414.5 7.5 all-to-all-start.2
  425.2 19.5 %copy.117 = f32[8,256,6,32]{0,3,2,1:T(8,128)} copy(f32[8,256,6,32]{1,3,2,0:T(8,128)S(1)} %bitcast.122) | data formatting | bytes 3145728 | tf_op jit(solution)/shard_map/concatenate | solution.py:150
  445.6 5.4 fusion.31
  451.0 131.8 %all-to-all-done.2 = f32[32,2,256,192]{2,3,1,0:T(8,128)} async-done(((f32[32,2,256,192]{2,3,1,0:T(8,128)}), f32[32,2,256,192]{2,3,1,0:T(8,128)}, u32[]{:S(2)}, u32[]{:S(2)}) %all-to-all-start.2) | async-done | bytes 12582944 | tf_op jit(solution)/shard_map/all_to_all | solution.py:145
  582.8 23.8 %copy.118 = f32[64,256,6,32]{0,3,2,1:T(8,128)} copy(f32[64,256,6,32]{1,3,2,0:T(8,128)} %bitcast.34) | data formatting | bytes 25165824 | tf_op jit(solution)/shard_map/concatenate | solution.py:150
  606.6 49.0 %convert_bitcast_fusion = bf16[8,256,6,32]{3,0,2,1:T(8,128)(2,1)} fusion(f32[72,8,6,256]{0,1,2,3:T(8,128)} %get-tuple-element.100, f32[8,6,256]{0,1,2:T(8,128)} %get-tuple-element.99, f32[72,6,256]{0,1,2:T(8,128)S(1)} %copy.125, pred[72,8]{0,1:T(8,128)(4,1)S(1)} %pad_add_fusion, f32[64,256,6,32]{0,3,2,1:T(8,128)} %copy.118, f32[8,256,6,32]{0,3,2,1:T(8,128)} %copy.117), kind=kOutput, calls=%fused_computation.59 | convolution fusion | flops 347209728 | bytes 18973248 | tf_op jit(solution)/shard_map/ecgq,eqgd->cqgd/dot_general | solution.py:170
  655.6 4.9 copy.126
  661.7 36.0 %all-gather.2.cloned.1.call-done = bf16[2048,768]{0,1:T(8,128)(2,1)} async-done(((bf16[2048,192]{0,1:T(8,128)(2,1)}), bf16[2048,768]{0,1:T(8,128)(2,1)}) %all-gather.2.cloned.1.call-update) | async-done | bytes 3145744 | tf_op jit(solution)/shard_map/all_gather | solution.py:180
  697.7 5.6 fusion.80
  703.3 2.6 copy-done.2
  706.7 13.0 %convolution_convert_fusion = bf16[2048,768]{0,1:T(8,128)(2,1)} fusion(f32[2048,768]{0,1:T(8,128)} %copy-done.2, f32[2048]{0:T(1024)S(1)} %add_rsqrt_fusion, f32[2048]{0:T(1024)S(1)} %broadcast_multiply_fusion, bf16[3072,768]{1,0:T(8,128)(2,1)} %param.18, s32[]{:T(128)S(6)} %select_n.86, bf16[768,3072]{1,0:T(8,128)(2,1)} %param.17), kind=kOutput, calls=%fused_computation.50 | convolution fusion | flops 4852285440 | bytes 11813888 | tf_op jit(solution)/shard_map/dot_general | solution.py:192
  719.7 38.6 %reduce-scatter.2.cloned.1.call-done = bf16[2048,192]{0,1:T(8,128)(2,1)} async-done(((bf16[2048,768]{0,1:T(8,128)(2,1)}), bf16[2048,192]{0,1:T(8,128)(2,1)}) %reduce-scatter.2.cloned.1.call-update) | async-done | bytes 786448 | tf_op jit(solution)/shard_map/reduce_scatter | solution.py:193
  758.2 2.7 add_convert_fusion
  (200 shorter events, 121.4 us)
Async XLA Ops:
  6.5 691.1 %copy-start = (bf16[768,768]{1,0:T(8,128)(2,1)S(1)}, bf16[768,768]{1,0:T(8,128)(2,1)}, u32[]{:S(2)}) copy-start(bf16[768,768]{1,0:T(8,128)(2,1)} %param.15) | copy-start | bytes 3538948
  11.1 10.1 %copy-start.11 = (bf16[3,768,192]{1,2,0:T(8,128)(2,1)S(1)}, bf16[3,768,192]{1,2,0:T(8,128)(2,1)}, u32[]{:S(2)}) copy-start(bf16[3,768,192]{1,2,0:T(8,128)(2,1)} %param.14) | copy-start | bytes 2654212
  15.9 5.3 copy-start.1
  28.0 0.6 copy-start.5
  30.0 0.6 copy-start.6
  39.2 86.4 %all-to-all-start = ((bf16[32,2,256,192]{2,3,1,0:T(8,128)(2,1)}), bf16[32,2,256,192]{2,3,1,0:T(8,128)(2,1)}, u32[]{:S(2)}, u32[]{:S(2)}) async-start(bf16[32,2,256,192]{2,3,1,0:T(8,128)(2,1)} %bitcast.113), calls=%async_computation | async-start | bytes 12582912 | tf_op jit(solution)/shard_map/all_to_all | solution.py:100
  125.6 5.7 copy-start.8
  125.6 5.8 copy-start.12
  125.6 6.3 copy-start.9
  125.6 166.6 %all-to-all-start.1 = ((bf16[32,2,256,384]{3,2,1,0:T(8,128)(2,1)}), bf16[32,2,256,384]{3,2,1,0:T(8,128)(2,1)}, u32[]{:S(2)}, u32[]{:S(2)}) async-start(bf16[32,2,256,384]{3,2,1,0:T(8,128)(2,1)} %bitcast.110), calls=%async_computation.1 | async-start | bytes 25165824 | tf_op jit(solution)/shard_map/all_to_all | solution.py:101
  292.2 8.9 %copy-start.3 = (bf16[1,2048,192]{2,1,0:T(8,128)(2,1)S(1)}, bf16[1,2048,192]{2,1,0:T(8,128)(2,1)}, u32[]{:S(2)}) copy-start(bf16[1,2048,192]{2,1,0:T(8,128)(2,1)} %copy.129) | copy-start | bytes 2359300
  292.2 8.9 %copy-start.4 = (bf16[1,2048,192]{2,1,0:T(8,128)(2,1)S(1)}, bf16[1,2048,192]{2,1,0:T(8,128)(2,1)}, u32[]{:S(2)}) copy-start(bf16[1,2048,192]{2,1,0:T(8,128)(2,1)} %copy.130) | copy-start | bytes 2359300
  395.8 18.7 %all-to-all-start.3 = ((f32[32,2,6,256]{3,1,2,0:T(2,128)}), f32[32,2,6,256]{3,1,2,0:T(2,128)S(1)}, u32[]{:S(2)}, u32[]{:S(2)}) async-start(f32[32,2,6,256]{3,1,2,0:T(2,128)} %copy.123), calls=%async_computation.3 | async-start | bytes 786432 | tf_op jit(solution)/shard_map/all_to_all | solution.py:144
  414.5 7.7 %copy-start.7 = (s32[32,2]{0,1:T(2,128)S(1)}, s32[32,2]{0,1:T(2,128)}, u32[]{:S(2)}) copy-start(s32[32,2]{0,1:T(2,128)} %copy-done.6) | copy-start | bytes 772
  414.5 7.9 %copy-start.10 = (s32[32,2]{0,1:T(2,128)S(1)}, s32[32,2]{0,1:T(2,128)}, u32[]{:S(2)}) copy-start(s32[32,2]{0,1:T(2,128)} %get-tuple-element.76) | copy-start | bytes 772
  414.5 168.3 %all-to-all-start.2 = ((f32[32,2,256,192]{2,3,1,0:T(8,128)}), f32[32,2,256,192]{2,3,1,0:T(8,128)}, u32[]{:S(2)}, u32[]{:S(2)}) async-start(f32[32,2,256,192]{2,3,1,0:T(8,128)} %bitcast.109), calls=%async_computation.2 | async-start | bytes 25165824 | tf_op jit(solution)/shard_map/all_to_all | solution.py:145
  422.0 275.7 %all-gather.2.cloned.1.call-start = ((), (), s32[]{:S(2)}) async-start(), calls=%async_computation.5 | async-start | bytes 3932160 | tf_op jit(solution)/shard_map/all_gather | solution.py:180
  661.6 96.6 %reduce-scatter.2.cloned.1.call-start = ((), (), s32[]{:S(2)}) async-start(), calls=%async_computation.6 | async-start | bytes 3932160 | tf_op jit(solution)/shard_map/reduce_scatter | solution.py:193
  703.3 2.7 copy-start.2
Sparse Core Ops, SparseCore 0:
  661.8 35.8 all-gather.1
  719.8 38.4 reduce-scatter.1
where the time goes:
time: 779 us; the launch traced here: 768 us
  waiting for transfers between devices  413 us (53%)
  local copies, waits for them, and re-layouts  153 us (20%)
  matrix products  96.9 us (12%)
  other arithmetic  64.5 us (8%)
  starting transfers between devices  25.8 us (3%)
  between operations  14 us (2%)
    all_to_all x1, waiting for transfers between devices, per_device(): lax.all_to_all(pair_send, 'owner', split_axis=0, concat_axis=0, tiled=True)  149 us
    all_to_all x1, waiting for transfers between devices, per_device(): lax.all_to_all(send_part, 'owner', split_axis=0, concat_axis=0, tiled=True)  132 us
    all_to_all x1, waiting for transfers between devices, per_device(): lax.all_to_all(query_send, 'owner', split_axis=0, concat_axis=0, tiled=True)  57.3 us
    dot_general x1, matrix products, per_device(): jnp.einsum('ecgq,eqgd->cqgd', shares, all_part.reshape(-1, CSIZE, groups,...  49 us
    concatenate x2, local copies, waits for them, and re-layouts, per_device(): jnp.concatenate([partials[tile_count:], back_part.reshape(workers * QUERY...  43.3 us
    reduce_scatter x1, waiting for transfers between devices, per_device(): lax.psum_scatter(terms.astype(jnp.bfloat16), 'head', scatter_dimension=1,...  38.6 us
    all_gather x1, waiting for transfers between devices, per_device(): lax.all_gather(attention, 'head', axis=1, tiled=True)  36 us
    dynamic_slice x30, local copies, waits for them, and re-layouts, per_device(): lax.map(group_partial, (all_queries.reshape(entries // 4, 4, CSIZE, featu...  25.2 us
  transfers between devices with their start and end apart: 6, of which 5 were waited for; matrix products, arithmetic and copies ran while one was open for 10% of the time, Pallas kernels for 0%

commit v1 on v0

v1 whole, which is shorter than its diff:
```python
import functools
import math

import jax
import jax.numpy as jnp
from jax import lax
from jax.experimental import pallas as pl
from jax.experimental.pallas import tpu as pltpu
from jax.sharding import PartitionSpec as P

CSIZE = 256
EPSILON = 1e-05
RING = 4
LOCAL = 8
PLAN_HEADS = 3
HEAD_SIZE = 32
PLAN_FEATURES = PLAN_HEADS * HEAD_SIZE
LIST_MAX = 544
UNROLL = 4
MESH = pl.DeviceIdType.MESH
LOG2E = math.log2(math.e)
NEVER = -1e30


def norm_rows(values):
    center = values - jnp.mean(values, axis=-1, keepdims=True)
    spread = jnp.mean(center * center, axis=-1, keepdims=True)
    return center * lax.rsqrt(spread + EPSILON)


def coordinates():
    me = lax.axis_index("owner")
    return lax.div(me, 8), lax.rem(lax.div(me, 2), 4), lax.rem(me, 2)


def ring_at(axis, step):
    z, y, c = coordinates()
    if axis == "z":
        z = lax.rem(z + step + RING, RING)
    else:
        y = lax.rem(y + step + RING, RING)
    return ((z * 4 + y) * 2 + c, lax.axis_index("head"))


def sibling():
    z, y, c = coordinates()
    return ((z * 4 + y) * 2 + 1 - c, lax.axis_index("head"))


def greet(partners):
    barrier = pltpu.get_barrier_semaphore()
    for partner in partners:
        pl.semaphore_signal(barrier, inc=1, device_id=partner, device_id_type=MESH)
    pl.semaphore_wait(barrier, len(partners))


def gather_kernel(q_ref, kv_ref, qg_ref, kvg_ref, ring_send, ring_recv, pair_send, pair_recv, own_sem):
    z, y, c = coordinates()
    greet([ring_at("z", 1), ring_at("z", -1), ring_at("y", 1), ring_at("y", -1), sibling()])
    half = LOCAL // 2
    sent = []
    own = []

    def part(h):
        return pl.ds(h * half, half)

    streams = []
    for plan in range(2):
        q_axis, kv_axis = ("z", "y") if plan == 0 else ("y", "z")
        for kind, axis in (("kv", kv_axis), ("q", q_axis)):
            at = z if axis == "z" else y
            if kind == "q":
                source = lambda h, plan=plan: q_ref.at[plan, part(h)]
                slot = lambda p, h, plan=plan: qg_ref.at[plan, p, part(h)]
            else:
                source = lambda h, plan=plan: kv_ref.at[plan, part(h)]
                slot = lambda p, h, plan=plan: kvg_ref.at[plan, p, c, part(h)]
            streams.append((len(streams), plan, kind, axis, at, source, slot))

    def send(src, dst, send_sem, recv_sem, device):
        copy = pltpu.make_async_remote_copy(
            src_ref=src, dst_ref=dst, send_sem=send_sem, recv_sem=recv_sem,
            device_id=device, device_id_type=MESH,
        )
        copy.start()
        sent.append(copy)

    def arrived(ref, sem):
        pltpu.make_async_remote_copy(
            src_ref=ref, dst_ref=ref, send_sem=ring_send.at[0, 0], recv_sem=sem,
            device_id=sibling(), device_id_type=MESH,
        ).wait_recv()

    for turn in range(2):
        for number, plan, kind, axis, at, source, slot in streams:
            up, down = turn, 1 - turn
            send(source(up), slot(at, up), ring_send.at[number, up], ring_recv.at[number, up], ring_at(axis, 1))
            send(source(down), slot(at, down), ring_send.at[number, 2 + down], ring_recv.at[number, 2 + down], ring_at(axis, -1))
    for number, plan, kind, axis, at, source, slot in streams:
        if kind == "kv":
            for h in range(2):
                send(source(h), slot(at, h), pair_send.at[plan, h], pair_recv.at[plan, h], sibling())
        for h in range(2):
            copy = pltpu.make_async_copy(source(h), slot(at, h), own_sem.at[number, h])
            copy.start()
            own.append(copy)

    def place(at, step):
        return lax.rem(at + step + RING, RING)

    for number, plan, kind, axis, at, source, slot in streams:
        before, after = slot(place(at, -1), 0), slot(place(at, 1), 1)
        arrived(before, ring_recv.at[number, 0])
        send(before, before, ring_send.at[number, 4], ring_recv.at[number, 4], ring_at(axis, 1))
        arrived(after, ring_recv.at[number, 3])
        send(after, after, ring_send.at[number, 5], ring_recv.at[number, 5], ring_at(axis, -1))
        if kind == "kv":
            send(before, before, pair_send.at[plan, 2], pair_recv.at[plan, 2], sibling())
            send(after, after, pair_send.at[plan, 5], pair_recv.at[plan, 5], sibling())
    for number, plan, kind, axis, at, source, slot in streams:
        before, after = slot(place(at, -1), 1), slot(place(at, 1), 0)
        arrived(before, ring_recv.at[number, 1])
        arrived(after, ring_recv.at[number, 2])
        if kind == "kv":
            send(before, before, pair_send.at[plan, 3], pair_recv.at[plan, 3], sibling())
            send(after, after, pair_send.at[plan, 4], pair_recv.at[plan, 4], sibling())
    for number, plan, kind, axis, at, source, slot in streams:
        for h in range(2):
            far = slot(place(at, 2), h)
            arrived(far, ring_recv.at[number, 4 + h])
            if kind == "kv":
                send(far, far, pair_send.at[plan, 6 + h], pair_recv.at[plan, 6 + h], sibling())
    for number, plan, kind, axis, at, source, slot in streams:
        if kind == "kv":
            for index, step in enumerate((0, -1, 1, 2)):
                for h in range(2):
                    arrived(kvg_ref.at[plan, place(at, step), 1 - c, part(h)], pair_recv.at[plan, 2 * index + h])
    for copy in sent:
        copy.wait_send()
    for copy in own:
        copy.wait()


def gather(q_blocks, kv_blocks):
    any_space = pl.BlockSpec(memory_space=pl.ANY)
    dma = pltpu.SemaphoreType.DMA
    return pl.pallas_call(
        gather_kernel,
        out_shape=[
            jax.ShapeDtypeStruct((2, RING, LOCAL, PLAN_FEATURES, CSIZE), jnp.bfloat16),
            jax.ShapeDtypeStruct((2, RING, 2, LOCAL, 2 * PLAN_FEATURES, CSIZE), jnp.bfloat16),
        ],
        in_specs=[any_space] * 2,
        out_specs=[any_space] * 2,
        scratch_shapes=[dma((4, 6)), dma((4, 6)), dma((2, 8)), dma((2, 8)), dma((4, 2))],
        compiler_params=pltpu.CompilerParams(collective_id=0, has_side_effects=True),
        name="gather",
    )(q_blocks, kv_blocks)


def tile_kernel(list_ref, bucket_ref, bias_ref, q_ref, kv_ref, part_ref, log_ref, m_ref, l_ref, acc_ref):
    heads = range(PLAN_HEADS)
    queries = q_ref.shape[0]
    m_ref[...] = jnp.full(m_ref.shape, NEVER, jnp.float32)
    l_ref[...] = jnp.zeros(l_ref.shape, jnp.float32)
    acc_ref[...] = jnp.zeros(acc_ref.shape, jnp.float32)
    ones = jnp.ones((16, CSIZE), jnp.bfloat16)

    def rows(h):
        return slice(HEAD_SIZE * h, HEAD_SIZE * (h + 1))

    def batch(step, carry):
        loaded = []
        for u in range(UNROLL):
            item = list_ref[step * UNROLL + u]
            state = lax.bitwise_and(item, 127)
            key = lax.bitwise_and(lax.shift_right_logical(item, 7), 127)
            tile = lax.bitwise_and(lax.shift_right_logical(item, 14), 2047)
            query = jnp.minimum(state, queries - 1)
            head0 = jnp.where(key >= kv_ref.shape[0] // 2, PLAN_HEADS, 0)
            bucket = jnp.where(tile >= 1024, 0, bucket_ref[jnp.minimum(tile, 1023)])
            bias = [bias_ref[bucket * (2 * PLAN_HEADS) + head0 + h] * LOG2E for h in heads]
            scores = [
                lax.dot_general(
                    kv_ref[key, rows(h), :], q_ref[query, rows(h), :],
                    (((0,), (0,)), ((), ())), preferred_element_type=jnp.float32,
                )
                for h in heads
            ]
            loaded.append((state, key, bias, scores))
        done = []
        for state, key, bias, scores in loaded:
            highest = [jnp.max(s, axis=0, keepdims=True) for s in scores]
            weights = [jnp.exp2(s - top).astype(jnp.bfloat16) for s, top in zip(scores, highest)]
            mixed = [
                jnp.dot(
                    jnp.concatenate([kv_ref[key, slice(PLAN_FEATURES + HEAD_SIZE * h, PLAN_FEATURES + HEAD_SIZE * (h + 1)), :], ones], 0),
                    weights[h], preferred_element_type=jnp.float32,
                )
                for h in heads
            ]
            done.append((state, [top + b for top, b in zip(highest, bias)], mixed))
        for state, tops, mixed in done:
            old_m = [m_ref[state, h : h + 1, :] for h in heads]
            old_l = [l_ref[state, h : h + 1, :] for h in heads]
            old_acc = [acc_ref[state, rows(h), :] for h in heads]
            new_m = [jnp.maximum(a, b) for a, b in zip(old_m, tops)]
            keep = [jnp.exp2(a - b) for a, b in zip(old_m, new_m)]
            fresh = [jnp.exp2(a - b) for a, b in zip(tops, new_m)]
            for h in heads:
                m_ref[state, h : h + 1, :] = new_m[h]
                l_ref[state, h : h + 1, :] = old_l[h] * keep[h] + mixed[h][HEAD_SIZE : HEAD_SIZE + 1] * fresh[h]
                acc_ref[state, rows(h), :] = old_acc[h] * keep[h] + mixed[h][:HEAD_SIZE] * fresh[h]
        return carry

    lax.fori_loop(0, lax.div(list_ref[LIST_MAX] + UNROLL - 1, UNROLL), batch, 0)

    def finish(group, carry):
        for local in range(LOCAL):
            state = group * LOCAL + local
            for h in heads:
                total = l_ref[state, h : h + 1, :]
                held = total > 0
                safe = jnp.where(held, total, 1.0)
                part_ref[state, rows(h), :] = (acc_ref[state, rows(h), :] * (1.0 / safe)).astype(jnp.bfloat16)
                row = local * PLAN_HEADS + h
                log_ref[group, row : row + 1, :] = m_ref[state, h : h + 1, :] + jnp.log2(safe)
        return carry

    lax.fori_loop(0, queries // LOCAL, finish, 0)


def tiles(items, buckets, bias, q_all, kv_all):
    queries = q_all.shape[0]
    whole = lambda shape: pl.BlockSpec(shape, lambda i, *_: (0,) * len(shape))
    log_shape = (queries // LOCAL, LOCAL * PLAN_HEADS, CSIZE)
    return pl.pallas_call(
        tile_kernel,
        grid_spec=pltpu.PrefetchScalarGridSpec(
            num_scalar_prefetch=3,
            grid=(1,),
            in_specs=[whole(q_all.shape), whole(kv_all.shape)],
            out_specs=[whole(q_all.shape), whole(log_shape)],
            scratch_shapes=[
                pltpu.VMEM((queries + 1, 8, CSIZE), jnp.float32),
                pltpu.VMEM((queries + 1, 8, CSIZE), jnp.float32),
                pltpu.VMEM((queries + 1, PLAN_FEATURES, CSIZE), jnp.float32),
            ],
        ),
        out_shape=[
            jax.ShapeDtypeStruct(q_all.shape, jnp.bfloat16),
            jax.ShapeDtypeStruct(log_shape, jnp.float32),
        ],
        compiler_params=pltpu.CompilerParams(vmem_limit_bytes=56 * 2**20),
        name="tiles",
    )(items, buckets, bias, q_all, kv_all)


def tile_list(key_owner, key_local, query_owner, query_local):
    z, y, c = coordinates()
    key_owner, query_owner = key_owner.reshape(8, 128), query_owner.reshape(8, 128)
    key_local, query_local = key_local.reshape(8, 128), query_local.reshape(8, 128)
    qz, qy, qc = query_owner // 8, query_owner // 2 % 4, query_owner % 2
    kz, ky, kc = key_owner // 8, key_owner // 2 % 4, key_owner % 2
    number = jnp.arange(1024, dtype=jnp.int32).reshape(8, 128)
    mine_a = (qy == y) & (qc == c) & (kz == z)
    mine_b = (qz == z) & (qc == c) & (ky == y)
    item_a = (qz * 8 + query_local) + ((ky * 16 + kc * 8 + key_local) << 7) + (number << 14)
    item_b = (32 + qy * 8 + query_local) + ((64 + kz * 16 + kc * 8 + key_local) << 7) + (number << 14)
    mine = jnp.concatenate([mine_a, mine_b], 0)
    items = jnp.concatenate([item_a, item_b], 0)
    ones = mine.astype(jnp.float32)
    lane = jnp.arange(128)
    row = jnp.arange(16)
    inside = jnp.dot(ones, (lane[:, None] < lane[None, :]).astype(jnp.float32))
    counts = jnp.sum(ones, axis=1)
    ahead = jnp.sum(jnp.where(row[None, :] < row[:, None], counts[None, :], 0.0), axis=1)
    rank = (inside + ahead[:, None]).astype(jnp.int32) + 16
    rank = jnp.where(mine, rank, -1).reshape(2048)
    own = jnp.arange(8, dtype=jnp.int32)
    own_a = (z * 8 + own) + ((y * 16 + c * 8 + own) << 7) + (1024 << 14)
    own_b = (32 + y * 8 + own) + ((64 + z * 16 + c * 8 + own) << 7) + (1024 << 14)
    place = jnp.arange(LIST_MAX, dtype=jnp.int32)
    total = jnp.sum(counts).astype(jnp.int32) + 16
    listed = jnp.sum(jnp.where(place[:, None] == rank[None, :], items.reshape(2048)[None, :], 0), axis=1)
    listed = jnp.where(place < total, listed, 64 + (1024 << 14))
    return jnp.concatenate([own_a, own_b, listed[16:], total[None]])


def per_device(
    nodes, qkv_weight, out_weight, hop_bias, up_weight, down_weight,
    key_owner, key_local, query_owner, query_local, hop_bucket,
):
    head_rank = lax.axis_index("head")
    model_width = nodes.shape[1]
    items = tile_list(key_owner, key_local, query_owner, query_local)
    buckets = lax.all_gather(hop_bucket, "owner", axis=0, tiled=True)
    normed = norm_rows(nodes.astype(jnp.float32)).astype(jnp.bfloat16)
    projected = jnp.einsum("sdf,rd->sfr", qkv_weight, normed, preferred_element_type=jnp.float32)
    q_rows = (projected[0] * (LOG2E / math.sqrt(HEAD_SIZE))).astype(jnp.bfloat16)
    kv_rows = projected[1:].astype(jnp.bfloat16)
    q_blocks = q_rows.reshape(2, PLAN_FEATURES, LOCAL, CSIZE).transpose(0, 2, 1, 3)
    kv_blocks = (
        kv_rows.reshape(2, 2, PLAN_FEATURES, LOCAL, CSIZE)
        .transpose(1, 3, 0, 2, 4)
        .reshape(2, LOCAL, 2 * PLAN_FEATURES, CSIZE)
    )
    q_all, kv_all = gather(q_blocks, kv_blocks)
    parts, logs = tiles(
        items, buckets, hop_bias.reshape(-1),
        q_all.reshape(2 * RING * LOCAL, PLAN_FEATURES, CSIZE),
        kv_all.reshape(2 * RING * 2 * LOCAL, 2 * PLAN_FEATURES, CSIZE),
    )
    parts = parts.reshape(2, RING, LOCAL, PLAN_HEADS, HEAD_SIZE, CSIZE)
    logs = logs.reshape(2, RING, LOCAL, PLAN_HEADS, CSIZE)
    along_z = [[(z * 4 + y) * 2 + c for z in range(4)] for y in range(4) for c in range(2)]
    along_y = [[(z * 4 + y) * 2 + c for y in range(4)] for z in range(4) for c in range(2)]
    back = lambda x, groups: lax.all_to_all(x, "owner", 0, 0, axis_index_groups=groups, tiled=True)
    merged = []
    for plan, groups in enumerate((along_z, along_y)):
        part, log = back(parts[plan], groups), back(logs[plan], groups)
        share = jnp.exp2(log - jnp.max(log, axis=0))
        share = share / jnp.sum(share, axis=0)
        merged.append(jnp.sum(share[:, :, :, None, :] * part.astype(jnp.float32), axis=0).astype(jnp.bfloat16))
    attention = jnp.concatenate(merged, axis=1).reshape(LOCAL, 2 * PLAN_FEATURES, CSIZE)
    attention = lax.all_to_all(attention, "head", 0, 0, tiled=True).reshape(4, 2, 2 * PLAN_FEATURES, CSIZE)
    mixed = jnp.einsum(
        "xcfr,xfd->crd", attention, out_weight.reshape(4, 2 * PLAN_FEATURES, model_width),
        preferred_element_type=jnp.float32,
    ).reshape(2 * CSIZE, model_width)
    resid = lax.dynamic_slice_in_dim(nodes, head_rank * 2 * CSIZE, 2 * CSIZE, 0).astype(jnp.float32) + mixed
    normed_again = norm_rows(resid).astype(jnp.bfloat16)
    hidden = jax.nn.gelu(
        jnp.dot(normed_again, up_weight, preferred_element_type=jnp.float32)
    ).astype(jnp.bfloat16)
    out = (resid + jnp.dot(hidden, down_weight, preferred_element_type=jnp.float32)).astype(jnp.bfloat16)
    return lax.all_to_all(out, "head", 1, 0, tiled=True)


def solution(mesh):
    placed = (
        P("owner", None), P(None, None, "head"), P(), P(None, "head"), P(), P(),
        P(), P(), P(), P(), P("owner"),
    )
    return jax.shard_map(
        per_device, mesh=mesh, in_specs=placed, out_specs=P("owner", "head"), check_vma=False
    )
```

time: 779 us -> 249 us (0.32); the launches traced: 768 us -> 248 us
  waiting for transfers between devices: 413 us -> 30.9 us
  local copies, waits for them, and re-layouts: 153 us -> 15.4 us
  Pallas kernels: 0 us -> 106 us
  matrix products: 96.9 us -> 14.6 us
  other arithmetic: 64.5 us -> 11.6 us
  blocking collectives: 0 us -> 50.4 us
  between operations: 14 us -> 1.58 us
  starting transfers between devices: 25.8 us -> 18 us
    all_to_all x4, waiting for transfers between devices: 339 us -> 30.9 us  [the longest x3 21.4 us: per_device(): lax.all_to_all(x, 'owner', 0, 0, axis_index_groups=groups, tiled=True)]
    pallas_call x0 -> x2, Pallas kernels: none -> 106 us  [the longest x1 74 us: gather(): pl.pallas_call(gather_kernel, out_shape=[jax.ShapeDtypeStruct((2, RING, L...]
    dot_general x24 -> x3, matrix products: 94.9 us -> 12 us  [the longest x1 9.12 us: per_device(): jnp.dot(hidden, down_weight, preferred_element_type=jnp.float32)]
    concatenate x6 -> x0, local copies, waits for them, and re-layouts: 46.4 us -> none  [the longest x2 43.3 us: per_device(): jnp.concatenate([partials[tile_count:], back_part.reshape(workers * QUERY...]
    reduce_scatter x1 -> x0, waiting for transfers between devices: 38.6 us -> none  [per_device(): lax.psum_scatter(terms.astype(jnp.bfloat16), 'head', scatter_dimension=1,...]
    all_gather x1 -> x0, waiting for transfers between devices: 36 us -> none  [per_device(): lax.all_gather(attention, 'head', axis=1, tiled=True)]
    gather x7 -> x0, local copies, waits for them, and re-layouts: 35.5 us -> none  [the longest x1 8.87 us: per_device(): tile_pairs = pair_recv[my_key_owner * KEY_CAP + my_key_rank]]
    all_to_all x0 -> x2, blocking collectives: none -> 31.6 us  [the longest x1 19.7 us: per_device(): lax.all_to_all(x, 'owner', 0, 0, axis_index_groups=groups, tiled=True)]
  transfers between devices with their start and end apart: 6 -> 4, of which waited for: 5 -> 4; matrix products, arithmetic and copies ran while one was open for 10% -> 2% of each run, Pallas kernels for 0% -> 0%
where the time goes in v1:
time: 249 us; the launch traced here: 248 us
  Pallas kernels  106 us (43%)
  blocking collectives  50.4 us (20%)
  waiting for transfers between devices  30.9 us (12%)
  starting transfers between devices  18 us (7%)
  local copies, waits for them, and re-layouts  15.4 us (6%)
  matrix products  14.6 us (6%)
  other arithmetic  11.6 us (5%)
    pallas_call x1, Pallas kernels, gather(): pl.pallas_call(gather_kernel, out_shape=[jax.ShapeDtypeStruct((2, RING, L...  74 us
    pallas_call x1, Pallas kernels, tiles(): pl.pallas_call(tile_kernel, grid_spec=pltpu.PrefetchScalarGridSpec(num_sc...  32 us
    all_to_all x3, waiting for transfers between devices, per_device(): lax.all_to_all(x, 'owner', 0, 0, axis_index_groups=groups, tiled=True)  21.4 us
    all_to_all x1, blocking collectives, per_device(): lax.all_to_all(x, 'owner', 0, 0, axis_index_groups=groups, tiled=True)  19.7 us
    unnamed x1, blocking collectives  18.8 us
    all_to_all x3, starting transfers between devices, per_device(): lax.all_to_all(x, 'owner', 0, 0, axis_index_groups=groups, tiled=True)  13.7 us
    all_to_all x1, blocking collectives, per_device(): return lax.all_to_all(out, 'head', 1, 0, tiled=True)  11.9 us
    all_to_all x1, waiting for transfers between devices, per_device(): lax.all_to_all(attention, 'head', 0, 0, tiled=True)  9.49 us
  transfers between devices with their start and end apart: 4, of which 4 were waited for; matrix products, arithmetic and copies ran while one was open for 2% of the time, Pallas kernels for 0%

profile of v1, /device:TPU:0, one launch (start us, length us, event | category | flops | bytes accessed | tf_op | source)
XLA Modules:
  0.0 248.5 jit_solution(1291820450883168405)
XLA Ops:
  0.0 2.5 %convert_reduce_fusion = f32[2048]{0:T(1024)S(1)} fusion(bf16[2048,768]{1,0:T(8,128)(2,1)} %param.11), kind=kLoop, calls=%fused_computation.2 | loop fusion | flops 3143680 | bytes 3153920 | tf_op jit(solution)/shard_map/reduce_sum | solution.py:26
  2.9 1.1 fusion.2
  4.1 2.6 %fusion.12 = f32[2048,576]{0,1:S(1)} fusion(bf16[768,576]{0,1:T(8,128)(2,1)S(1)} %bitcast.97, bf16[2048,768]{1,0:T(8,128)(2,1)S(1)} %copy-done.1, f32[2048]{0:T(1024)S(1)} %add_rsqrt_fusion, f32[2048]{0:T(1024)S(1)} %broadcast_multiply_fusion), kind=kOutput, calls=%fused_computation.17 | convolution fusion | flops 1818230784 | bytes 8765440
  7.4 0.7 convert_reduce_fusion.1
  8.7 1.4 select_reduce_fusion.1
  10.1 1.3 dynamic-slice
  12.1 0.9 dynamic-update-slice
  13.0 18.8 %all-reduce.bucket_ref = s32[1024]{0:T(1024)} all-reduce(s32[1024]{0:T(1024)S(1)} %dynamic-update-slice), channel_id=1, replica_groups=mesh['owner'=32,'head'=4] {'owner'}, use_global_device_ids=true, to_apply=%add | all-reduce | flops 1024 | bytes 8192
  31.8 0.8 fusion.24
  32.7 0.8 fusion.42
  34.7 0.8 copy.55
  36.6 1.5 copy.57
  38.3 1.1 copy.72
  39.3 74.0 %gather.1 = (bf16[2,4,8,96,256]{4,3,2,1,0:T(8,128)(2,1)}, bf16[2,4,2,8,192,256]{5,4,3,2,1,0:T(8,128)(2,1)}) custom-call(bf16[2,8,96,256]{3,2,1,0:T(8,128)(2,1)} %bitcast.87, bf16[2,8,192,256]{3,2,1,0:T(8,128)(2,1)} %bitcast.77), custom_call_target="tpu_custom_call" | custom-call | tf_op jit(solution)/shard_map/gather/pallas_call | solution.py:147
  114.0 32.0 %tiles.1 = (bf16[64,96,256]{2,1,0:T(8,128)(2,1)}, f32[8,24,256]{2,1,0:T(8,128)}) custom-call(s32[545]{0:T(1024)} %pad_add_fusion.1.list_ref, s32[1024]{0:T(1024)} %all-reduce.bucket_ref, f32[192]{0:T(256)} %reshape.108.bias_ref, bf16[64,96,256]{2,1,0:T(8,128)(2,1)} %bitcast.81, bf16[128,192,256]{2,1,0:T(8,128)(2,1)} %bitcast.75), custom_call_target="tpu_custom_call" | custom-call | tf_op jit(solution)/shard_map/tiles/pallas_call | solution.py:237
  146.0 1.0 fusion.56
  147.7 3.3 %all-to-all-start = ((f32[4,8,3,256]{3,1,2,0:T(8,128)}), f32[4,8,3,256]{3,1,2,0:T(8,128)S(1)}, u32[]{:S(2)}, u32[]{:S(2)}) async-start(f32[4,8,3,256]{3,1,2,0:T(8,128)} %copy.59), calls=%async_computation | async-start | bytes 196608 | tf_op jit(solution)/shard_map/all_to_all | solution.py:318
  151.7 5.5 %all-to-all-done = f32[4,8,3,256]{3,1,2,0:T(8,128)S(1)} async-done(((f32[4,8,3,256]{3,1,2,0:T(8,128)}), f32[4,8,3,256]{3,1,2,0:T(8,128)S(1)}, u32[]{:S(2)}, u32[]{:S(2)}) %all-to-all-start) | async-done | bytes 98336 | tf_op jit(solution)/shard_map/all_to_all | solution.py:318
  157.2 6.8 %all-to-all-start.2 = ((f32[4,8,3,256]{3,1,2,0:T(8,128)}), f32[4,8,3,256]{3,1,2,0:T(8,128)S(1)}, u32[]{:S(2)}, u32[]{:S(2)}) async-start(f32[4,8,3,256]{3,1,2,0:T(8,128)} %copy.62), calls=%async_computation.2 | async-start | bytes 196608 | tf_op jit(solution)/shard_map/all_to_all | solution.py:318
  164.1 3.2 %fusion.55 = (bf16[32,96,256]{2,1,0:T(8,128)(2,1)}, bf16[32,96,256]{2,1,0:T(8,128)(2,1)S(1)}) fusion(bf16[64,96,256]{2,1,0:T(8,128)(2,1)} %get-tuple-element.12), kind=kLoop, calls=%fused_computation.113 | loop fusion | bytes 6291456 | tf_op jit(solution)/shard_map/slice | solution.py:321
  167.3 2.6 %all-to-all-done.2 = f32[4,8,3,256]{3,1,2,0:T(8,128)S(1)} async-done(((f32[4,8,3,256]{3,1,2,0:T(8,128)}), f32[4,8,3,256]{3,1,2,0:T(8,128)S(1)}, u32[]{:S(2)}, u32[]{:S(2)}) %all-to-all-start.2) | async-done | bytes 98336 | tf_op jit(solution)/shard_map/all_to_all | solution.py:318
  169.9 19.7 %all_to_all.44 = bf16[4,8,3,32,256]{4,3,2,1,0:T(8,128)(2,1)} all-to-all(bf16[4,8,3,32,256]{4,3,2,1,0:T(8,128)(2,1)S(1)} %bitcast.80), channel_id=1, replica_groups={{0,8,16,24},{4,12,20,28},{32,40,48,56},{36,44,52,60},{64,72,80,88},{68,..., dimensions={0} | all-to-all | bytes 3145728 | tf_op jit(solution)/shard_map/all_to_all | solution.py:318
  189.5 3.6 %all-to-all-start.1 = ((bf16[4,8,3,32,256]{4,3,2,1,0:T(8,128)(2,1)}), bf16[4,8,3,32,256]{4,3,2,1,0:T(8,128)(2,1)S(1)}, u32[]{:S(2)}, u32[]{:S(2)}) async-start(bf16[4,8,3,32,256]{4,3,2,1,0:T(8,128)(2,1)} %bitcast.79), calls=%async_computation.1 | async-start | bytes 3145728 | tf_op jit(solution)/shard_map/all_to_all | solution.py:318
  193.4 1.9 multiply_reduce_fusion
  195.2 13.4 %all-to-all-done.1 = bf16[4,8,3,32,256]{4,3,2,1,0:T(8,128)(2,1)S(1)} async-done(((bf16[4,8,3,32,256]{4,3,2,1,0:T(8,128)(2,1)}), bf16[4,8,3,32,256]{4,3,2,1,0:T(8,128)(2,1)S(1)}, u32[]{:S(2)}, u32[]{:S(2)}) %all-to-all-start.1) | async-done | bytes 1572896 | tf_op jit(solution)/shard_map/all_to_all | solution.py:318
  209.0 0.9 pad_maximum_fusion
  210.0 4.3 %all-to-all-start.4 = ((bf16[8,192,256]{2,1,0:T(8,128)(2,1)}), bf16[8,192,256]{2,1,0:T(8,128)(2,1)S(1)}, u32[]{:S(2)}, u32[]{:S(2)}) async-start(bf16[8,192,256]{2,1,0:T(8,128)(2,1)} %bitcast.22), calls=%async_computation.4 | async-start | bytes 1572864 | tf_op jit(solution)/shard_map/all_to_all | solution.py:326
  214.3 9.5 %all-to-all-done.4 = bf16[8,192,256]{2,1,0:T(8,128)(2,1)S(1)} async-done(((bf16[8,192,256]{2,1,0:T(8,128)(2,1)}), bf16[8,192,256]{2,1,0:T(8,128)(2,1)S(1)}, u32[]{:S(2)}, u32[]{:S(2)}) %all-to-all-start.4) | async-done | bytes 786464 | tf_op jit(solution)/shard_map/all_to_all | solution.py:326
  223.8 2.0 fusion.57
  226.2 9.1 %add_convert_fusion = bf16[512,768]{1,0:T(8,128)(2,1)S(1)} fusion(f32[512,768]{1,0:T(8,128)S(1)} %get-tuple-element.24, bf16[3072,768]{1,0:T(8,128)(2,1)} %param.16, bf16[768,3072]{1,0:T(8,128)(2,1)} %param.15, f32[512]{0:T(512)S(1)} %add_rsqrt_fusion.1, f32[512]{0:T(512)S(1)} %broadcast_multiply_fusion.1), kind=kOutput, calls=%fused_computation.27 | convolution fusion | flops 4847960064 | bytes 11800576 | tf_op jit(solution)/shard_map/dot_general | solution.py:336
  235.6 11.9 %all_to_all.45 = bf16[512,4,192]{0,2,1:T(8,128)(2,1)S(1)} all-to-all(bf16[512,4,192]{0,2,1:T(8,128)(2,1)S(1)} %bitcast.84), channel_id=1, replica_groups=mesh['owner'=32,'head'=4] {'head'}, dimensions={1} | all-to-all | bytes 1572864 | tf_op jit(solution)/shard_map/all_to_all | solution.py:337
  247.5 1.0 copy.68
  (47 shorter events, 7.0 us)
Async XLA Ops:
  0.0 223.8 %copy-start = (bf16[768,768]{1,0:T(8,128)(2,1)S(1)}, bf16[768,768]{1,0:T(8,128)(2,1)}, u32[]{:S(2)}) copy-start(bf16[768,768]{1,0:T(8,128)(2,1)} %param.13) | copy-start | bytes 3538948
  0.0 2.9 %copy-start.1 = (bf16[2048,768]{1,0:T(8,128)(2,1)S(1)}, bf16[2048,768]{1,0:T(8,128)(2,1)}, u32[]{:S(2)}) copy-start(bf16[2048,768]{1,0:T(8,128)(2,1)} %param.11) | copy-start | bytes 9437188
  0.0 4.0 %copy-start.6 = (bf16[3,768,192]{1,2,0:T(8,128)(2,1)S(1)}, bf16[3,768,192]{1,2,0:T(8,128)(2,1)}, u32[]{:S(2)}) copy-start(bf16[3,768,192]{1,2,0:T(8,128)(2,1)} %param.12) | copy-start | bytes 2654212
  6.7 0.7 copy-start.2
  6.7 0.7 copy-start.3
  7.4 4.7 %copy-start.5 = (pred[8,128]{1,0:T(8,128)(4,1)}, pred[8,128]{1,0:T(8,128)(4,1)S(1)}, u32[]{:S(2)}) copy-start(pred[8,128]{1,0:T(8,128)(4,1)S(1)} %get-tuple-element.22) | copy-start | bytes 3076
  38.1 75.3 %copy-start.4 = (s32[528]{0:T(1024)S(1)}, s32[528]{0:T(1024)}, u32[]{:S(2)}) copy-start(s32[528]{0:T(1024)} %slice.26) | copy-start | bytes 6340
  147.7 9.5 %all-to-all-start = ((f32[4,8,3,256]{3,1,2,0:T(8,128)}), f32[4,8,3,256]{3,1,2,0:T(8,128)S(1)}, u32[]{:S(2)}, u32[]{:S(2)}) async-start(f32[4,8,3,256]{3,1,2,0:T(8,128)} %copy.59), calls=%async_computation | async-start | bytes 196608 | tf_op jit(solution)/shard_map/all_to_all | solution.py:318
  157.2 12.6 %all-to-all-start.2 = ((f32[4,8,3,256]{3,1,2,0:T(8,128)}), f32[4,8,3,256]{3,1,2,0:T(8,128)S(1)}, u32[]{:S(2)}, u32[]{:S(2)}) async-start(f32[4,8,3,256]{3,1,2,0:T(8,128)} %copy.62), calls=%async_computation.2 | async-start | bytes 196608 | tf_op jit(solution)/shard_map/all_to_all | solution.py:318
  189.5 19.1 %all-to-all-start.1 = ((bf16[4,8,3,32,256]{4,3,2,1,0:T(8,128)(2,1)}), bf16[4,8,3,32,256]{4,3,2,1,0:T(8,128)(2,1)S(1)}, u32[]{:S(2)}, u32[]{:S(2)}) async-start(bf16[4,8,3,32,256]{4,3,2,1,0:T(8,128)(2,1)} %bitcast.79), calls=%async_computation.1 | async-start | bytes 3145728 | tf_op jit(solution)/shard_map/all_to_all | solution.py:318
  210.0 13.8 %all-to-all-start.4 = ((bf16[8,192,256]{2,1,0:T(8,128)(2,1)}), bf16[8,192,256]{2,1,0:T(8,128)(2,1)S(1)}, u32[]{:S(2)}, u32[]{:S(2)}) async-start(bf16[8,192,256]{2,1,0:T(8,128)(2,1)} %bitcast.22), calls=%async_computation.4 | async-start | bytes 1572864 | tf_op jit(solution)/shard_map/all_to_all | solution.py:326

commit v2 on v1

--- a/solution.py
+++ b/solution.py
@@ -33,12 +33,16 @@
     return lax.div(me, 8), lax.rem(lax.div(me, 2), 4), lax.rem(me, 2)
 
 
+def place(at, step):
+    return lax.rem(at + step + RING, RING)
+
+
 def ring_at(axis, step):
     z, y, c = coordinates()
     if axis == "z":
-        z = lax.rem(z + step + RING, RING)
+        z = place(z, step)
     else:
-        y = lax.rem(y + step + RING, RING)
+        y = place(y, step)
     return ((z * 4 + y) * 2 + c, lax.axis_index("head"))
 
 
@@ -54,12 +58,16 @@
     pl.semaphore_wait(barrier, len(partners))
 
 
-def gather_kernel(q_ref, kv_ref, qg_ref, kvg_ref, ring_send, ring_recv, pair_send, pair_recv, own_sem):
+def gather_kernel(
+    q_ref, kv_ref, bucket_ref, qg_ref, kvg_ref, table_ref,
+    ring_send, ring_recv, pair_send, pair_recv, table_send, table_recv, own_sem,
+):
     z, y, c = coordinates()
-    greet([ring_at("z", 1), ring_at("z", -1), ring_at("y", 1), ring_at("y", -1), sibling()])
+    own = pltpu.make_async_copy(bucket_ref, table_ref.at[c, z, y], own_sem)
+    own.start()
+    greet([ring_at(axis, step) for axis in "zy" for step in (1, 2, 3)] + [sibling()])
     half = LOCAL // 2
     sent = []
-    own = []
 
     def part(h):
         return pl.ds(h * half, half)
@@ -91,6 +99,8 @@
             device_id=sibling(), device_id_type=MESH,
         ).wait_recv()
 
+    for step in (1, 2, 3):
+        send(bucket_ref, table_ref.at[c, z, y], table_send.at[step - 1], table_recv.at[step - 1], ring_at("y", step))
     for turn in range(2):
         for number, plan, kind, axis, at, source, slot in streams:
             up, down = turn, 1 - turn
@@ -100,14 +110,12 @@
         if kind == "kv":
             for h in range(2):
                 send(source(h), slot(at, h), pair_send.at[plan, h], pair_recv.at[plan, h], sibling())
-        for h in range(2):
-            copy = pltpu.make_async_copy(source(h), slot(at, h), own_sem.at[number, h])
-            copy.start()
-            own.append(copy)
-
-    def place(at, step):
-        return lax.rem(at + step + RING, RING)
-
+
+    own.wait()
+    for step in (1, 2, 3):
+        arrived(table_ref.at[c, z, place(y, -step)], table_recv.at[step - 1])
+    for step in (1, 2, 3):
+        send(table_ref.at[c, z], table_ref.at[c, z], table_send.at[2 + step], table_recv.at[2 + step], ring_at("z", step))
     for number, plan, kind, axis, at, source, slot in streams:
         before, after = slot(place(at, -1), 0), slot(place(at, 1), 1)
         arrived(before, ring_recv.at[number, 0])
@@ -117,6 +125,9 @@
         if kind == "kv":
             send(before, before, pair_send.at[plan, 2], pair_recv.at[plan, 2], sibling())
             send(after, after, pair_send.at[plan, 5], pair_recv.at[plan, 5], sibling())
+    for step in (1, 2, 3):
+        arrived(table_ref.at[c, place(z, -step)], table_recv.at[2 + step])
+    send(table_ref.at[c], table_ref.at[c], table_send.at[6], table_recv.at[6], sibling())
     for number, plan, kind, axis, at, source, slot in streams:
         before, after = slot(place(at, -1), 1), slot(place(at, 1), 0)
         arrived(before, ring_recv.at[number, 1])
@@ -135,13 +146,12 @@
             for index, step in enumerate((0, -1, 1, 2)):
                 for h in range(2):
                     arrived(kvg_ref.at[plan, place(at, step), 1 - c, part(h)], pair_recv.at[plan, 2 * index + h])
+    arrived(table_ref.at[1 - c], table_recv.at[6])
     for copy in sent:
         copy.wait_send()
-    for copy in own:
-        copy.wait()
-
-
-def gather(q_blocks, kv_blocks):
+
+
+def gather(q_blocks, kv_blocks, buckets):
     any_space = pl.BlockSpec(memory_space=pl.ANY)
     dma = pltpu.SemaphoreType.DMA
     return pl.pallas_call(
@@ -149,18 +159,54 @@
         out_shape=[
             jax.ShapeDtypeStruct((2, RING, LOCAL, PLAN_FEATURES, CSIZE), jnp.bfloat16),
             jax.ShapeDtypeStruct((2, RING, 2, LOCAL, 2 * PLAN_FEATURES, CSIZE), jnp.bfloat16),
+            jax.ShapeDtypeStruct((2, RING, RING, 1, 128), jnp.int32),
         ],
-        in_specs=[any_space] * 2,
-        out_specs=[any_space] * 2,
-        scratch_shapes=[dma((4, 6)), dma((4, 6)), dma((2, 8)), dma((2, 8)), dma((4, 2))],
+        in_specs=[any_space] * 3,
+        out_specs=[any_space] * 3,
+        scratch_shapes=[dma((4, 6)), dma((4, 6)), dma((2, 8)), dma((2, 8)), dma((7,)), dma((7,)), dma(())],
         compiler_params=pltpu.CompilerParams(collective_id=0, has_side_effects=True),
         name="gather",
-    )(q_blocks, kv_blocks)
-
-
-def tile_kernel(list_ref, bucket_ref, bias_ref, q_ref, kv_ref, part_ref, log_ref, m_ref, l_ref, acc_ref):
+    )(q_blocks, kv_blocks, buckets)
+
+
+def tile_kernel(
+    list_ref, bias_ref, own_q_ref, own_kv_ref, qg_ref, kvg_ref, table_hbm, part_ref, log_ref,
+    q_ref, kv_ref, table_ref, m_ref, l_ref, acc_ref, own_sem, q_sem, kv_sem, table_sem,
+):
     heads = range(PLAN_HEADS)
-    queries = q_ref.shape[0]
+    z, y, c = coordinates()
+    queries = part_ref.shape[0]
+    keys = 2 * queries
+
+    def load(source, target, sem):
+        copy = pltpu.make_async_copy(source, target, sem)
+        copy.start()
+        return copy
+
+    own, later = [load(table_hbm, table_ref, table_sem)], ([], [])
+    for plan in range(2):
+        q_at, kv_at = (z, y) if plan == 0 else (y, z)
+        q_own = pl.ds((plan * RING + q_at) * LOCAL, LOCAL)
+        kv_own = pl.ds(((plan * RING + kv_at) * 2 + c) * LOCAL, LOCAL)
+        own.append(load(own_q_ref.at[plan], q_ref.at[q_own], own_sem.at[plan, 0]))
+        own.append(load(own_kv_ref.at[plan], kv_ref.at[kv_own], own_sem.at[plan, 1]))
+    for plan in range(2):
+        q_at, kv_at = (z, y) if plan == 0 else (y, z)
+        for step in range(RING):
+            p = place(q_at, step)
+            if step > 0:
+                later[plan].append(load(
+                    qg_ref.at[plan, p], q_ref.at[pl.ds((plan * RING + p) * LOCAL, LOCAL)], q_sem.at[plan, step - 1]
+                ))
+            p = place(kv_at, step)
+            for other in range(2):
+                if step + other > 0:
+                    core = c if other == 0 else 1 - c
+                    later[plan].append(load(
+                        kvg_ref.at[plan, p, core],
+                        kv_ref.at[pl.ds(((plan * RING + p) * 2 + core) * LOCAL, LOCAL)],
+                        kv_sem.at[plan, 2 * step + other - 1],
+                    ))
     m_ref[...] = jnp.full(m_ref.shape, NEVER, jnp.float32)
     l_ref[...] = jnp.zeros(l_ref.shape, jnp.float32)
     acc_ref[...] = jnp.zeros(acc_ref.shape, jnp.float32)
@@ -177,8 +223,14 @@
             key = lax.bitwise_and(lax.shift_right_logical(item, 7), 127)
             tile = lax.bitwise_and(lax.shift_right_logical(item, 14), 2047)
             query = jnp.minimum(state, queries - 1)
-            head0 = jnp.where(key >= kv_ref.shape[0] // 2, PLAN_HEADS, 0)
-            bucket = jnp.where(tile >= 1024, 0, bucket_ref[jnp.minimum(tile, 1023)])
+            head0 = jnp.where(key >= keys // 2, PLAN_HEADS, 0)
+            named = jnp.minimum(tile, 1023)
+            worker = lax.shift_right_logical(named, 5)
+            bucket = table_ref[
+                lax.bitwise_and(worker, 1), lax.shift_right_logical(worker, 3),
+                lax.bitwise_and(lax.shift_right_logical(worker, 1), 3), 0, lax.bitwise_and(named, 31),
+            ]
+            bucket = jnp.where(tile >= 1024, 0, bucket)
             bias = [bias_ref[bucket * (2 * PLAN_HEADS) + head0 + h] * LOG2E for h in heads]
             scores = [
                 lax.dot_general(
@@ -213,7 +265,16 @@
                 acc_ref[state, rows(h), :] = old_acc[h] * keep[h] + mixed[h][:HEAD_SIZE] * fresh[h]
         return carry
 
-    lax.fori_loop(0, lax.div(list_ref[LIST_MAX] + UNROLL - 1, UNROLL), batch, 0)
+    for copy in own:
+        copy.wait()
+    lax.fori_loop(0, 2 * LOCAL // UNROLL, batch, 0)
+    for copy in later[0]:
+        copy.wait()
+    split = lax.div(list_ref[LIST_MAX], UNROLL)
+    lax.fori_loop(2 * LOCAL // UNROLL, split, batch, 0)
+    for copy in later[1]:
+        copy.wait()
+    lax.fori_loop(split, lax.div(list_ref[LIST_MAX + 1] + UNROLL - 1, UNROLL), batch, 0)
 
     def finish(group, carry):
         for local in range(LOCAL):
@@ -223,37 +284,215 @@
                 held = total > 0
                 safe = jnp.where(held, total, 1.0)
                 part_ref[state, rows(h), :] = (acc_ref[state, rows(h), :] * (1.0 / safe)).astype(jnp.bfloat16)
-                row = local * PLAN_HEADS + h
-                log_ref[group, row : row + 1, :] = m_ref[state, h : h + 1, :] + jnp.log2(safe)
+                row = local % 2 * PLAN_HEADS + h
+                log_ref[group, local // 2, row : row + 1, :] = m_ref[state, h : h + 1, :] + jnp.log2(safe)
         return carry
 
     lax.fori_loop(0, queries // LOCAL, finish, 0)
 
 
-def tiles(items, buckets, bias, q_all, kv_all):
-    queries = q_all.shape[0]
+def tiles(items, bias, own_q, own_kv, q_all, kv_all, table):
+    queries, keys = 2 * RING * LOCAL, 2 * RING * 2 * LOCAL
+    any_space = pl.BlockSpec(memory_space=pl.ANY)
     whole = lambda shape: pl.BlockSpec(shape, lambda i, *_: (0,) * len(shape))
-    log_shape = (queries // LOCAL, LOCAL * PLAN_HEADS, CSIZE)
+    part_shape = (queries, PLAN_FEATURES, CSIZE)
+    log_shape = (2 * RING, RING, 8, CSIZE)
+    dma = pltpu.SemaphoreType.DMA
     return pl.pallas_call(
         tile_kernel,
         grid_spec=pltpu.PrefetchScalarGridSpec(
-            num_scalar_prefetch=3,
+            num_scalar_prefetch=2,
             grid=(1,),
-            in_specs=[whole(q_all.shape), whole(kv_all.shape)],
-            out_specs=[whole(q_all.shape), whole(log_shape)],
+            in_specs=[any_space] * 5,
+            out_specs=[whole(part_shape), whole(log_shape)],
             scratch_shapes=[
+                pltpu.VMEM((queries, PLAN_FEATURES, CSIZE), jnp.bfloat16),
+                pltpu.VMEM((keys, 2 * PLAN_FEATURES, CSIZE), jnp.bfloat16),
+                pltpu.SMEM((2, RING, RING, 1, 128), jnp.int32),
                 pltpu.VMEM((queries + 1, 8, CSIZE), jnp.float32),
                 pltpu.VMEM((queries + 1, 8, CSIZE), jnp.float32),
                 pltpu.VMEM((queries + 1, PLAN_FEATURES, CSIZE), jnp.float32),
+                dma((2, 2)), dma((2, 3)), dma((2, 7)), dma(()),
             ],
         ),
         out_shape=[
-            jax.ShapeDtypeStruct(q_all.shape, jnp.bfloat16),
+            jax.ShapeDtypeStruct(part_shape, jnp.bfloat16),
             jax.ShapeDtypeStruct(log_shape, jnp.float32),
         ],
         compiler_params=pltpu.CompilerParams(vmem_limit_bytes=56 * 2**20),
         name="tiles",
-    )(items, buckets, bias, q_all, kv_all)
+    )(items, bias, own_q, own_kv, q_all, kv_all, table)
+
+
+def tail_kernel(
+    part_ref, log_ref, nodes_ref, wo_hbm, up_hbm, down_hbm, out_ref,
+    wo_ref, up_ref, down_ref, rows_ref, part_in, log_in, own_part, own_log, merged, gathered, resid_ref, normed_ref, staged,
+    weight_sem, own_sem, part_send, part_recv, log_send, log_recv, x_send, x_recv, out_send, out_recv, out_own,
+):
+    z, y, c = coordinates()
+    me = lax.axis_index("owner")
+    x = lax.axis_index("head")
+    heads = range(PLAN_HEADS)
+    features = 2 * PLAN_FEATURES
+
+    def load(source, target, sem):
+        copy = pltpu.make_async_copy(source, target, sem)
+        copy.start()
+        return copy
+
+    def across(step):
+        return (me, place(x, step))
+
+    ready = []
+    for plan in range(2):
+        at = z if plan == 0 else y
+        ready.append(load(part_ref.at[plan, at], own_part.at[plan], own_sem.at[plan, 0]))
+        ready.append(load(log_ref.at[plan, at], own_log.at[plan], own_sem.at[plan, 1]))
+    weights = [
+        load(nodes_ref.at[pl.ds(x * 2 * CSIZE, 2 * CSIZE)], rows_ref, weight_sem.at[0]),
+        load(wo_hbm, wo_ref, weight_sem.at[1]),
+        load(up_hbm, up_ref, weight_sem.at[2]),
+        load(down_hbm, down_ref, weight_sem.at[3]),
+    ]
+    greet([ring_at(axis, step) for axis in "zy" for step in (1, 2, 3)] + [across(step) for step in (1, 2, 3)])
+    sent = []
+
+    def send(src, dst, send_sem, recv_sem, device):
+        copy = pltpu.make_async_remote_copy(
+            src_ref=src, dst_ref=dst, send_sem=send_sem, recv_sem=recv_sem,
+            device_id=device, device_id_type=MESH,
+        )
+        copy.start()
+        sent.append(copy)
+
+    def arrived(ref, sem):
+        pltpu.make_async_remote_copy(
+            src_ref=ref, dst_ref=ref, send_sem=x_send.at[0], recv_sem=sem,
+            device_id=across(1), device_id_type=MESH,
+        ).wait_recv()
+
+    for turn in range(RING):
+        chunk = place(x, turn + 1)
+        for plan, axis in enumerate("zy"):
+            at = z if plan == 0 else y
+            for step in (2, 1, 3):
+                to = place(at, step)
+                send(
+                    part_ref.at[plan, to, pl.ds(chunk * 2, 2)], part_in.at[plan, step - 1, pl.ds(chunk * 2, 2)],
+                    part_send.at[plan, step - 1, turn], part_recv.at[plan, step - 1, turn], ring_at(axis, step),
+                )
+                send(
+                    log_ref.at[plan, to, chunk], log_in.at[plan, step - 1, chunk],
+                    log_send.at[plan, step - 1, turn], log_recv.at[plan, step - 1, turn], ring_at(axis, step),
+                )
+    for copy in ready:
+        copy.wait()
+    for turn in range(RING):
+        chunk = place(x, turn + 1)
+        for plan in range(2):
+            for step in (2, 1, 3):
+                arrived(part_in.at[plan, step - 1, pl.ds(chunk * 2, 2)], part_recv.at[plan, step - 1, turn])
+                arrived(log_in.at[plan, step - 1, chunk], log_recv.at[plan, step - 1, turn])
+        for plan in range(2):
+            logs = [own_log[plan, chunk]] + [log_in[plan, i, chunk] for i in range(3)]
+            best = jnp.maximum(jnp.maximum(logs[0], logs[1]), jnp.maximum(logs[2], logs[3]))
+            shares = [jnp.exp2(log - best) for log in logs]
+            scale = 1.0 / (shares[0] + shares[1] + shares[2] + shares[3])
+            shares = [share * scale for share in shares]
+            for local in range(2):
+                for h in heads:
+                    row = local * PLAN_HEADS + h
+                    rows = slice(HEAD_SIZE * h, HEAD_SIZE * (h + 1))
+                    total = own_part[plan, chunk * 2 + local, rows, :].astype(jnp.float32) * shares[0][row : row + 1]
+                    for i in range(3):
+                        total += part_in[plan, i, chunk * 2 + local, rows, :].astype(jnp.float32) * shares[i + 1][row : row + 1]
+                    first = plan * PLAN_FEATURES + HEAD_SIZE * h
+                    merged[turn, local, first : first + HEAD_SIZE, :] = total.astype(jnp.bfloat16)
+        if turn < RING - 1:
+            send(
+                merged.at[turn], gathered.at[:, pl.ds(pl.multiple_of(x * features, 64), features), :],
+                x_send.at[turn], x_recv.at[turn], across(turn + 1),
+            )
+    gathered[:, pl.ds(pl.multiple_of(x * features, 64), features), :] = merged[RING - 1]
+    for turn in range(RING - 1):
+        source = place(x, -(turn + 1))
+        arrived(gathered.at[:, pl.ds(pl.multiple_of(source * features, 64), features), :], x_recv.at[turn])
+    for copy in weights:
+        copy.wait()
+    out_copies = []
+    for local in range(2):
+        rows = slice(local * CSIZE, (local + 1) * CSIZE)
+        mixed = lax.dot_general(
+            gathered[local], wo_ref[...], (((0,), (0,)), ((), ())), preferred_element_type=jnp.float32
+        )
+        resid = rows_ref[rows, :].astype(jnp.float32) + mixed
+        resid_ref[rows, :] = resid
+        normed_ref[rows, :] = norm_rows(resid).astype(jnp.bfloat16)
+    wide = up_ref.shape[1] // RING
+    for local in range(2):
+        rows = slice(local * CSIZE, (local + 1) * CSIZE)
+
+        def block(step, carry):
+            units = pl.ds(pl.multiple_of(step * wide, 128), wide)
+            hidden = jax.nn.gelu(
+                jnp.dot(normed_ref[rows, :], up_ref[:, units], preferred_element_type=jnp.float32)
+            ).astype(jnp.bfloat16)
+            resid_ref[rows, :] += jnp.dot(hidden, down_ref[units, :], preferred_element_type=jnp.float32)
+            return carry
+
+        lax.fori_loop(0, RING, block, 0)
+        result = resid_ref[rows, :].astype(jnp.bfloat16)
+        for j in range(RING):
+            staged[j, rows, :] = result[:, features * j : features * (j + 1)]
+        target = out_ref.at[pl.ds(x * 2 * CSIZE + local * CSIZE, CSIZE)]
+        for step in (2, 1, 3):
+            send(
+                staged.at[place(x, step), rows], target,
+                out_send.at[local, step - 1], out_recv.at[local, step - 1], across(step),
+            )
+        out_copies.append(load(staged.at[x, rows], target, out_own.at[local]))
+    for local in range(2):
+        for step in (1, 2, 3):
+            source = place(x, -step)
+            arrived(out_ref.at[pl.ds(source * 2 * CSIZE + local * CSIZE, CSIZE)], out_recv.at[local, step - 1])
+    for copy in out_copies:
+        copy.wait()
+    for copy in sent:
+        copy.wait_send()
+
+
+def tail(parts, logs, nodes, out_weight, up_weight, down_weight):
+    any_space = pl.BlockSpec(memory_space=pl.ANY)
+    dma, vmem = pltpu.SemaphoreType.DMA, pltpu.VMEM
+    width = nodes.shape[1]
+    features = 2 * PLAN_FEATURES
+    return pl.pallas_call(
+        tail_kernel,
+        out_shape=jax.ShapeDtypeStruct((nodes.shape[0], features), jnp.bfloat16),
+        in_specs=[any_space] * 6,
+        out_specs=any_space,
+        scratch_shapes=[
+            vmem(out_weight.shape, jnp.bfloat16),
+            vmem(up_weight.shape, jnp.bfloat16),
+            vmem(down_weight.shape, jnp.bfloat16),
+            vmem((2 * CSIZE, width), jnp.bfloat16),
+            vmem((2, 3, LOCAL, PLAN_FEATURES, CSIZE), jnp.bfloat16),
+            vmem((2, 3, RING, 8, CSIZE), jnp.float32),
+            vmem((2, LOCAL, PLAN_FEATURES, CSIZE), jnp.bfloat16),
+            vmem((2, RING, 8, CSIZE), jnp.float32),
+            vmem((RING, 2, features, CSIZE), jnp.bfloat16),
+            vmem((2, width, CSIZE), jnp.bfloat16),
+            vmem((2 * CSIZE, width), jnp.float32),
+            vmem((2 * CSIZE, width), jnp.bfloat16),
+            vmem((RING, 2 * CSIZE, features), jnp.bfloat16),
+            dma((4,)), dma((2, 2)), dma((2, 3, 4)), dma((2, 3, 4)), dma((2, 3, 4)), dma((2, 3, 4)),
+            dma((3,)), dma((3,)), dma((2, 3)), dma((2, 3)), dma((2,)),
+        ],
+        compiler_params=pltpu.CompilerParams(
+            collective_id=1, has_side_effects=True, vmem_limit_bytes=56 * 2**20
+        ),
+        name="tail",
+    )(parts, logs, nodes, out_weight, up_weight, down_weight)
 
 
 def tile_list(key_owner, key_local, query_owner, query_local):
@@ -274,27 +513,29 @@
     row = jnp.arange(16)
     inside = jnp.dot(ones, (lane[:, None] < lane[None, :]).astype(jnp.float32))
     counts = jnp.sum(ones, axis=1)
+    filler = -jnp.sum(counts[:8]).astype(jnp.int32) % UNROLL
     ahead = jnp.sum(jnp.where(row[None, :] < row[:, None], counts[None, :], 0.0), axis=1)
     rank = (inside + ahead[:, None]).astype(jnp.int32) + 16
+    rank = rank + jnp.where(row[:, None] < 8, 0, filler)
     rank = jnp.where(mine, rank, -1).reshape(2048)
     own = jnp.arange(8, dtype=jnp.int32)
     own_a = (z * 8 + own) + ((y * 16 + c * 8 + own) << 7) + (1024 << 14)
     own_b = (32 + y * 8 + own) + ((64 + z * 16 + c * 8 + own) << 7) + (1024 << 14)
-    place = jnp.arange(LIST_MAX, dtype=jnp.int32)
-    total = jnp.sum(counts).astype(jnp.int32) + 16
-    listed = jnp.sum(jnp.where(place[:, None] == rank[None, :], items.reshape(2048)[None, :], 0), axis=1)
-    listed = jnp.where(place < total, listed, 64 + (1024 << 14))
-    return jnp.concatenate([own_a, own_b, listed[16:], total[None]])
+    slot = jnp.arange(LIST_MAX, dtype=jnp.int32)
+    total = jnp.sum(counts).astype(jnp.int32) + 16 + filler
+    split = jnp.sum(counts[:8]).astype(jnp.int32) + 16 + filler
+    nothing = 64 + (1024 << 14)
+    listed = nothing + jnp.sum(
+        jnp.where(slot[:, None] == rank[None, :], items.reshape(2048)[None, :] - nothing, 0), axis=1
+    )
+    return jnp.concatenate([own_a, own_b, listed[16:], split[None], total[None]])
 
 
 def per_device(
     nodes, qkv_weight, out_weight, hop_bias, up_weight, down_weight,
     key_owner, key_local, query_owner, query_local, hop_bucket,
 ):
-    head_rank = lax.axis_index("head")
-    model_width = nodes.shape[1]
     items = tile_list(key_owner, key_local, query_owner, query_local)
-    buckets = lax.all_gather(hop_bucket, "owner", axis=0, tiled=True)
     normed = norm_rows(nodes.astype(jnp.float32)).astype(jnp.bfloat16)
     projected = jnp.einsum("sdf,rd->sfr", qkv_weight, normed, preferred_element_type=jnp.float32)
     q_rows = (projected[0] * (LOG2E / math.sqrt(HEAD_SIZE))).astype(jnp.bfloat16)
@@ -305,36 +546,13 @@
         .transpose(1, 3, 0, 2, 4)
         .reshape(2, LOCAL, 2 * PLAN_FEATURES, CSIZE)
     )
-    q_all, kv_all = gather(q_blocks, kv_blocks)
-    parts, logs = tiles(
-        items, buckets, hop_bias.reshape(-1),
-        q_all.reshape(2 * RING * LOCAL, PLAN_FEATURES, CSIZE),
-        kv_all.reshape(2 * RING * 2 * LOCAL, 2 * PLAN_FEATURES, CSIZE),
+    buckets = jnp.pad(hop_bucket, (0, 128 - hop_bucket.shape[0]))[None]
+    q_all, kv_all, table = gather(q_blocks, kv_blocks, buckets)
+    parts, logs = tiles(items, hop_bias.reshape(-1), q_blocks, kv_blocks, q_all, kv_all, table)
+    return tail(
+        parts.reshape(2, RING, LOCAL, PLAN_FEATURES, CSIZE), logs.reshape(2, RING, RING, 8, CSIZE),
+        nodes, out_weight, up_weight, down_weight,
     )
-    parts = parts.reshape(2, RING, LOCAL, PLAN_HEADS, HEAD_SIZE, CSIZE)
-    logs = logs.reshape(2, RING, LOCAL, PLAN_HEADS, CSIZE)
-    along_z = [[(z * 4 + y) * 2 + c for z in range(4)] for y in range(4) for c in range(2)]
-    along_y = [[(z * 4 + y) * 2 + c for y in range(4)] for z in range(4) for c in range(2)]
-    back = lambda x, groups: lax.all_to_all(x, "owner", 0, 0, axis_index_groups=groups, tiled=True)
-    merged = []
-    for plan, groups in enumerate((along_z, along_y)):
-        part, log = back(parts[plan], groups), back(logs[plan], groups)
-        share = jnp.exp2(log - jnp.max(log, axis=0))
-        share = share / jnp.sum(share, axis=0)
-        merged.append(jnp.sum(share[:, :, :, None, :] * part.astype(jnp.float32), axis=0).astype(jnp.bfloat16))
-    attention = jnp.concatenate(merged, axis=1).reshape(LOCAL, 2 * PLAN_FEATURES, CSIZE)
-    attention = lax.all_to_all(attention, "head", 0, 0, tiled=True).reshape(4, 2, 2 * PLAN_FEATURES, CSIZE)
-    mixed = jnp.einsum(
-        "xcfr,xfd->crd", attention, out_weight.reshape(4, 2 * PLAN_FEATURES, model_width),
-        preferred_element_type=jnp.float32,
-    ).reshape(2 * CSIZE, model_width)
-    resid = lax.dynamic_slice_in_dim(nodes, head_rank * 2 * CSIZE, 2 * CSIZE, 0).astype(jnp.float32) + mixed
-    normed_again = norm_rows(resid).astype(jnp.bfloat16)
-    hidden = jax.nn.gelu(
-        jnp.dot(normed_again, up_weight, preferred_element_type=jnp.float32)
-    ).astype(jnp.bfloat16)
-    out = (resid + jnp.dot(hidden, down_weight, preferred_element_type=jnp.float32)).astype(jnp.bfloat16)
-    return lax.all_to_all(out, "head", 1, 0, tiled=True)
 
 
 def solution(mesh):

time: 249 us -> 147 us (0.59)
  blocking collectives: 50.4 us -> 0 us
  waiting for transfers between devices: 30.9 us -> 0 us
  Pallas kernels: 106 us -> 125 us
  starting transfers between devices: 18 us -> 0 us
  matrix products: 14.6 us -> 4.08 us
  local copies, waits for them, and re-layouts: 15.4 us -> 9.53 us
  other arithmetic: 11.6 us -> 6.43 us
    pallas_call x0 -> x1, Pallas kernels: none -> 52 us  [tail(): pl.pallas_call(tail_kernel, out_shape=jax.ShapeDtypeStruct((nodes.shape[0...]
    all_to_all x2 -> x0, blocking collectives: 31.6 us -> none  [the longest x1 19.7 us: per_device(): lax.all_to_all(x, 'owner', 0, 0, axis_index_groups=groups, tiled=True)]
    all_to_all x4 -> x0, waiting for transfers between devices: 30.9 us -> none  [the longest x3 21.4 us: per_device(): lax.all_to_all(x, 'owner', 0, 0, axis_index_groups=groups, tiled=True)]
    pallas_call x1, Pallas kernels: 74 us -> 49.1 us  [gather(): pl.pallas_call(gather_kernel, out_shape=[jax.ShapeDtypeStruct((2, RING, L...]
    unnamed x1 -> x0, blocking collectives: 18.8 us -> none
    all_to_all x4 -> x0, starting transfers between devices: 18 us -> none  [the longest x3 13.7 us: per_device(): lax.all_to_all(x, 'owner', 0, 0, axis_index_groups=groups, tiled=True)]
    dot_general x2 -> x0, matrix products: 11.2 us -> none  [the longest x1 9.12 us: per_device(): jnp.dot(hidden, down_weight, preferred_element_type=jnp.float32)]
    pallas_call x1, Pallas kernels: 32 us -> 23.8 us  [tiles(): pl.pallas_call(tile_kernel, grid_spec=pltpu.PrefetchScalarGridSpec(num_sc...]
  transfers between devices with their start and end apart: 4 -> 0, of which waited for: 4 -> 0; matrix products, arithmetic and copies ran while one was open for 2% -> 0% of each run, Pallas kernels for 0% -> 0%
where the time goes in v2:
time: 147 us; the launch traced here: 146 us
  Pallas kernels  125 us (85%)
  local copies, waits for them, and re-layouts  9.53 us (6%)
  other arithmetic  6.43 us (4%)
  matrix products  4.08 us (3%)
  between operations  1.53 us (1%)
    pallas_call x1, Pallas kernels, tail(): pl.pallas_call(tail_kernel, out_shape=jax.ShapeDtypeStruct((nodes.shape[0...  52 us
    pallas_call x1, Pallas kernels, gather(): pl.pallas_call(gather_kernel, out_shape=[jax.ShapeDtypeStruct((2, RING, L...  49.1 us
    pallas_call x1, Pallas kernels, tiles(): pl.pallas_call(tile_kernel, grid_spec=pltpu.PrefetchScalarGridSpec(num_sc...  23.8 us
    unnamed x1, matrix products  3.99 us

profile of v2, /device:TPU:0, one launch (start us, length us, event | category | flops | bytes accessed | tf_op | source)
XLA Modules:
  0.0 146.5 jit_solution(10019886903685203707)
XLA Ops:
  0.0 0.0 copy-start
  0.0 0.0 copy-start.3
  0.0 0.0 copy-start.4
  0.1 1.1 copy-done
  1.2 1.2 pad_bitcast_fusion.bucket_ref
  2.4 0.7 compare_and_fusion.1
  3.1 0.6 convert_reduce_fusion.1
  4.4 0.6 slice_reduce_fusion
  5.7 0.0 copy-start.1
  5.7 0.1 select_reduce_fusion.1
  5.8 0.1 fusion.13
  5.9 2.6 %convert_reduce_fusion = f32[2048]{0:T(1024)S(1)} fusion(bf16[2048,768]{1,0:T(8,128)(2,1)} %nodes_ref.1), kind=kLoop, calls=%fused_computation.1 | loop fusion | flops 3143680 | bytes 3153920 | tf_op jit(solution)/shard_map/reduce_sum | solution.py:26
  8.5 0.0 copy-done.1
  8.5 1.1 fusion.2
  9.6 0.0 copy-done.6
  9.6 0.0 copy-done.2
  9.7 0.5 select_reduce_fusion
  10.2 0.1 slice.15
  10.3 0.7 concatenate.11.list_ref
  11.0 0.1 copy.18
  11.1 0.6 reshape.81.bias_ref
  11.7 4.0 %fusion.4 = f32[2048,576]{0,1:S(1)} fusion(bf16[768,576]{0,1:T(8,128)(2,1)S(1)} %bitcast.55, bf16[2048,768]{1,0:T(8,128)(2,1)} %nodes_ref.1, f32[2048]{0:T(1024)S(1)} %add_rsqrt_fusion, f32[2048]{0:T(1024)S(1)} %broadcast_multiply_fusion), kind=kOutput, calls=%fused_computation.8 | convolution fusion | flops 1818230784 | bytes 8765440
  15.7 0.1 fusion.8
  15.9 0.2 slice.25
  16.1 0.5 copy.23
  16.6 1.5 %copy.20 = bf16[2,2,96,8,256]{4,2,0,3,1:T(8,128)(2,1)} copy(bf16[2,2,96,8,256]{4,3,2,1,0:T(8,128)(2,1)S(1)} %bitcast.61) | data formatting | bytes 3145728 | tf_op jit(solution)/shard_map/reshape | solution.py:545
  18.1 0.2 copy.22
  18.3 1.1 copy.25
  19.4 49.1 %gather.1 = (bf16[2,4,8,96,256]{4,3,2,1,0:T(8,128)(2,1)}, bf16[2,4,2,8,192,256]{5,4,3,2,1,0:T(8,128)(2,1)}, s32[2,4,4,1,128]{4,3,2,1,0:T(1,128)}) custom-call(bf16[2,8,96,256]{3,2,1,0:T(8,128)(2,1)} %bitcast.58, bf16[2,8,192,256]{3,2,1,0:T(8,128)(2,1)} %bitcast.56, s32[1,128]{1,0:T(1,128)} %pad_bitcast_fusion.bucket_ref), custom_call_target="tpu_custom_call" | custom-call | tf_op jit(solution)/shard_map/gather/pallas_call | solution.py:157
  68.5 23.8 %tiles.1 = (bf16[64,96,256]{2,1,0:T(8,128)(2,1)}, f32[8,4,8,256]{3,2,1,0:T(8,128)}) custom-call(s32[546]{0:T(1024)} %concatenate.11.list_ref, f32[192]{0:T(256)} %reshape.81.bias_ref, bf16[2,8,96,256]{3,2,1,0:T(8,128)(2,1)} %bitcast.59, bf16[2,8,192,256]{3,2,1,0:T(8,128)(2,1)} %bitcast.57, bf16[2,4,8,96,256]{4,3,2,1,0:T(8,128)(2,1)} %get-tuple-element.10.qg_ref, ...), custom_call_target="tpu_custom_call" | custom-call | tf_op jit(solution)/shard_map/tiles/pallas_call | solution.py:301
  92.3 52.0 %tail.1 = bf16[2048,192]{1,0:T(8,128)(2,1)} custom-call(bf16[2,4,8,96,256]{4,3,2,1,0:T(8,128)(2,1)} %bitcast.64, f32[2,4,4,8,256]{4,3,2,1,0:T(8,128)} %bitcast.67, bf16[2048,768]{1,0:T(8,128)(2,1)} %nodes_ref.1, bf16[768,768]{1,0:T(8,128)(2,1)} %wo_hbm.1, bf16[768,3072]{1,0:T(8,128)(2,1)} %up_hbm.1, bf16[3072,768]{1,0:T(8,128)(2,1)} %down_hbm.1), custom_call_target="tpu_custom_call" | custom-call | tf_op jit(solution)/shard_map/tail/pallas_call | solution.py:469
  144.3 2.2 %copy.21 = bf16[2048,192]{0,1:T(8,128)(2,1)} copy(bf16[2048,192]{1,0:T(8,128)(2,1)} %tail.1) | data formatting | bytes 1572864 | tf_op jit(solution)/shard_map/tail/pallas_call | solution.py:469
  (13 shorter events, 0.1 us)
Async XLA Ops:
  0.0 1.2 copy-start
  0.0 9.6 %copy-start.6 = (s32[1024]{0:T(1024)S(1)}, s32[1024]{0:T(1024)}, u32[]{:S(2)}) copy-start(s32[1024]{0:T(1024)} %param.20) | copy-start | bytes 12292
  0.0 9.6 %copy-start.2 = (s32[1024,1]{0,1:T(1,128)S(1)}, s32[1024,1]{0,1:T(1,128)}, u32[]{:S(2)}) copy-start(s32[1024,1]{0,1:T(1,128)} %param.19) | copy-start | bytes 12292
  0.0 9.6 %copy-start.5 = (s32[1024]{0:T(1024)S(1)}, s32[1024]{0:T(1024)}, u32[]{:S(2)}) copy-start(s32[1024]{0:T(1024)} %param.18) | copy-start | bytes 12292
  0.0 9.6 %copy-start.3 = (s32[1024,1]{0,1:T(1,128)S(1)}, s32[1024,1]{0,1:T(1,128)}, u32[]{:S(2)}) copy-start(s32[1024,1]{0,1:T(1,128)} %param.17) | copy-start | bytes 12292
  0.0 11.0 %copy-start.4 = (f32[32,6]{0,1:T(8,128)S(1)}, f32[32,6]{0,1:T(8,128)}, u32[]{:S(2)}) copy-start(f32[32,6]{0,1:T(8,128)} %param.14) | copy-start | bytes 2308
  5.7 2.8 %copy-start.1 = (bf16[2048,768]{1,0:T(8,128)(2,1)S(1)}, bf16[2048,768]{1,0:T(8,128)(2,1)}, u32[]{:S(2)}) copy-start(bf16[2048,768]{1,0:T(8,128)(2,1)} %nodes_ref.1) | copy-start | bytes 9437188

commit v3 on v2

v3 whole, which is shorter than its diff:
```python
import functools
import math

import jax
import jax.numpy as jnp
from jax import lax
from jax.experimental import pallas as pl
from jax.experimental.pallas import tpu as pltpu
from jax.sharding import PartitionSpec as P

CSIZE = 256
EPSILON = 1e-05
RING = 4
LOCAL = 8
PLAN_HEADS = 3
HEAD_SIZE = 32
PLAN_FEATURES = PLAN_HEADS * HEAD_SIZE
LIST_MAX = 640
UNROLL = 4
MESH = pl.DeviceIdType.MESH
LOG2E = math.log2(math.e)
NEVER = -1e30
NOTHING = 64


def norm_rows(values):
    center = values - jnp.mean(values, axis=-1, keepdims=True)
    spread = jnp.mean(center * center, axis=-1, keepdims=True)
    return center * lax.rsqrt(spread + EPSILON)


def coordinates():
    me = lax.axis_index("owner")
    return lax.div(me, 8), lax.rem(lax.div(me, 2), 4), lax.rem(me, 2)


def place(at, step):
    return lax.rem(at + step + RING, RING)


def ring_at(axis, step):
    z, y, c = coordinates()
    if axis == "z":
        z = place(z, step)
    else:
        y = place(y, step)
    return ((z * 4 + y) * 2 + c, lax.axis_index("head"))


def sibling():
    z, y, c = coordinates()
    return ((z * 4 + y) * 2 + 1 - c, lax.axis_index("head"))


def greet(partners):
    barrier = pltpu.get_barrier_semaphore()
    for partner in partners:
        pl.semaphore_signal(barrier, inc=1, device_id=partner, device_id_type=MESH)
    pl.semaphore_wait(barrier, len(partners))


def rows(h, first=0):
    return slice(first + HEAD_SIZE * h, first + HEAD_SIZE * (h + 1))


def attend(pairs):
    heads = range(PLAN_HEADS)
    ones = jnp.ones((16, CSIZE), jnp.bfloat16)
    scored = [
        [
            lax.dot_general(key(h), query(h), (((0,), (0,)), ((), ())), preferred_element_type=jnp.float32)
            for h in heads
        ]
        for query, key, value in pairs
    ]
    done = []
    for (query, key, value), scores in zip(pairs, scored):
        highest = [jnp.max(s, axis=0, keepdims=True) for s in scores]
        weights = [jnp.exp2(s - top).astype(jnp.bfloat16) for s, top in zip(scores, highest)]
        mixed = [
            jnp.dot(jnp.concatenate([value(h), ones], 0), weights[h], preferred_element_type=jnp.float32)
            for h in heads
        ]
        done.append((highest, mixed))
    return done


def make_list(query_owner, query_local, key_owner, key_local):
    z, y, c = coordinates()
    div, rem = lax.div, lax.rem
    qz, qy, qc = div(query_owner, 8), rem(div(query_owner, 2), 4), rem(query_owner, 2)
    kz, ky, kc = div(key_owner, 8), rem(div(key_owner, 2), 4), rem(key_owner, 2)
    iota = lax.broadcasted_iota
    number = iota(jnp.int32, (8, 128), 0) * 128 + iota(jnp.int32, (8, 128), 1)
    mine_a = (qy == y) & (qc == c) & (kz == z)
    mine_b = (qz == z) & (qc == c) & (ky == y)
    item_a = (qz * 8 + query_local) + (ky * 16 + kc * 8 + key_local) * 128 + number * 16384
    item_b = (32 + qy * 8 + query_local) + (64 + kz * 16 + kc * 8 + key_local) * 128 + number * 16384
    zero, one = jnp.zeros((8, 128), jnp.float32), jnp.ones((8, 128), jnp.float32)
    ones = jnp.concatenate([jnp.where(mine_a, one, zero), jnp.where(mine_b, one, zero)], 0)
    items = jnp.concatenate([item_a, item_b], 0).astype(jnp.float32)
    before = jnp.where(iota(jnp.int32, (128, 128), 0) < iota(jnp.int32, (128, 128), 1), 1.0, 0.0)
    inside = jnp.dot(ones, before, preferred_element_type=jnp.float32)
    counts = jnp.sum(ones, axis=1, keepdims=True)
    row = iota(jnp.int32, (16, 128), 0)
    wide = jnp.broadcast_to(counts, (16, 128))
    first = jnp.sum(jnp.where(row < 8, wide, 0.0), axis=0, keepdims=True)
    filled = jnp.floor((first + (UNROLL - 1)) * (1.0 / UNROLL)) * UNROLL
    total = filled + jnp.sum(jnp.where(row >= 8, wide, 0.0), axis=0, keepdims=True)
    ahead = [jnp.zeros((1, 128), jnp.float32)]
    for r in range(15):
        ahead.append(ahead[-1] + wide[r : r + 1] if r != 7 else filled)
    rank = jnp.where(ones > 0, inside + jnp.concatenate(ahead, 0), -1.0).T
    values = items.T - NOTHING
    place = iota(jnp.int32, (128, LIST_MAX), 1).astype(jnp.float32)
    listed = jnp.zeros((128, LIST_MAX), jnp.float32)
    for r in range(16):
        listed += jnp.where(rank[:, r : r + 1] == place, values[:, r : r + 1], 0.0)
    listed = jnp.sum(listed, axis=0, keepdims=True) + NOTHING
    at = iota(jnp.int32, (1, LIST_MAX), 1)
    repeat = lambda v: jnp.concatenate([v] * (LIST_MAX // 128), 1)
    listed = jnp.where(at == LIST_MAX - 2, repeat(filled), listed)
    listed = jnp.where(at == LIST_MAX - 1, repeat(total), listed)
    return listed.astype(jnp.int32)


def gather_kernel(
    nodes_hbm, weight_hbm, bias_ref, bucket_ref, ko_ref, kl_ref, qo_ref, ql_ref,
    qg_ref, kvg_ref, table_ref, list_out, m_out, l_out, acc_out,
    nodes_ref, weight_ref, turned_ref, q_ref, kv_ref, bucket_row, list_ref, m_ref, l_ref, acc_ref,
    ring_send, ring_recv, pair_send, pair_recv, table_send, table_recv, own_sem, load_sem, weight_sem, store_sem,
):
    z, y, c = coordinates()
    half = LOCAL // 2
    heads = range(PLAN_HEADS)

    def local_copy(source, target, sem):
        copy = pltpu.make_async_copy(source, target, sem)
        copy.start()
        return copy

    weight_loads = [local_copy(weight_hbm.at[i], weight_ref.at[i], weight_sem.at[i]) for i in range(3)]
    node_rows = lambda h: pl.ds(h * half * CSIZE, half * CSIZE)
    node_loads = [local_copy(nodes_hbm.at[node_rows(h)], nodes_ref.at[node_rows(h)], load_sem.at[h]) for h in range(2)]
    bucket_row[...] = jnp.zeros(bucket_row.shape, jnp.int32)
    bucket_row[:, : bucket_ref.shape[1]] = bucket_ref[...]
    stores = [local_copy(bucket_row, table_ref.at[c, z, y], store_sem.at[4])]
    greet([ring_at(axis, step) for axis in "zy" for step in (1, 2, 3)] + [sibling()])
    sent = []

    def part(h):
        return pl.ds(h * half, half)

    streams = []
    for plan in range(2):
        q_axis, kv_axis = ("z", "y") if plan == 0 else ("y", "z")
        for kind, axis in (("kv", kv_axis), ("q", q_axis)):
            at = z if axis == "z" else y
            if kind == "q":
                source = lambda h, plan=plan: q_ref.at[plan, part(h)]
                slot = lambda p, h, plan=plan: qg_ref.at[plan, p, part(h)]
            else:
                source = lambda h, plan=plan: kv_ref.at[plan, part(h)]
                slot = lambda p, h, plan=plan: kvg_ref.at[plan, p, c, part(h)]
            streams.append((len(streams), plan, kind, axis, at, source, slot))

    def send(src, dst, send_sem, recv_sem, device):
        copy = pltpu.make_async_remote_copy(
            src_ref=src, dst_ref=dst, send_sem=send_sem, recv_sem=recv_sem,
            device_id=device, device_id_type=MESH,
        )
        copy.start()
        sent.append(copy)

    def arrived(ref, sem):
        pltpu.make_async_remote_copy(
            src_ref=ref, dst_ref=ref, send_sem=ring_send.at[0, 0], recv_sem=sem,
            device_id=sibling(), device_id_type=MESH,
        ).wait_recv()

    for step in (1, 2, 3):
        send(bucket_row, table_ref.at[c, z, y], table_send.at[step - 1], table_recv.at[step - 1], ring_at("y", step))
    for copy in weight_loads:
        copy.wait()
    for i in range(3):
        turned_ref[i] = weight_ref[i].T
    features = 2 * PLAN_FEATURES

    def project(cluster, carry):
        normed = norm_rows(nodes_ref[pl.ds(cluster * CSIZE, CSIZE), :].astype(jnp.float32)).astype(jnp.bfloat16)
        for i in range(3):
            projected = lax.dot_general(
                turned_ref[i], normed, (((1,), (1,)), ((), ())), preferred_element_type=jnp.float32
            )
            if i == 0:
                projected = projected * (LOG2E / math.sqrt(HEAD_SIZE))
            projected = projected.astype(jnp.bfloat16)
            for plan in range(2):
                block = projected[plan * PLAN_FEATURES : (plan + 1) * PLAN_FEATURES]
                if i == 0:
                    q_ref[plan, cluster] = block
                else:
                    kv_ref[plan, cluster, (i - 1) * PLAN_FEATURES : i * PLAN_FEATURES, :] = block
        return carry

    for h in range(2):
        node_loads[h].wait()
        lax.fori_loop(h * half, (h + 1) * half, project, 0)
        for wanted in ("kv", "q"):
            for number, plan, kind, axis, at, source, slot in streams:
                if kind == wanted:
                    send(source(h), slot(at, h), ring_send.at[number, h], ring_recv.at[number, h], ring_at(axis, 1))
                    send(source(h), slot(at, h), ring_send.at[number, 2 + h], ring_recv.at[number, 2 + h], ring_at(axis, -1))
        for number, plan, kind, axis, at, source, slot in streams:
            if kind == "kv":
                send(source(h), slot(at, h), pair_send.at[plan, h], pair_recv.at[plan, h], sibling())
            stores.append(local_copy(source(h), slot(at, h), own_sem.at[number, h]))
    list_ref[...] = make_list(qo_ref[...], ql_ref[...], ko_ref[...], kl_ref[...])
    stores.append(local_copy(list_ref, list_out, store_sem.at[0]))

    for plan in range(2):
        bias = [bias_ref[plan * PLAN_HEADS + h] * LOG2E for h in heads]

        def own_tiles(step, carry):
            group = [step * UNROLL + u for u in range(UNROLL)]
            pairs = [
                (
                    lambda h, i=i: q_ref[plan, i, rows(h), :],
                    lambda h, i=i: kv_ref[plan, i, rows(h), :],
                    lambda h, i=i: kv_ref[plan, i, rows(h, PLAN_FEATURES), :],
                )
                for i in group
            ]
            for i, (highest, mixed) in zip(group, attend(pairs)):
                for h in heads:
                    m_ref[plan, i, h : h + 1, :] = highest[h] + bias[h]
                    l_ref[plan, i, h : h + 1, :] = mixed[h][HEAD_SIZE : HEAD_SIZE + 1]
                    acc_ref[plan, i, rows(h), :] = mixed[h][:HEAD_SIZE]
            return carry

        lax.fori_loop(0, LOCAL // UNROLL, own_tiles, 0)
    stores.append(local_copy(m_ref, m_out, store_sem.at[1]))
    stores.append(local_copy(l_ref, l_out, store_sem.at[2]))
    stores.append(local_copy(acc_ref, acc_out, store_sem.at[3]))
    stores[0].wait()
    for step in (1, 2, 3):
        arrived(table_ref.at[c, z, place(y, -step)], table_recv.at[step - 1])
    for step in (1, 2, 3):
        send(table_ref.at[c, z], table_ref.at[c, z], table_send.at[2 + step], table_recv.at[2 + step], ring_at("z", step))
    for number, plan, kind, axis, at, source, slot in streams:
        before, after = slot(place(at, -1), 0), slot(place(at, 1), 1)
        arrived(before, ring_recv.at[number, 0])
        send(before, before, ring_send.at[number, 4], ring_recv.at[number, 4], ring_at(axis, 1))
        arrived(after, ring_recv.at[number, 3])
        send(after, after, ring_send.at[number, 5], ring_recv.at[number, 5], ring_at(axis, -1))
        if kind == "kv":
            send(before, before, pair_send.at[plan, 2], pair_recv.at[plan, 2], sibling())
            send(after, after, pair_send.at[plan, 5], pair_recv.at[plan, 5], sibling())
    for step in (1, 2, 3):
        arrived(table_ref.at[c, place(z, -step)], table_recv.at[2 + step])
    send(table_ref.at[c], table_ref.at[c], table_send.at[6], table_recv.at[6], sibling())
    for number, plan, kind, axis, at, source, slot in streams:
        before, after = slot(place(at, -1), 1), slot(place(at, 1), 0)
        arrived(before, ring_recv.at[number, 1])
        arrived(after, ring_recv.at[number, 2])
        if kind == "kv":
            send(before, before, pair_send.at[plan, 3], pair_recv.at[plan, 3], sibling())
            send(after, after, pair_send.at[plan, 4], pair_recv.at[plan, 4], sibling())
    for number, plan, kind, axis, at, source, slot in streams:
        for h in range(2):
            far = slot(place(at, 2), h)
            arrived(far, ring_recv.at[number, 4 + h])
            if kind == "kv":
                send(far, far, pair_send.at[plan, 6 + h], pair_recv.at[plan, 6 + h], sibling())
    for number, plan, kind, axis, at, source, slot in streams:
        if kind == "kv":
            for index, step in enumerate((0, -1, 1, 2)):
                for h in range(2):
                    arrived(kvg_ref.at[plan, place(at, step), 1 - c, part(h)], pair_recv.at[plan, 2 * index + h])
    arrived(table_ref.at[1 - c], table_recv.at[6])
    for copy in stores[1:]:
        copy.wait()
    for copy in sent:
        copy.wait_send()


def gather(nodes, qkv_weight, bias, bucket, key_owner, key_local, query_owner, query_local):
    any_space, in_vmem = pl.BlockSpec(memory_space=pl.ANY), pl.BlockSpec(memory_space=pltpu.VMEM)
    dma, vmem = pltpu.SemaphoreType.DMA, pltpu.VMEM
    shape = jax.ShapeDtypeStruct
    q_shape, kv_shape = (PLAN_FEATURES, CSIZE), (2 * PLAN_FEATURES, CSIZE)
    m_shape, acc_shape = (2, LOCAL, 8, CSIZE), (2, LOCAL, PLAN_FEATURES, CSIZE)
    return pl.pallas_call(
        gather_kernel,
        out_shape=[
            shape((2, RING, LOCAL) + q_shape, jnp.bfloat16),
            shape((2, RING, 2, LOCAL) + kv_shape, jnp.bfloat16),
            shape((2, RING, RING, 1, 128), jnp.int32),
            shape((1, LIST_MAX), jnp.int32),
            shape(m_shape, jnp.float32),
            shape(m_shape, jnp.float32),
            shape(acc_shape, jnp.float32),
        ],
        in_specs=[any_space] * 2 + [pl.BlockSpec(memory_space=pltpu.SMEM)] + [in_vmem] * 5,
        out_specs=[any_space] * 7,
        scratch_shapes=[
            vmem(nodes.shape, jnp.bfloat16),
            vmem(qkv_weight.shape, jnp.bfloat16),
            vmem((3, qkv_weight.shape[2], qkv_weight.shape[1]), jnp.bfloat16),
            vmem((2, LOCAL) + q_shape, jnp.bfloat16),
            vmem((2, LOCAL) + kv_shape, jnp.bfloat16),
            vmem((1, 128), jnp.int32),
            vmem((1, LIST_MAX), jnp.int32),
            vmem(m_shape, jnp.float32),
            vmem(m_shape, jnp.float32),
            vmem(acc_shape, jnp.float32),
            dma((4, 6)), dma((4, 6)), dma((2, 8)), dma((2, 8)), dma((7,)), dma((7,)),
            dma((4, 2)), dma((2,)), dma((3,)), dma((5,)),
        ],
        compiler_params=pltpu.CompilerParams(
            collective_id=0, has_side_effects=True, vmem_limit_bytes=56 * 2**20
        ),
        name="gather",
    )(nodes, qkv_weight, bias, bucket, key_owner, key_local, query_owner, query_local)


def tile_kernel(
    bias_ref, list_hbm, table_hbm, m_hbm, l_hbm, acc_hbm, qg_ref, kvg_ref, part_ref, log_ref,
    q_ref, kv_ref, list_ref, table_ref, m_ref, l_ref, acc_ref, q_sem, kv_sem, table_sem, state_sem,
):
    heads = range(PLAN_HEADS)
    z, y, c = coordinates()
    queries = part_ref.shape[0]
    keys = 2 * queries
    waits = ([], [])

    def load(plan, source, target, sem):
        copy = pltpu.make_async_copy(source, target, sem)
        copy.start()
        waits[plan].append(copy)

    load(0, list_hbm, list_ref, table_sem.at[0])
    load(0, table_hbm, table_ref, table_sem.at[1])
    for plan in range(2):
        side = pl.ds(plan * queries // 2, queries // 2)
        load(plan, qg_ref.at[side], q_ref.at[side], q_sem.at[plan])
        side = pl.ds(plan * keys // 2, keys // 2)
        load(plan, kvg_ref.at[side], kv_ref.at[side], kv_sem.at[plan])
    for plan in range(2):
        own = (z if plan == 0 else y) + plan * RING

        def clear(group, carry):
            @pl.when(group != own)
            def _():
                side = pl.ds(group * LOCAL, LOCAL)
                m_ref[side] = jnp.full((LOCAL, 8, CSIZE), NEVER, jnp.float32)
                l_ref[side] = jnp.zeros((LOCAL, 8, CSIZE), jnp.float32)
                acc_ref[side] = jnp.zeros((LOCAL, PLAN_FEATURES, CSIZE), jnp.float32)
            return carry

        side = pl.ds(own * LOCAL, LOCAL)
        load(plan, m_hbm.at[plan], m_ref.at[side], state_sem.at[plan, 0])
        load(plan, l_hbm.at[plan], l_ref.at[side], state_sem.at[plan, 1])
        load(plan, acc_hbm.at[plan], acc_ref.at[side], state_sem.at[plan, 2])
        lax.fori_loop(plan * RING, (plan + 1) * RING, clear, 0)
    m_ref[queries] = jnp.full((8, CSIZE), NEVER, jnp.float32)
    l_ref[queries] = jnp.zeros((8, CSIZE), jnp.float32)
    acc_ref[queries] = jnp.zeros((PLAN_FEATURES, CSIZE), jnp.float32)

    def batch(step, carry):
        items, pairs = [], []
        for u in range(UNROLL):
            item = list_ref[0, step * UNROLL + u]
            state = lax.bitwise_and(item, 127)
            key = lax.bitwise_and(lax.shift_right_logical(item, 7), 127)
            tile = lax.shift_right_logical(item, 14)
            query = jnp.minimum(state, queries - 1)
            worker = lax.shift_right_logical(tile, 5)
            bucket = table_ref[
                lax.bitwise_and(worker, 1), lax.shift_right_logical(worker, 3),
                lax.bitwise_and(lax.shift_right_logical(worker, 1), 3), 0, lax.bitwise_and(tile, 31),
            ]
            first = bucket * (2 * PLAN_HEADS) + jnp.where(key >= keys // 2, PLAN_HEADS, 0)
            items.append((state, [bias_ref[first + h] * LOG2E for h in heads]))
            pairs.append((
                lambda h, i=query: q_ref[i, rows(h), :],
                lambda h, i=key: kv_ref[i, rows(h), :],
                lambda h, i=key: kv_ref[i, rows(h, PLAN_FEATURES), :],
            ))
        for (state, bias), (highest, mixed) in zip(items, attend(pairs)):
            tops = [top + b for top, b in zip(highest, bias)]
            old_m = [m_ref[state, h : h + 1, :] for h in heads]
            old_l = [l_ref[state, h : h + 1, :] for h in heads]
            old_acc = [acc_ref[state, rows(h), :] for h in heads]
            new_m = [jnp.maximum(a, b) for a, b in zip(old_m, tops)]
            keep = [jnp.exp2(a - b) for a, b in zip(old_m, new_m)]
            fresh = [jnp.exp2(a - b) for a, b in zip(tops, new_m)]
            for h in heads:
                m_ref[state, h : h + 1, :] = new_m[h]
                l_ref[state, h : h + 1, :] = old_l[h] * keep[h] + mixed[h][HEAD_SIZE : HEAD_SIZE + 1] * fresh[h]
                acc_ref[state, rows(h), :] = old_acc[h] * keep[h] + mixed[h][:HEAD_SIZE] * fresh[h]
        return carry

    for copy in waits[0]:
        copy.wait()
    split = lax.div(list_ref[0, LIST_MAX - 2], UNROLL)
    lax.fori_loop(0, split, batch, 0)
    for copy in waits[1]:
        copy.wait()
    lax.fori_loop(split, lax.div(list_ref[0, LIST_MAX - 1] + UNROLL - 1, UNROLL), batch, 0)

    def finish(group, carry):
        for local in range(LOCAL):
            state = group * LOCAL + local
            for h in heads:
                total = l_ref[state, h : h + 1, :]
                held = total > 0
                safe = jnp.where(held, total, 1.0)
                part_ref[group * LOCAL + local % 2 * RING + local // 2, rows(h), :] = (acc_ref[state, rows(h), :] * (1.0 / safe)).astype(jnp.bfloat16)
                row = local // 2 * PLAN_HEADS + h
                log_ref[group, local % 2, row : row + 1, :] = m_ref[state, h : h + 1, :] + jnp.log2(safe)
        return carry

    lax.fori_loop(0, queries // LOCAL, finish, 0)


def tiles(bias, items, table, m, l, acc, q_all, kv_all):
    queries, keys = 2 * RING * LOCAL, 2 * RING * 2 * LOCAL
    any_space = pl.BlockSpec(memory_space=pl.ANY)
    whole = lambda shape: pl.BlockSpec(shape, lambda i, *_: (0,) * len(shape))
    part_shape = (queries, PLAN_FEATURES, CSIZE)
    log_shape = (2 * RING, 2, 16, CSIZE)
    dma, vmem = pltpu.SemaphoreType.DMA, pltpu.VMEM
    return pl.pallas_call(
        tile_kernel,
        grid_spec=pltpu.PrefetchScalarGridSpec(
            num_scalar_prefetch=1,
            grid=(1,),
            in_specs=[any_space] * 7,
            out_specs=[whole(part_shape), whole(log_shape)],
            scratch_shapes=[
                vmem((queries, PLAN_FEATURES, CSIZE), jnp.bfloat16),
                vmem((keys, 2 * PLAN_FEATURES, CSIZE), jnp.bfloat16),
                pltpu.SMEM((1, LIST_MAX), jnp.int32),
                pltpu.SMEM((2, RING, RING, 1, 128), jnp.int32),
                vmem((queries + 1, 8, CSIZE), jnp.float32),
                vmem((queries + 1, 8, CSIZE), jnp.float32),
                vmem((queries + 1, PLAN_FEATURES, CSIZE), jnp.float32),
                dma((2,)), dma((2,)), dma((2,)), dma((2, 3)),
            ],
        ),
        out_shape=[
            jax.ShapeDtypeStruct(part_shape, jnp.bfloat16),
            jax.ShapeDtypeStruct(log_shape, jnp.float32),
        ],
        compiler_params=pltpu.CompilerParams(vmem_limit_bytes=56 * 2**20),
        name="tiles",
    )(
        bias, items, table, m, l, acc,
        q_all.reshape(queries, PLAN_FEATURES, CSIZE), kv_all.reshape(keys, 2 * PLAN_FEATURES, CSIZE),
    )


def tail_kernel(
    part_ref, log_ref, nodes_ref, wo_hbm, up_hbm, down_hbm, out_ref,
    wo_ref, up_ref, down_ref, rows_ref, part_in, log_in, own_part, own_log, merged, gathered, resid_ref, normed_ref, staged,
    weight_sem, own_sem, part_send, part_recv, log_send, log_recv, x_send, x_recv, out_send, out_recv, out_own,
):
    z, y, c = coordinates()
    me = lax.axis_index("owner")
    x = lax.axis_index("head")
    heads = range(PLAN_HEADS)
    features = 2 * PLAN_FEATURES

    def load(source, target, sem):
        copy = pltpu.make_async_copy(source, target, sem)
        copy.start()
        return copy

    def across(step):
        return (me, place(x, step))

    ready = []
    for plan in range(2):
        at = z if plan == 0 else y
        ready.append(load(part_ref.at[plan, at], own_part.at[plan], own_sem.at[plan, 0]))
        ready.append(load(log_ref.at[plan, at], own_log.at[plan], own_sem.at[plan, 1]))
    weights = [
        load(nodes_ref.at[pl.ds(x * 2 * CSIZE, 2 * CSIZE)], rows_ref, weight_sem.at[0]),
        load(wo_hbm, wo_ref, weight_sem.at[1]),
        load(up_hbm, up_ref, weight_sem.at[2]),
        load(down_hbm, down_ref, weight_sem.at[3]),
    ]
    greet([ring_at(axis, step) for axis in "zy" for step in (1, 2, 3)] + [across(step) for step in (1, 2, 3)])
    sent = []

    def send(src, dst, send_sem, recv_sem, device):
        copy = pltpu.make_async_remote_copy(
            src_ref=src, dst_ref=dst, send_sem=send_sem, recv_sem=recv_sem,
            device_id=device, device_id_type=MESH,
        )
        copy.start()
        sent.append(copy)

    def arrived(ref, sem):
        pltpu.make_async_remote_copy(
            src_ref=ref, dst_ref=ref, send_sem=x_send.at[0, 0], recv_sem=sem,
            device_id=across(1), device_id_type=MESH,
        ).wait_recv()

    for turn in range(2):
        for plan, axis in enumerate("zy"):
            at = z if plan == 0 else y
            for step in (2, 1, 3):
                to = place(at, step)
                send(
                    part_ref.at[plan, to, turn], part_in.at[plan, step - 1, turn],
                    part_send.at[plan, step - 1, turn], part_recv.at[plan, step - 1, turn], ring_at(axis, step),
                )
                send(
                    log_ref.at[plan, to, turn], log_in.at[plan, step - 1, turn],
                    log_send.at[plan, step - 1, turn], log_recv.at[plan, step - 1, turn], ring_at(axis, step),
                )
    for copy in ready:
        copy.wait()
    mine = pl.ds(pl.multiple_of(x * features, 64), features)

    def merge(turn):
        for plan in range(2):
            for step in (2, 1, 3):
                arrived(part_in.at[plan, step - 1, turn], part_recv.at[plan, step - 1, turn])
                arrived(log_in.at[plan, step - 1, turn], log_recv.at[plan, step - 1, turn])
        for plan in range(2):
            logs = [own_log[plan, turn]] + [log_in[plan, i, turn] for i in range(3)]
            best = jnp.maximum(jnp.maximum(logs[0], logs[1]), jnp.maximum(logs[2], logs[3]))
            shares = [jnp.exp2(log - best) for log in logs]
            scale = 1.0 / (shares[0] + shares[1] + shares[2] + shares[3])
            shares = [share * scale for share in shares]
            for to in range(RING):
                for h in heads:
                    row = to * PLAN_HEADS + h
                    total = own_part[plan, turn, to, rows(h), :].astype(jnp.float32) * shares[0][row : row + 1]
                    for i in range(3):
                        total += part_in[plan, i, turn, to, rows(h), :].astype(jnp.float32) * shares[i + 1][row : row + 1]
                    merged[turn, to, rows(h, plan * PLAN_FEATURES), :] = total.astype(jnp.bfloat16)
        for step in (2, 1, 3):
            send(
                merged.at[turn, place(x, step)], gathered.at[turn, mine],
                x_send.at[turn, step - 1], x_recv.at[turn, step - 1], across(step),
            )
        gathered[turn, mine, :] = merged[turn, x]

    wide = up_ref.shape[1] // RING
    out_copies = []

    def begin(turn):
        part = slice(turn * CSIZE, (turn + 1) * CSIZE)
        for step in (1, 2, 3):
            source = place(x, -step)
            arrived(gathered.at[turn, pl.ds(pl.multiple_of(source * features, 64), features)], x_recv.at[turn, step - 1])
        mixed = lax.dot_general(
            gathered[turn], wo_ref[...], (((0,), (0,)), ((), ())), preferred_element_type=jnp.float32
        )
        resid = rows_ref[part, :].astype(jnp.float32) + mixed
        resid_ref[part, :] = resid
        normed_ref[part, :] = norm_rows(resid).astype(jnp.bfloat16)

    def feed(turn, first, last):
        part = slice(turn * CSIZE, (turn + 1) * CSIZE)

        def block(step, carry):
            units = pl.ds(pl.multiple_of(step * wide, 128), wide)
            hidden = jax.nn.gelu(
                jnp.dot(normed_ref[part, :], up_ref[:, units], preferred_element_type=jnp.float32)
            ).astype(jnp.bfloat16)
            resid_ref[part, :] += jnp.dot(hidden, down_ref[units, :], preferred_element_type=jnp.float32)
            return carry

        lax.fori_loop(first, last, block, 0)

    def hand_out(turn):
        part = slice(turn * CSIZE, (turn + 1) * CSIZE)
        result = resid_ref[part, :].astype(jnp.bfloat16)
        for j in range(RING):
            staged[j, part, :] = result[:, features * j : features * (j + 1)]
        target = out_ref.at[pl.ds((x * 2 + turn) * CSIZE, CSIZE)]
        for step in (2, 1, 3):
            send(
                staged.at[place(x, step), part], target,
                out_send.at[turn, step - 1], out_recv.at[turn, step - 1], across(step),
            )
        out_copies.append(load(staged.at[x, part], target, out_own.at[turn]))

    merge(0)
    for copy in weights:
        copy.wait()
    begin(0)
    feed(0, 0, 2)
    merge(1)
    feed(0, 2, RING)
    hand_out(0)
    begin(1)
    feed(1, 0, RING)
    hand_out(1)
    for turn in range(2):
        for step in (1, 2, 3):
            source = place(x, -step)
            arrived(out_ref.at[pl.ds((source * 2 + turn) * CSIZE, CSIZE)], out_recv.at[turn, step - 1])
    for copy in out_copies:
        copy.wait()
    for copy in sent:
        copy.wait_send()


def tail(parts, logs, nodes, out_weight, up_weight, down_weight):
    any_space = pl.BlockSpec(memory_space=pl.ANY)
    dma, vmem = pltpu.SemaphoreType.DMA, pltpu.VMEM
    width = nodes.shape[1]
    features = 2 * PLAN_FEATURES
    return pl.pallas_call(
        tail_kernel,
        out_shape=jax.ShapeDtypeStruct((nodes.shape[0], features), jnp.bfloat16),
        in_specs=[any_space] * 6,
        out_specs=any_space,
        scratch_shapes=[
            vmem(out_weight.shape, jnp.bfloat16),
            vmem(up_weight.shape, jnp.bfloat16),
            vmem(down_weight.shape, jnp.bfloat16),
            vmem((2 * CSIZE, width), jnp.bfloat16),
            vmem((2, 3, 2, RING, PLAN_FEATURES, CSIZE), jnp.bfloat16),
            vmem((2, 3, 2, 16, CSIZE), jnp.float32),
            vmem((2, 2, RING, PLAN_FEATURES, CSIZE), jnp.bfloat16),
            vmem((2, 2, 16, CSIZE), jnp.float32),
            vmem((2, RING, features, CSIZE), jnp.bfloat16),
            vmem((2, width, CSIZE), jnp.bfloat16),
            vmem((2 * CSIZE, width), jnp.float32),
            vmem((2 * CSIZE, width), jnp.bfloat16),
            vmem((RING, 2 * CSIZE, features), jnp.bfloat16),
            dma((4,)), dma((2, 2)), dma((2, 3, 2)), dma((2, 3, 2)), dma((2, 3, 2)), dma((2, 3, 2)),
            dma((2, 3)), dma((2, 3)), dma((2, 3)), dma((2, 3)), dma((2,)),
        ],
        compiler_params=pltpu.CompilerParams(
            collective_id=1, has_side_effects=True, vmem_limit_bytes=56 * 2**20
        ),
        name="tail",
    )(parts, logs, nodes, out_weight, up_weight, down_weight)


def per_device(
    nodes, qkv_weight, out_weight, hop_bias, up_weight, down_weight,
    key_owner, key_local, query_owner, query_local, hop_bucket,
):
    bias = hop_bias.reshape(-1)
    lists = [array.reshape(8, 128) for array in (key_owner, key_local, query_owner, query_local)]
    q_all, kv_all, table, items, m, l, acc = gather(
        nodes, qkv_weight, bias, hop_bucket.reshape(1, -1), *lists
    )
    parts, logs = tiles(bias, items, table, m, l, acc, q_all, kv_all)
    return tail(
        parts.reshape(2, RING, 2, RING, PLAN_FEATURES, CSIZE), logs.reshape(2, RING, 2, 16, CSIZE),
        nodes, out_weight, up_weight, down_weight,
    )


def solution(mesh):
    placed = (
        P("owner", None), P(None, None, "head"), P(), P(None, "head"), P(), P(),
        P(), P(), P(), P(), P("owner"),
    )
    return jax.shard_map(
        per_device, mesh=mesh, in_specs=placed, out_specs=P("owner", "head"), check_vma=False
    )
```

time: 147 us -> 136 us (0.925); the launches traced: 146 us -> 134 us
  other arithmetic: 6.43 us -> 0 us
  matrix products: 4.08 us -> 0 us
  local copies, waits for them, and re-layouts: 9.53 us -> 5.96 us
  Pallas kernels: 125 us -> 128 us
  between operations: 1.53 us -> 0.03 us
    reduce_sum x6 -> x0, other arithmetic: 5.51 us -> none  [the longest x1 2.57 us: norm_rows(): center = values - jnp.mean(values, axis=-1, keepdims=True)]
    pallas_call x1, Pallas kernels: 49.1 us -> 53.5 us  [gather(): pl.pallas_call(gather_kernel, out_shape=[shape((2, RING, LOCAL) + q_shape...]
    unnamed x1 -> x0, matrix products: 3.99 us -> none
    pallas_call x1, Pallas kernels: 52 us -> 48.6 us  [tail(): pl.pallas_call(tail_kernel, out_shape=jax.ShapeDtypeStruct((nodes.shape[0...]
    pallas_call x1, Pallas kernels: 23.8 us -> 25.6 us  [tiles(): pl.pallas_call(tile_kernel, grid_spec=pltpu.PrefetchScalarGridSpec(num_sc...]
    reshape x2 -> x1, local copies, waits for them, and re-layouts: 2.19 us -> 0.68 us  [per_device(): bias = hop_bias.reshape(-1)]
    unnamed x17 -> x2, local copies, waits for them, and re-layouts: 1.91 us -> 3.09 us
where the time goes in v3:
time: 136 us; the launch traced here: 134 us
  Pallas kernels  128 us (94%)
  local copies, waits for them, and re-layouts  5.96 us (4%)
    pallas_call x1, Pallas kernels, gather(): pl.pallas_call(gather_kernel, out_shape=[shape((2, RING, LOCAL) + q_shape...  53.5 us
    pallas_call x1, Pallas kernels, tail(): pl.pallas_call(tail_kernel, out_shape=jax.ShapeDtypeStruct((nodes.shape[0...  48.6 us
    pallas_call x1, Pallas kernels, tiles(): pl.pallas_call(tile_kernel, grid_spec=pltpu.PrefetchScalarGridSpec(num_sc...  25.6 us
    unnamed x2, local copies, waits for them, and re-layouts  3.09 us

profile of v3, /device:TPU:0, one launch (start us, length us, event | category | flops | bytes accessed | tf_op | source)
XLA Modules:
  0.0 133.7 jit_solution(6727579686668376543)
XLA Ops:
  0.0 0.8 copy.14
  0.8 0.7 reshape.30.bias_ref
  1.5 2.3 %copy.15.weight_hbm = bf16[3,768,192]{2,1,0:T(8,128)(2,1)} copy(bf16[3,768,192]{1,2,0:T(8,128)(2,1)} %param.12) | data formatting | bytes 1769472 | tf_op args[1]
  3.8 53.5 %gather.1 = (bf16[2,4,8,96,256]{4,3,2,1,0:T(8,128)(2,1)}, bf16[2,4,2,8,192,256]{5,4,3,2,1,0:T(8,128)(2,1)}, s32[2,4,4,1,128]{4,3,2,1,0:T(1,128)}, s32[1,640]{1,0...) custom-call(bf16[2048,768]{1,0:T(8,128)(2,1)} %nodes_ref.1, ...), custom_call_target="tpu_custom_call" | custom-call | tf_op jit(solution)/shard_map/gather/pallas_call | solution.py:293
  57.3 25.6 %tiles.1 = (bf16[64,96,256]{2,1,0:T(8,128)(2,1)}, f32[8,2,16,256]{3,2,1,0:T(8,128)}) custom-call(f32[192]{0:T(256)} %reshape.30.bias_ref, s32[1,640]{1,0:T(1,128)} %get-tuple-element.14.list_hbm, s32[2,4,4,1,128]{4,3,2,1,0:T(1,128)} %get-tuple-element.15.table_hbm, f32[2,8,8,256]{3,2,1,0:T(8,128)} %get-tuple-element.16.m_hbm, ...), custom_call_target="tpu_custom_call" | custom-call | tf_op jit(solution)/shard_map/tiles/pallas_call | solution.py:434
  82.9 48.6 %tail.1 = bf16[2048,192]{1,0:T(8,128)(2,1)} custom-call(bf16[2,4,2,4,96,256]{5,4,3,2,1,0:T(8,128)(2,1)} %bitcast.11, f32[2,4,2,16,256]{4,3,2,1,0:T(8,128)} %bitcast.12, bf16[2048,768]{1,0:T(8,128)(2,1)} %nodes_ref.1, bf16[768,768]{1,0:T(8,128)(2,1)} %wo_hbm.1, bf16[768,3072]{1,0:T(8,128)(2,1)} %up_hbm.1, bf16[3072,768]{1,0:T(8,128)(2,1)} %down_hbm.1), custom_call_target="tpu_custom_call" | custom-call | tf_op jit(solution)/shard_map/tail/pallas_call | solution.py:620
  131.5 2.2 %copy.16 = bf16[2048,192]{0,1:T(8,128)(2,1)} copy(bf16[2048,192]{1,0:T(8,128)(2,1)} %tail.1) | data formatting | bytes 1572864 | tf_op jit(solution)/shard_map/tail/pallas_call | solution.py:620

commit v4 on v3

--- a/solution.py
+++ b/solution.py
@@ -21,6 +21,7 @@
 LOG2E = math.log2(math.e)
 NEVER = -1e30
 NOTHING = 64
+PIECES = 4
 
 
 def norm_rows(values):
@@ -53,10 +54,12 @@
 
 
 def greet(partners):
-    barrier = pltpu.get_barrier_semaphore()
     for partner in partners:
-        pl.semaphore_signal(barrier, inc=1, device_id=partner, device_id_type=MESH)
-    pl.semaphore_wait(barrier, len(partners))
+        pl.semaphore_signal(pltpu.get_barrier_semaphore(), inc=1, device_id=partner, device_id_type=MESH)
+
+
+def greeted(partners):
+    pl.semaphore_wait(pltpu.get_barrier_semaphore(), len(partners))
 
 
 def rows(h, first=0):
@@ -125,31 +128,39 @@
 
 
 def gather_kernel(
-    nodes_hbm, weight_hbm, bias_ref, bucket_ref, ko_ref, kl_ref, qo_ref, ql_ref,
-    qg_ref, kvg_ref, table_ref, list_out, m_out, l_out, acc_out,
-    nodes_ref, weight_ref, turned_ref, q_ref, kv_ref, bucket_row, list_ref, m_ref, l_ref, acc_ref,
+    nodes_hbm, weight_hbm, bias_in, bucket_ref, ko_ref, kl_ref, qo_ref, ql_ref,
+    qg_ref, kvg_ref, table_ref, list_out, bias_out, m_out, l_out, acc_out,
+    nodes_ref, weight_ref, q_ref, kv_ref, bucket_row, list_ref, bias_ref, m_ref, l_ref, acc_ref,
     ring_send, ring_recv, pair_send, pair_recv, table_send, table_recv, own_sem, load_sem, weight_sem, store_sem,
 ):
     z, y, c = coordinates()
-    half = LOCAL // 2
     heads = range(PLAN_HEADS)
+    size = LOCAL // PIECES
+    partners = [ring_at(axis, step) for axis in "zy" for step in (1, 2, 3)] + [sibling()]
+    greet(partners)
 
     def local_copy(source, target, sem):
         copy = pltpu.make_async_copy(source, target, sem)
         copy.start()
         return copy
 
-    weight_loads = [local_copy(weight_hbm.at[i], weight_ref.at[i], weight_sem.at[i]) for i in range(3)]
-    node_rows = lambda h: pl.ds(h * half * CSIZE, half * CSIZE)
-    node_loads = [local_copy(nodes_hbm.at[node_rows(h)], nodes_ref.at[node_rows(h)], load_sem.at[h]) for h in range(2)]
+    node_rows = lambda p: pl.ds(p * size * CSIZE, size * CSIZE)
+    load_nodes = lambda p: local_copy(nodes_hbm.at[node_rows(p)], nodes_ref.at[node_rows(p)], load_sem.at[p])
+    node_loads = [load_nodes(0)]
+    weight_load = local_copy(weight_hbm, weight_ref, weight_sem)
+    node_loads += [load_nodes(p) for p in range(1, PIECES)]
     bucket_row[...] = jnp.zeros(bucket_row.shape, jnp.int32)
     bucket_row[:, : bucket_ref.shape[1]] = bucket_ref[...]
+    for i in range(2 * PLAN_HEADS):
+        bias_ref[i, :, : bias_in.shape[1]] = bias_in[i : i + 1] * LOG2E
     stores = [local_copy(bucket_row, table_ref.at[c, z, y], store_sem.at[4])]
-    greet([ring_at(axis, step) for axis in "zy" for step in (1, 2, 3)] + [sibling()])
     sent = []
 
-    def part(h):
-        return pl.ds(h * half, half)
+    def part(p):
+        return pl.ds(p * size, size)
+
+    def side(h):
+        return pl.ds(h * (LOCAL // 2), LOCAL // 2)
 
     streams = []
     for plan in range(2):
@@ -157,11 +168,11 @@
         for kind, axis in (("kv", kv_axis), ("q", q_axis)):
             at = z if axis == "z" else y
             if kind == "q":
-                source = lambda h, plan=plan: q_ref.at[plan, part(h)]
-                slot = lambda p, h, plan=plan: qg_ref.at[plan, p, part(h)]
+                source = lambda r, plan=plan: q_ref.at[plan, r]
+                slot = lambda p, r, plan=plan: qg_ref.at[plan, p, r]
             else:
-                source = lambda h, plan=plan: kv_ref.at[plan, part(h)]
-                slot = lambda p, h, plan=plan: kvg_ref.at[plan, p, c, part(h)]
+                source = lambda r, plan=plan: kv_ref.at[plan, r]
+                slot = lambda p, r, plan=plan: kvg_ref.at[plan, p, c, r]
             streams.append((len(streams), plan, kind, axis, at, source, slot))
 
     def send(src, dst, send_sem, recv_sem, device):
@@ -178,19 +189,14 @@
             device_id=sibling(), device_id_type=MESH,
         ).wait_recv()
 
-    for step in (1, 2, 3):
-        send(bucket_row, table_ref.at[c, z, y], table_send.at[step - 1], table_recv.at[step - 1], ring_at("y", step))
-    for copy in weight_loads:
-        copy.wait()
-    for i in range(3):
-        turned_ref[i] = weight_ref[i].T
+    weight_load.wait()
     features = 2 * PLAN_FEATURES
 
     def project(cluster, carry):
         normed = norm_rows(nodes_ref[pl.ds(cluster * CSIZE, CSIZE), :].astype(jnp.float32)).astype(jnp.bfloat16)
         for i in range(3):
             projected = lax.dot_general(
-                turned_ref[i], normed, (((1,), (1,)), ((), ())), preferred_element_type=jnp.float32
+                weight_ref[i], normed, (((1,), (1,)), ((), ())), preferred_element_type=jnp.float32
             )
             if i == 0:
                 projected = projected * (LOG2E / math.sqrt(HEAD_SIZE))
@@ -203,23 +209,32 @@
                     kv_ref[plan, cluster, (i - 1) * PLAN_FEATURES : i * PLAN_FEATURES, :] = block
         return carry
 
-    for h in range(2):
-        node_loads[h].wait()
-        lax.fori_loop(h * half, (h + 1) * half, project, 0)
-        for wanted in ("kv", "q"):
-            for number, plan, kind, axis, at, source, slot in streams:
-                if kind == wanted:
-                    send(source(h), slot(at, h), ring_send.at[number, h], ring_recv.at[number, h], ring_at(axis, 1))
-                    send(source(h), slot(at, h), ring_send.at[number, 2 + h], ring_recv.at[number, 2 + h], ring_at(axis, -1))
-        for number, plan, kind, axis, at, source, slot in streams:
-            if kind == "kv":
-                send(source(h), slot(at, h), pair_send.at[plan, h], pair_recv.at[plan, h], sibling())
-            stores.append(local_copy(source(h), slot(at, h), own_sem.at[number, h]))
+    ordered = [s for s in streams if s[2] == "kv"] + [s for s in streams if s[2] == "q"]
+    for p in range(PIECES):
+        node_loads[p].wait()
+        lax.fori_loop(p * size, (p + 1) * size, project, 0)
+        if p == 0:
+            greeted(partners)
+            for step in (1, 2, 3):
+                send(bucket_row, table_ref.at[c, z, y], table_send.at[step - 1], table_recv.at[step - 1], ring_at("y", step))
+        for number, plan, kind, axis, at, source, slot in ordered:
+            for way, first in ((1, 0), (-1, PIECES)):
+                send(
+                    source(part(p)), slot(at, part(p)),
+                    ring_send.at[number, first + p], ring_recv.at[number, first + p], ring_at(axis, way),
+                )
+        if p % (PIECES // 2) == PIECES // 2 - 1:
+            h = p // (PIECES // 2)
+            for number, plan, kind, axis, at, source, slot in ordered:
+                if kind == "kv":
+                    send(source(side(h)), slot(at, side(h)), pair_send.at[plan, h], pair_recv.at[plan, h], sibling())
+                stores.append(local_copy(source(side(h)), slot(at, side(h)), own_sem.at[number, h]))
     list_ref[...] = make_list(qo_ref[...], ql_ref[...], ko_ref[...], kl_ref[...])
     stores.append(local_copy(list_ref, list_out, store_sem.at[0]))
+    stores.append(local_copy(bias_ref, bias_out, store_sem.at[5]))
 
     for plan in range(2):
-        bias = [bias_ref[plan * PLAN_HEADS + h] * LOG2E for h in heads]
+        bias = [bias_ref[plan * PLAN_HEADS + h, :, 0:1] for h in heads]
 
         def own_tiles(step, carry):
             group = [step * UNROLL + u for u in range(UNROLL)]
@@ -247,36 +262,36 @@
         arrived(table_ref.at[c, z, place(y, -step)], table_recv.at[step - 1])
     for step in (1, 2, 3):
         send(table_ref.at[c, z], table_ref.at[c, z], table_send.at[2 + step], table_recv.at[2 + step], ring_at("z", step))
-    for number, plan, kind, axis, at, source, slot in streams:
-        before, after = slot(place(at, -1), 0), slot(place(at, 1), 1)
-        arrived(before, ring_recv.at[number, 0])
-        send(before, before, ring_send.at[number, 4], ring_recv.at[number, 4], ring_at(axis, 1))
-        arrived(after, ring_recv.at[number, 3])
-        send(after, after, ring_send.at[number, 5], ring_recv.at[number, 5], ring_at(axis, -1))
-        if kind == "kv":
-            send(before, before, pair_send.at[plan, 2], pair_recv.at[plan, 2], sibling())
-            send(after, after, pair_send.at[plan, 5], pair_recv.at[plan, 5], sibling())
-    for step in (1, 2, 3):
-        arrived(table_ref.at[c, place(z, -step)], table_recv.at[2 + step])
-    send(table_ref.at[c], table_ref.at[c], table_send.at[6], table_recv.at[6], sibling())
-    for number, plan, kind, axis, at, source, slot in streams:
-        before, after = slot(place(at, -1), 1), slot(place(at, 1), 0)
-        arrived(before, ring_recv.at[number, 1])
-        arrived(after, ring_recv.at[number, 2])
-        if kind == "kv":
-            send(before, before, pair_send.at[plan, 3], pair_recv.at[plan, 3], sibling())
-            send(after, after, pair_send.at[plan, 4], pair_recv.at[plan, 4], sibling())
-    for number, plan, kind, axis, at, source, slot in streams:
-        for h in range(2):
-            far = slot(place(at, 2), h)
-            arrived(far, ring_recv.at[number, 4 + h])
+    for h in range(2):
+        for p in range(h * PIECES // 2, (h + 1) * PIECES // 2):
+            for number, plan, kind, axis, at, source, slot in ordered:
+                before, after = slot(place(at, -1), part(p)), slot(place(at, 1), part(p))
+                arrived(before, ring_recv.at[number, p])
+                arrived(after, ring_recv.at[number, PIECES + p])
+                onward, way = (before, 1) if h == 0 else (after, -1)
+                far = 2 * PIECES + p
+                send(onward, onward, ring_send.at[number, far], ring_recv.at[number, far], ring_at(axis, way))
+        for number, plan, kind, axis, at, source, slot in ordered:
             if kind == "kv":
+                for index, step in ((1, -1), (2, 1)):
+                    block, sem = slot(place(at, step), side(h)), 2 * index + h
+                    send(block, block, pair_send.at[plan, sem], pair_recv.at[plan, sem], sibling())
+        if h == 0:
+            for step in (1, 2, 3):
+                arrived(table_ref.at[c, place(z, -step)], table_recv.at[2 + step])
+            send(table_ref.at[c], table_ref.at[c], table_send.at[6], table_recv.at[6], sibling())
+    for h in range(2):
+        for number, plan, kind, axis, at, source, slot in ordered:
+            for p in range(h * PIECES // 2, (h + 1) * PIECES // 2):
+                arrived(slot(place(at, 2), part(p)), ring_recv.at[number, 2 * PIECES + p])
+            if kind == "kv":
+                far = slot(place(at, 2), side(h))
                 send(far, far, pair_send.at[plan, 6 + h], pair_recv.at[plan, 6 + h], sibling())
     for number, plan, kind, axis, at, source, slot in streams:
         if kind == "kv":
             for index, step in enumerate((0, -1, 1, 2)):
                 for h in range(2):
-                    arrived(kvg_ref.at[plan, place(at, step), 1 - c, part(h)], pair_recv.at[plan, 2 * index + h])
+                    arrived(kvg_ref.at[plan, place(at, step), 1 - c, side(h)], pair_recv.at[plan, 2 * index + h])
     arrived(table_ref.at[1 - c], table_recv.at[6])
     for copy in stores[1:]:
         copy.wait()
@@ -297,25 +312,26 @@
             shape((2, RING, 2, LOCAL) + kv_shape, jnp.bfloat16),
             shape((2, RING, RING, 1, 128), jnp.int32),
             shape((1, LIST_MAX), jnp.int32),
+            shape((2 * PLAN_HEADS, 1, 128), jnp.float32),
             shape(m_shape, jnp.float32),
             shape(m_shape, jnp.float32),
             shape(acc_shape, jnp.float32),
         ],
-        in_specs=[any_space] * 2 + [pl.BlockSpec(memory_space=pltpu.SMEM)] + [in_vmem] * 5,
-        out_specs=[any_space] * 7,
+        in_specs=[any_space] * 2 + [in_vmem] * 6,
+        out_specs=[any_space] * 8,
         scratch_shapes=[
             vmem(nodes.shape, jnp.bfloat16),
             vmem(qkv_weight.shape, jnp.bfloat16),
-            vmem((3, qkv_weight.shape[2], qkv_weight.shape[1]), jnp.bfloat16),
             vmem((2, LOCAL) + q_shape, jnp.bfloat16),
             vmem((2, LOCAL) + kv_shape, jnp.bfloat16),
             vmem((1, 128), jnp.int32),
             vmem((1, LIST_MAX), jnp.int32),
+            vmem((2 * PLAN_HEADS, 1, 128), jnp.float32),
             vmem(m_shape, jnp.float32),
             vmem(m_shape, jnp.float32),
             vmem(acc_shape, jnp.float32),
-            dma((4, 6)), dma((4, 6)), dma((2, 8)), dma((2, 8)), dma((7,)), dma((7,)),
-            dma((4, 2)), dma((2,)), dma((3,)), dma((5,)),
+            dma((4, 3 * PIECES)), dma((4, 3 * PIECES)), dma((2, 8)), dma((2, 8)), dma((7,)), dma((7,)),
+            dma((4, 2)), dma((PIECES,)), dma(()), dma((6,)),
         ],
         compiler_params=pltpu.CompilerParams(
             collective_id=0, has_side_effects=True, vmem_limit_bytes=56 * 2**20
@@ -325,8 +341,8 @@
 
 
 def tile_kernel(
-    bias_ref, list_hbm, table_hbm, m_hbm, l_hbm, acc_hbm, qg_ref, kvg_ref, part_ref, log_ref,
-    q_ref, kv_ref, list_ref, table_ref, m_ref, l_ref, acc_ref, q_sem, kv_sem, table_sem, state_sem,
+    list_hbm, bias_hbm, table_hbm, m_hbm, l_hbm, acc_hbm, qg_ref, kvg_ref, part_ref, log_ref,
+    q_ref, kv_ref, list_ref, bias_ref, table_ref, m_ref, l_ref, acc_ref, q_sem, kv_sem, table_sem, state_sem,
 ):
     heads = range(PLAN_HEADS)
     z, y, c = coordinates()
@@ -341,6 +357,7 @@
 
     load(0, list_hbm, list_ref, table_sem.at[0])
     load(0, table_hbm, table_ref, table_sem.at[1])
+    load(0, bias_hbm, bias_ref, table_sem.at[2])
     for plan in range(2):
         side = pl.ds(plan * queries // 2, queries // 2)
         load(plan, qg_ref.at[side], q_ref.at[side], q_sem.at[plan])
@@ -380,8 +397,8 @@
                 lax.bitwise_and(worker, 1), lax.shift_right_logical(worker, 3),
                 lax.bitwise_and(lax.shift_right_logical(worker, 1), 3), 0, lax.bitwise_and(tile, 31),
             ]
-            first = bucket * (2 * PLAN_HEADS) + jnp.where(key >= keys // 2, PLAN_HEADS, 0)
-            items.append((state, [bias_ref[first + h] * LOG2E for h in heads]))
+            first = jnp.where(key >= keys // 2, PLAN_HEADS, 0)
+            items.append((state, [bias_ref[first + h, 0, bucket] for h in heads]))
             pairs.append((
                 lambda h, i=query: q_ref[i, rows(h), :],
                 lambda h, i=key: kv_ref[i, rows(h), :],
@@ -417,36 +434,37 @@
                 held = total > 0
                 safe = jnp.where(held, total, 1.0)
                 part_ref[group * LOCAL + local % 2 * RING + local // 2, rows(h), :] = (acc_ref[state, rows(h), :] * (1.0 / safe)).astype(jnp.bfloat16)
-                row = local // 2 * PLAN_HEADS + h
-                log_ref[group, local % 2, row : row + 1, :] = m_ref[state, h : h + 1, :] + jnp.log2(safe)
+                row = local // 2 % 2 * PLAN_HEADS + h
+                log_ref[group, local % 2, local // 4, row : row + 1, :] = m_ref[state, h : h + 1, :] + jnp.log2(safe)
         return carry
 
     lax.fori_loop(0, queries // LOCAL, finish, 0)
 
 
-def tiles(bias, items, table, m, l, acc, q_all, kv_all):
+def tiles(items, bias, table, m, l, acc, q_all, kv_all):
     queries, keys = 2 * RING * LOCAL, 2 * RING * 2 * LOCAL
     any_space = pl.BlockSpec(memory_space=pl.ANY)
     whole = lambda shape: pl.BlockSpec(shape, lambda i, *_: (0,) * len(shape))
     part_shape = (queries, PLAN_FEATURES, CSIZE)
-    log_shape = (2 * RING, 2, 16, CSIZE)
+    log_shape = (2 * RING, 2, 2, 8, CSIZE)
     dma, vmem = pltpu.SemaphoreType.DMA, pltpu.VMEM
     return pl.pallas_call(
         tile_kernel,
         grid_spec=pltpu.PrefetchScalarGridSpec(
-            num_scalar_prefetch=1,
+            num_scalar_prefetch=0,
             grid=(1,),
-            in_specs=[any_space] * 7,
+            in_specs=[any_space] * 8,
             out_specs=[whole(part_shape), whole(log_shape)],
             scratch_shapes=[
                 vmem((queries, PLAN_FEATURES, CSIZE), jnp.bfloat16),
                 vmem((keys, 2 * PLAN_FEATURES, CSIZE), jnp.bfloat16),
                 pltpu.SMEM((1, LIST_MAX), jnp.int32),
+                pltpu.SMEM((2 * PLAN_HEADS, 1, 128), jnp.float32),
                 pltpu.SMEM((2, RING, RING, 1, 128), jnp.int32),
                 vmem((queries + 1, 8, CSIZE), jnp.float32),
                 vmem((queries + 1, 8, CSIZE), jnp.float32),
                 vmem((queries + 1, PLAN_FEATURES, CSIZE), jnp.float32),
-                dma((2,)), dma((2,)), dma((2,)), dma((2, 3)),
+                dma((2,)), dma((2,)), dma((3,)), dma((2, 3)),
             ],
         ),
         out_shape=[
@@ -456,15 +474,16 @@
         compiler_params=pltpu.CompilerParams(vmem_limit_bytes=56 * 2**20),
         name="tiles",
     )(
-        bias, items, table, m, l, acc,
+        items, bias, table, m, l, acc,
         q_all.reshape(queries, PLAN_FEATURES, CSIZE), kv_all.reshape(keys, 2 * PLAN_FEATURES, CSIZE),
     )
 
 
 def tail_kernel(
     part_ref, log_ref, nodes_ref, wo_hbm, up_hbm, down_hbm, out_ref,
-    wo_ref, up_ref, down_ref, rows_ref, part_in, log_in, own_part, own_log, merged, gathered, resid_ref, normed_ref, staged,
-    weight_sem, own_sem, part_send, part_recv, log_send, log_recv, x_send, x_recv, out_send, out_recv, out_own,
+    wo_ref, up_ref, down_ref, rows_ref, part_in, log_in, far_part, far_log, own_part, own_log, near_part, near_log,
+    both_part, both_log, merged, gathered, resid_ref, normed_ref, staged,
+    weight_sem, own_sem, near_sem, back_send, back_recv, x_send, x_recv, out_send, out_recv, out_own,
 ):
     z, y, c = coordinates()
     me = lax.axis_index("owner")
@@ -480,9 +499,24 @@
     def across(step):
         return (me, place(x, step))
 
-    ready = []
-    for plan in range(2):
-        at = z if plan == 0 else y
+    partners = [ring_at(axis, step) for axis in "zy" for step in (1, 3)] + [across(step) for step in (1, 2, 3)]
+    greet(partners)
+    ways = ((0, 1), (1, -1))
+    ring = [(0, "z", z), (1, "y", y)]
+    half = lambda h: pl.ds(h * (RING // 2), RING // 2)
+    near, ready = [], []
+    for plan, axis, at in ring:
+        for way, step in ways:
+            for turn in range(2):
+                near.append(load(
+                    part_ref.at[plan, place(at, step), turn, half(way)], near_part.at[plan, way, turn],
+                    near_sem.at[plan, way, turn, 0],
+                ))
+                near.append(load(
+                    log_ref.at[plan, place(at, step), turn, way], near_log.at[plan, way, turn],
+                    near_sem.at[plan, way, turn, 1],
+                ))
+    for plan, axis, at in ring:
         ready.append(load(part_ref.at[plan, at], own_part.at[plan], own_sem.at[plan, 0]))
         ready.append(load(log_ref.at[plan, at], own_log.at[plan], own_sem.at[plan, 1]))
     weights = [
@@ -491,7 +525,7 @@
         load(up_hbm, up_ref, weight_sem.at[2]),
         load(down_hbm, down_ref, weight_sem.at[3]),
     ]
-    greet([ring_at(axis, step) for axis in "zy" for step in (1, 2, 3)] + [across(step) for step in (1, 2, 3)])
+    greeted(partners)
     sent = []
 
     def send(src, dst, send_sem, recv_sem, device):
@@ -508,40 +542,72 @@
             device_id=across(1), device_id_type=MESH,
         ).wait_recv()
 
-    for turn in range(2):
-        for plan, axis in enumerate("zy"):
-            at = z if plan == 0 else y
-            for step in (2, 1, 3):
-                to = place(at, step)
-                send(
-                    part_ref.at[plan, to, turn], part_in.at[plan, step - 1, turn],
-                    part_send.at[plan, step - 1, turn], part_recv.at[plan, step - 1, turn], ring_at(axis, step),
+    def back(plan, way, turn, kind, src, dst, device):
+        send(src, dst, back_send.at[plan, way, turn, kind], back_recv.at[plan, way, turn, kind], device)
+
+    def send_out(turn):
+        for plan, axis, at in ring:
+            for way, step in ways:
+                to, far = ring_at(axis, step), place(at, 2)
+                back(plan, way, turn, 0, part_ref.at[plan, far, turn, half(way)], far_part.at[plan, way, turn], to)
+                back(plan, way, turn, 1, log_ref.at[plan, far, turn, way], far_log.at[plan, way, turn], to)
+        for plan, axis, at in ring:
+            for way, step in ways:
+                to, next_at = ring_at(axis, step), place(at, step)
+                back(
+                    plan, way, turn, 2, part_ref.at[plan, next_at, turn, half(1 - way)],
+                    part_in.at[plan, way, turn, half(1 - way)], to,
                 )
-                send(
-                    log_ref.at[plan, to, turn], log_in.at[plan, step - 1, turn],
-                    log_send.at[plan, step - 1, turn], log_recv.at[plan, step - 1, turn], ring_at(axis, step),
+                back(
+                    plan, way, turn, 3, log_ref.at[plan, next_at, turn, 1 - way],
+                    log_in.at[plan, way, turn, 1 - way], to,
                 )
-    for copy in ready:
-        copy.wait()
+
+    def combine(turn):
+        for plan, axis, at in ring:
+            for way, step in ways:
+                arrived(far_part.at[plan, way, turn], back_recv.at[plan, way, turn, 0])
+                arrived(far_log.at[plan, way, turn], back_recv.at[plan, way, turn, 1])
+                one, two = near_log[plan, way, turn], far_log[plan, way, turn]
+                best = jnp.maximum(one, two)
+                shares = [jnp.exp2(one - best), jnp.exp2(two - best)]
+                total = shares[0] + shares[1]
+                both_log[plan, way, turn] = best + jnp.log2(total)
+                scale = 1.0 / total
+                shares = [share * scale for share in shares]
+                for to in range(2):
+                    for h in heads:
+                        row = to * PLAN_HEADS + h
+                        both_part[plan, way, turn, to, rows(h), :] = (
+                            near_part[plan, way, turn, to, rows(h), :].astype(jnp.float32) * shares[0][row : row + 1]
+                            + far_part[plan, way, turn, to, rows(h), :].astype(jnp.float32) * shares[1][row : row + 1]
+                        ).astype(jnp.bfloat16)
+                to = ring_at(axis, step)
+                back(plan, way, turn, 4, both_part.at[plan, way, turn], part_in.at[plan, way, turn, half(way)], to)
+                back(plan, way, turn, 5, both_log.at[plan, way, turn], log_in.at[plan, way, turn, way], to)
+
     mine = pl.ds(pl.multiple_of(x * features, 64), features)
 
     def merge(turn):
         for plan in range(2):
-            for step in (2, 1, 3):
-                arrived(part_in.at[plan, step - 1, turn], part_recv.at[plan, step - 1, turn])
-                arrived(log_in.at[plan, step - 1, turn], log_recv.at[plan, step - 1, turn])
+            for way in range(2):
+                arrived(part_in.at[plan, way, turn, half(1 - way)], back_recv.at[plan, way, turn, 2])
+                arrived(log_in.at[plan, way, turn, 1 - way], back_recv.at[plan, way, turn, 3])
+                arrived(part_in.at[plan, way, turn, half(way)], back_recv.at[plan, way, turn, 4])
+                arrived(log_in.at[plan, way, turn, way], back_recv.at[plan, way, turn, 5])
         for plan in range(2):
-            logs = [own_log[plan, turn]] + [log_in[plan, i, turn] for i in range(3)]
-            best = jnp.maximum(jnp.maximum(logs[0], logs[1]), jnp.maximum(logs[2], logs[3]))
-            shares = [jnp.exp2(log - best) for log in logs]
-            scale = 1.0 / (shares[0] + shares[1] + shares[2] + shares[3])
-            shares = [share * scale for share in shares]
             for to in range(RING):
+                h0 = to // 2
+                logs = [own_log[plan, turn, h0]] + [log_in[plan, way, turn, h0] for way in range(2)]
+                best = jnp.maximum(jnp.maximum(logs[0], logs[1]), logs[2])
+                shares = [jnp.exp2(log - best) for log in logs]
+                scale = 1.0 / (shares[0] + shares[1] + shares[2])
+                shares = [share * scale for share in shares]
                 for h in heads:
-                    row = to * PLAN_HEADS + h
+                    row = to % 2 * PLAN_HEADS + h
                     total = own_part[plan, turn, to, rows(h), :].astype(jnp.float32) * shares[0][row : row + 1]
-                    for i in range(3):
-                        total += part_in[plan, i, turn, to, rows(h), :].astype(jnp.float32) * shares[i + 1][row : row + 1]
+                    for way in range(2):
+                        total += part_in[plan, way, turn, to, rows(h), :].astype(jnp.float32) * shares[way + 1][row : row + 1]
                     merged[turn, to, rows(h, plan * PLAN_FEATURES), :] = total.astype(jnp.bfloat16)
         for step in (2, 1, 3):
             send(
@@ -580,18 +646,24 @@
 
     def hand_out(turn):
         part = slice(turn * CSIZE, (turn + 1) * CSIZE)
-        result = resid_ref[part, :].astype(jnp.bfloat16)
-        for j in range(RING):
-            staged[j, part, :] = result[:, features * j : features * (j + 1)]
-        target = out_ref.at[pl.ds((x * 2 + turn) * CSIZE, CSIZE)]
+        staged[:, part] = resid_ref[part, :].astype(jnp.bfloat16).T
+        target = out_ref.at[:, pl.ds(pl.multiple_of((x * 2 + turn) * CSIZE, CSIZE), CSIZE)]
+        block = lambda j: staged.at[pl.ds(pl.multiple_of(j * features, 64), features), part]
         for step in (2, 1, 3):
             send(
-                staged.at[place(x, step), part], target,
-                out_send.at[turn, step - 1], out_recv.at[turn, step - 1], across(step),
+                block(place(x, step)), target, out_send.at[turn, step - 1], out_recv.at[turn, step - 1], across(step)
             )
-        out_copies.append(load(staged.at[x, part], target, out_own.at[turn]))
-
+        out_copies.append(load(block(x), target, out_own.at[turn]))
+
+    send_out(0)
+    for copy in near:
+        copy.wait()
+    combine(0)
+    send_out(1)
+    for copy in ready:
+        copy.wait()
     merge(0)
+    combine(1)
     for copy in weights:
         copy.wait()
     begin(0)
@@ -605,7 +677,7 @@
     for turn in range(2):
         for step in (1, 2, 3):
             source = place(x, -step)
-            arrived(out_ref.at[pl.ds((source * 2 + turn) * CSIZE, CSIZE)], out_recv.at[turn, step - 1])
+            arrived(out_ref.at[:, pl.ds(pl.multiple_of((source * 2 + turn) * CSIZE, CSIZE), CSIZE)], out_recv.at[turn, step - 1])
     for copy in out_copies:
         copy.wait()
     for copy in sent:
@@ -619,7 +691,7 @@
     features = 2 * PLAN_FEATURES
     return pl.pallas_call(
         tail_kernel,
-        out_shape=jax.ShapeDtypeStruct((nodes.shape[0], features), jnp.bfloat16),
+        out_shape=jax.ShapeDtypeStruct((features, nodes.shape[0]), jnp.bfloat16),
         in_specs=[any_space] * 6,
         out_specs=any_space,
         scratch_shapes=[
@@ -627,16 +699,22 @@
             vmem(up_weight.shape, jnp.bfloat16),
             vmem(down_weight.shape, jnp.bfloat16),
             vmem((2 * CSIZE, width), jnp.bfloat16),
-            vmem((2, 3, 2, RING, PLAN_FEATURES, CSIZE), jnp.bfloat16),
-            vmem((2, 3, 2, 16, CSIZE), jnp.float32),
+            vmem((2, 2, 2, RING, PLAN_FEATURES, CSIZE), jnp.bfloat16),
+            vmem((2, 2, 2, 2, 8, CSIZE), jnp.float32),
+            vmem((2, 2, 2, 2, PLAN_FEATURES, CSIZE), jnp.bfloat16),
+            vmem((2, 2, 2, 8, CSIZE), jnp.float32),
             vmem((2, 2, RING, PLAN_FEATURES, CSIZE), jnp.bfloat16),
-            vmem((2, 2, 16, CSIZE), jnp.float32),
+            vmem((2, 2, 2, 8, CSIZE), jnp.float32),
+            vmem((2, 2, 2, 2, PLAN_FEATURES, CSIZE), jnp.bfloat16),
+            vmem((2, 2, 2, 8, CSIZE), jnp.float32),
+            vmem((2, 2, 2, 2, PLAN_FEATURES, CSIZE), jnp.bfloat16),
+            vmem((2, 2, 2, 8, CSIZE), jnp.float32),
             vmem((2, RING, features, CSIZE), jnp.bfloat16),
             vmem((2, width, CSIZE), jnp.bfloat16),
             vmem((2 * CSIZE, width), jnp.float32),
             vmem((2 * CSIZE, width), jnp.bfloat16),
-            vmem((RING, 2 * CSIZE, features), jnp.bfloat16),
-            dma((4,)), dma((2, 2)), dma((2, 3, 2)), dma((2, 3, 2)), dma((2, 3, 2)), dma((2, 3, 2)),
+            vmem((RING * features, 2 * CSIZE), jnp.bfloat16),
+            dma((4,)), dma((2, 2)), dma((2, 2, 2, 2)), dma((2, 2, 2, 6)), dma((2, 2, 2, 6)),
             dma((2, 3)), dma((2, 3)), dma((2, 3)), dma((2, 3)), dma((2,)),
         ],
         compiler_params=pltpu.CompilerParams(
@@ -650,16 +728,15 @@
     nodes, qkv_weight, out_weight, hop_bias, up_weight, down_weight,
     key_owner, key_local, query_owner, query_local, hop_bucket,
 ):
-    bias = hop_bias.reshape(-1)
     lists = [array.reshape(8, 128) for array in (key_owner, key_local, query_owner, query_local)]
-    q_all, kv_all, table, items, m, l, acc = gather(
-        nodes, qkv_weight, bias, hop_bucket.reshape(1, -1), *lists
+    q_all, kv_all, table, items, bias, m, l, acc = gather(
+        nodes, qkv_weight.swapaxes(1, 2), hop_bias.T, hop_bucket.reshape(1, -1), *lists
     )
-    parts, logs = tiles(bias, items, table, m, l, acc, q_all, kv_all)
+    parts, logs = tiles(items, bias, table, m, l, acc, q_all, kv_all)
     return tail(
-        parts.reshape(2, RING, 2, RING, PLAN_FEATURES, CSIZE), logs.reshape(2, RING, 2, 16, CSIZE),
+        parts.reshape(2, RING, 2, RING, PLAN_FEATURES, CSIZE), logs.reshape(2, RING, 2, 2, 8, CSIZE),
         nodes, out_weight, up_weight, down_weight,
-    )
+    ).T
 
 
 def solution(mesh):

time: 136 us -> 130 us (0.956); the launches traced: 134 us -> 130 us
  local copies, waits for them, and re-layouts: 5.96 us -> 2.09 us
    pallas_call x1, Pallas kernels: 25.6 us -> 29.2 us  [tiles(): pl.pallas_call(tile_kernel, grid_spec=pltpu.PrefetchScalarGridSpec(num_sc...]
    pallas_call x1 -> x0, local copies, waits for them, and re-layouts: 2.19 us -> none  [tail(): pl.pallas_call(tail_kernel, out_shape=jax.ShapeDtypeStruct((nodes.shape[0...]
    pallas_call x1, Pallas kernels: 48.6 us -> 46.7 us  [tail(): pl.pallas_call(tail_kernel, out_shape=jax.ShapeDtypeStruct((features, nod...]
    pallas_call x1, Pallas kernels: 53.5 us -> 51.8 us  [gather(): pl.pallas_call(gather_kernel, out_shape=[shape((2, RING, LOCAL) + q_shape...]
    unnamed x2 -> x1, local copies, waits for them, and re-layouts: 3.09 us -> 2.09 us
where the time goes in v4:
time: 130 us
  Pallas kernels  128 us (98%)
  local copies, waits for them, and re-layouts  2.09 us (2%)
    pallas_call x1, Pallas kernels, gather(): pl.pallas_call(gather_kernel, out_shape=[shape((2, RING, LOCAL) + q_shape...  51.8 us
    pallas_call x1, Pallas kernels, tail(): pl.pallas_call(tail_kernel, out_shape=jax.ShapeDtypeStruct((features, nod...  46.7 us
    pallas_call x1, Pallas kernels, tiles(): pl.pallas_call(tile_kernel, grid_spec=pltpu.PrefetchScalarGridSpec(num_sc...  29.2 us

profile of v4, /device:TPU:0, one launch (start us, length us, event | category | flops | bytes accessed | tf_op | source)
XLA Modules:
  0.0 129.8 jit_solution(4262480211663349077)
XLA Ops:
  0.0 51.8 %gather.1 = (bf16[2,4,8,96,256]{4,3,2,1,0:T(8,128)(2,1)}, bf16[2,4,2,8,192,256]{5,4,3,2,1,0:T(8,128)(2,1)}, s32[2,4,4,1,128]{4,3,2,1,0:T(1,128)}, s32[1,640]{1,0...) custom-call(bf16[2048,768]{1,0:T(8,128)(2,1)} %nodes_ref.1, ...), custom_call_target="tpu_custom_call" | custom-call | tf_op jit(solution)/shard_map/gather/pallas_call | solution.py:308
  51.8 29.2 %tiles.1 = (bf16[64,96,256]{2,1,0:T(8,128)(2,1)}, f32[8,2,2,8,256]{4,3,2,1,0:T(8,128)}) custom-call(s32[1,640]{1,0:T(1,128)} %get-tuple-element.15.list_hbm, f32[6,1,128]{2,1,0:T(1,128)} %get-tuple-element.16.bias_hbm, s32[2,4,4,1,128]{4,3,2,1,0:T(1,128)} %get-tuple-element.17.table_hbm, f32[2,8,8,256]{3,2,1,0:T(8,128)} %get-tuple-element.18.m_hbm, ...), custom_call_target="tpu_custom_call" | custom-call | tf_op jit(solution)/shard_map/tiles/pallas_call | solution.py:451
  81.0 46.7 %tail.1 = bf16[192,2048]{1,0:T(8,128)(2,1)} custom-call(bf16[2,4,2,4,96,256]{5,4,3,2,1,0:T(8,128)(2,1)} %bitcast.15, f32[2,4,2,2,8,256]{5,4,3,2,1,0:T(8,128)} %bitcast.17, bf16[2048,768]{1,0:T(8,128)(2,1)} %nodes_ref.1, bf16[768,768]{1,0:T(8,128)(2,1)} %wo_hbm.1, bf16[768,3072]{1,0:T(8,128)(2,1)} %up_hbm.1, bf16[3072,768]{1,0:T(8,128)(2,1)} %down_hbm.1), custom_call_target="tpu_custom_call" | custom-call | tf_op jit(solution)/shard_map/tail/pallas_call | solution.py:692
  127.7 2.1 %copy.13 = bf16[2048,192]{0,1:T(8,128)(2,1)} copy(bf16[2048,192]{0,1:T(8,128)(2,1)} %bitcast.13) | data formatting | bytes 1572864

commit v5 on v4

--- a/solution.py
+++ b/solution.py
@@ -129,9 +129,9 @@
 
 def gather_kernel(
     nodes_hbm, weight_hbm, bias_in, bucket_ref, ko_ref, kl_ref, qo_ref, ql_ref,
-    qg_ref, kvg_ref, table_ref, list_out, bias_out, m_out, l_out, acc_out,
-    nodes_ref, weight_ref, q_ref, kv_ref, bucket_row, list_ref, bias_ref, m_ref, l_ref, acc_ref,
-    ring_send, ring_recv, pair_send, pair_recv, table_send, table_recv, own_sem, load_sem, weight_sem, store_sem,
+    qg_ref, kvg_ref, table_ref, list_ref, bias_ref, m_ref, l_ref, acc_ref,
+    nodes_ref, weight_ref,
+    ring_send, ring_recv, pair_send, pair_recv, table_send, table_recv, load_sem, weight_sem,
 ):
     z, y, c = coordinates()
     heads = range(PLAN_HEADS)
@@ -149,11 +149,11 @@
     node_loads = [load_nodes(0)]
     weight_load = local_copy(weight_hbm, weight_ref, weight_sem)
     node_loads += [load_nodes(p) for p in range(1, PIECES)]
-    bucket_row[...] = jnp.zeros(bucket_row.shape, jnp.int32)
-    bucket_row[:, : bucket_ref.shape[1]] = bucket_ref[...]
+    table_ref[c, z, y] = jnp.concatenate(
+        [bucket_ref[...], jnp.zeros((1, 128 - bucket_ref.shape[1]), jnp.int32)], 1
+    )
     for i in range(2 * PLAN_HEADS):
         bias_ref[i, :, : bias_in.shape[1]] = bias_in[i : i + 1] * LOG2E
-    stores = [local_copy(bucket_row, table_ref.at[c, z, y], store_sem.at[4])]
     sent = []
 
     def part(p):
@@ -168,12 +168,10 @@
         for kind, axis in (("kv", kv_axis), ("q", q_axis)):
             at = z if axis == "z" else y
             if kind == "q":
-                source = lambda r, plan=plan: q_ref.at[plan, r]
                 slot = lambda p, r, plan=plan: qg_ref.at[plan, p, r]
             else:
-                source = lambda r, plan=plan: kv_ref.at[plan, r]
                 slot = lambda p, r, plan=plan: kvg_ref.at[plan, p, c, r]
-            streams.append((len(streams), plan, kind, axis, at, source, slot))
+            streams.append((len(streams), plan, kind, axis, at, slot))
 
     def send(src, dst, send_sem, recv_sem, device):
         copy = pltpu.make_async_remote_copy(
@@ -190,7 +188,7 @@
         ).wait_recv()
 
     weight_load.wait()
-    features = 2 * PLAN_FEATURES
+    own_at = ((z, y), (y, z))
 
     def project(cluster, carry):
         normed = norm_rows(nodes_ref[pl.ds(cluster * CSIZE, CSIZE), :].astype(jnp.float32)).astype(jnp.bfloat16)
@@ -204,9 +202,9 @@
             for plan in range(2):
                 block = projected[plan * PLAN_FEATURES : (plan + 1) * PLAN_FEATURES]
                 if i == 0:
-                    q_ref[plan, cluster] = block
+                    qg_ref[plan, own_at[plan][0], cluster] = block
                 else:
-                    kv_ref[plan, cluster, (i - 1) * PLAN_FEATURES : i * PLAN_FEATURES, :] = block
+                    kvg_ref[plan, own_at[plan][1], c, cluster, (i - 1) * PLAN_FEATURES : i * PLAN_FEATURES, :] = block
         return carry
 
     ordered = [s for s in streams if s[2] == "kv"] + [s for s in streams if s[2] == "q"]
@@ -216,22 +214,19 @@
         if p == 0:
             greeted(partners)
             for step in (1, 2, 3):
-                send(bucket_row, table_ref.at[c, z, y], table_send.at[step - 1], table_recv.at[step - 1], ring_at("y", step))
-        for number, plan, kind, axis, at, source, slot in ordered:
+                send(table_ref.at[c, z, y], table_ref.at[c, z, y], table_send.at[step - 1], table_recv.at[step - 1], ring_at("y", step))
+        for number, plan, kind, axis, at, slot in ordered:
             for way, first in ((1, 0), (-1, PIECES)):
                 send(
-                    source(part(p)), slot(at, part(p)),
+                    slot(at, part(p)), slot(at, part(p)),
                     ring_send.at[number, first + p], ring_recv.at[number, first + p], ring_at(axis, way),
                 )
         if p % (PIECES // 2) == PIECES // 2 - 1:
             h = p // (PIECES // 2)
-            for number, plan, kind, axis, at, source, slot in ordered:
+            for number, plan, kind, axis, at, slot in ordered:
                 if kind == "kv":
-                    send(source(side(h)), slot(at, side(h)), pair_send.at[plan, h], pair_recv.at[plan, h], sibling())
-                stores.append(local_copy(source(side(h)), slot(at, side(h)), own_sem.at[number, h]))
+                    send(slot(at, side(h)), slot(at, side(h)), pair_send.at[plan, h], pair_recv.at[plan, h], sibling())
     list_ref[...] = make_list(qo_ref[...], ql_ref[...], ko_ref[...], kl_ref[...])
-    stores.append(local_copy(list_ref, list_out, store_sem.at[0]))
-    stores.append(local_copy(bias_ref, bias_out, store_sem.at[5]))
 
     for plan in range(2):
         bias = [bias_ref[plan * PLAN_HEADS + h, :, 0:1] for h in heads]
@@ -240,9 +235,9 @@
             group = [step * UNROLL + u for u in range(UNROLL)]
             pairs = [
                 (
-                    lambda h, i=i: q_ref[plan, i, rows(h), :],
-                    lambda h, i=i: kv_ref[plan, i, rows(h), :],
-                    lambda h, i=i: kv_ref[plan, i, rows(h, PLAN_FEATURES), :],
+                    lambda h, i=i: qg_ref[plan, own_at[plan][0], i, rows(h), :],
+                    lambda h, i=i: kvg_ref[plan, own_at[plan][1], c, i, rows(h), :],
+                    lambda h, i=i: kvg_ref[plan, own_at[plan][1], c, i, rows(h, PLAN_FEATURES), :],
                 )
                 for i in group
             ]
@@ -254,24 +249,20 @@
             return carry
 
         lax.fori_loop(0, LOCAL // UNROLL, own_tiles, 0)
-    stores.append(local_copy(m_ref, m_out, store_sem.at[1]))
-    stores.append(local_copy(l_ref, l_out, store_sem.at[2]))
-    stores.append(local_copy(acc_ref, acc_out, store_sem.at[3]))
-    stores[0].wait()
     for step in (1, 2, 3):
         arrived(table_ref.at[c, z, place(y, -step)], table_recv.at[step - 1])
     for step in (1, 2, 3):
         send(table_ref.at[c, z], table_ref.at[c, z], table_send.at[2 + step], table_recv.at[2 + step], ring_at("z", step))
     for h in range(2):
         for p in range(h * PIECES // 2, (h + 1) * PIECES // 2):
-            for number, plan, kind, axis, at, source, slot in ordered:
+            for number, plan, kind, axis, at, slot in ordered:
                 before, after = slot(place(at, -1), part(p)), slot(place(at, 1), part(p))
                 arrived(before, ring_recv.at[number, p])
                 arrived(after, ring_recv.at[number, PIECES + p])
                 onward, way = (before, 1) if h == 0 else (after, -1)
                 far = 2 * PIECES + p
                 send(onward, onward, ring_send.at[number, far], ring_recv.at[number, far], ring_at(axis, way))
-        for number, plan, kind, axis, at, source, slot in ordered:
+        for number, plan, kind, axis, at, slot in ordered:
             if kind == "kv":
                 for index, step in ((1, -1), (2, 1)):
                     block, sem = slot(place(at, step), side(h)), 2 * index + h
@@ -281,20 +272,18 @@
                 arrived(table_ref.at[c, place(z, -step)], table_recv.at[2 + step])
             send(table_ref.at[c], table_ref.at[c], table_send.at[6], table_recv.at[6], sibling())
     for h in range(2):
-        for number, plan, kind, axis, at, source, slot in ordered:
+        for number, plan, kind, axis, at, slot in ordered:
             for p in range(h * PIECES // 2, (h + 1) * PIECES // 2):
                 arrived(slot(place(at, 2), part(p)), ring_recv.at[number, 2 * PIECES + p])
             if kind == "kv":
                 far = slot(place(at, 2), side(h))
                 send(far, far, pair_send.at[plan, 6 + h], pair_recv.at[plan, 6 + h], sibling())
-    for number, plan, kind, axis, at, source, slot in streams:
+    for number, plan, kind, axis, at, slot in streams:
         if kind == "kv":
             for index, step in enumerate((0, -1, 1, 2)):
                 for h in range(2):
                     arrived(kvg_ref.at[plan, place(at, step), 1 - c, side(h)], pair_recv.at[plan, 2 * index + h])
     arrived(table_ref.at[1 - c], table_recv.at[6])
-    for copy in stores[1:]:
-        copy.wait()
     for copy in sent:
         copy.wait_send()
 
@@ -302,47 +291,38 @@
 def gather(nodes, qkv_weight, bias, bucket, key_owner, key_local, query_owner, query_local):
     any_space, in_vmem = pl.BlockSpec(memory_space=pl.ANY), pl.BlockSpec(memory_space=pltpu.VMEM)
     dma, vmem = pltpu.SemaphoreType.DMA, pltpu.VMEM
-    shape = jax.ShapeDtypeStruct
     q_shape, kv_shape = (PLAN_FEATURES, CSIZE), (2 * PLAN_FEATURES, CSIZE)
     m_shape, acc_shape = (2, LOCAL, 8, CSIZE), (2, LOCAL, PLAN_FEATURES, CSIZE)
     return pl.pallas_call(
         gather_kernel,
         out_shape=[
-            shape((2, RING, LOCAL) + q_shape, jnp.bfloat16),
-            shape((2, RING, 2, LOCAL) + kv_shape, jnp.bfloat16),
-            shape((2, RING, RING, 1, 128), jnp.int32),
-            shape((1, LIST_MAX), jnp.int32),
-            shape((2 * PLAN_HEADS, 1, 128), jnp.float32),
-            shape(m_shape, jnp.float32),
-            shape(m_shape, jnp.float32),
-            shape(acc_shape, jnp.float32),
-        ],
-        in_specs=[any_space] * 2 + [in_vmem] * 6,
-        out_specs=[any_space] * 8,
-        scratch_shapes=[
-            vmem(nodes.shape, jnp.bfloat16),
-            vmem(qkv_weight.shape, jnp.bfloat16),
-            vmem((2, LOCAL) + q_shape, jnp.bfloat16),
-            vmem((2, LOCAL) + kv_shape, jnp.bfloat16),
-            vmem((1, 128), jnp.int32),
+            vmem((2, RING, LOCAL) + q_shape, jnp.bfloat16),
+            vmem((2, RING, 2, LOCAL) + kv_shape, jnp.bfloat16),
+            vmem((2, RING, RING, 1, 128), jnp.int32),
             vmem((1, LIST_MAX), jnp.int32),
             vmem((2 * PLAN_HEADS, 1, 128), jnp.float32),
             vmem(m_shape, jnp.float32),
             vmem(m_shape, jnp.float32),
             vmem(acc_shape, jnp.float32),
+        ],
+        in_specs=[any_space] * 2 + [in_vmem] * 6,
+        out_specs=[in_vmem] * 8,
+        scratch_shapes=[
+            vmem(nodes.shape, jnp.bfloat16),
+            vmem(qkv_weight.shape, jnp.bfloat16),
             dma((4, 3 * PIECES)), dma((4, 3 * PIECES)), dma((2, 8)), dma((2, 8)), dma((7,)), dma((7,)),
-            dma((4, 2)), dma((PIECES,)), dma(()), dma((6,)),
+            dma((PIECES,)), dma(()),
         ],
         compiler_params=pltpu.CompilerParams(
-            collective_id=0, has_side_effects=True, vmem_limit_bytes=56 * 2**20
+            collective_id=0, has_side_effects=True, vmem_limit_bytes=42 * 2**20
         ),
         name="gather",
     )(nodes, qkv_weight, bias, bucket, key_owner, key_local, query_owner, query_local)
 
 
 def tile_kernel(
-    list_hbm, bias_hbm, table_hbm, m_hbm, l_hbm, acc_hbm, qg_ref, kvg_ref, part_ref, log_ref,
-    q_ref, kv_ref, list_ref, bias_ref, table_ref, m_ref, l_ref, acc_ref, q_sem, kv_sem, table_sem, state_sem,
+    list_hbm, bias_hbm, table_hbm, m_hbm, l_hbm, acc_hbm, q_ref, kv_ref, part_ref, log_ref,
+    list_ref, bias_ref, table_ref, m_ref, l_ref, acc_ref, table_sem, state_sem,
 ):
     heads = range(PLAN_HEADS)
     z, y, c = coordinates()
@@ -358,11 +338,6 @@
     load(0, list_hbm, list_ref, table_sem.at[0])
     load(0, table_hbm, table_ref, table_sem.at[1])
     load(0, bias_hbm, bias_ref, table_sem.at[2])
-    for plan in range(2):
-        side = pl.ds(plan * queries // 2, queries // 2)
-        load(plan, qg_ref.at[side], q_ref.at[side], q_sem.at[plan])
-        side = pl.ds(plan * keys // 2, keys // 2)
-        load(plan, kvg_ref.at[side], kv_ref.at[side], kv_sem.at[plan])
     for plan in range(2):
         own = (z if plan == 0 else y) + plan * RING
 
@@ -443,35 +418,25 @@
 
 def tiles(items, bias, table, m, l, acc, q_all, kv_all):
     queries, keys = 2 * RING * LOCAL, 2 * RING * 2 * LOCAL
-    any_space = pl.BlockSpec(memory_space=pl.ANY)
-    whole = lambda shape: pl.BlockSpec(shape, lambda i, *_: (0,) * len(shape))
+    in_vmem = pl.BlockSpec(memory_space=pltpu.VMEM)
     part_shape = (queries, PLAN_FEATURES, CSIZE)
     log_shape = (2 * RING, 2, 2, 8, CSIZE)
     dma, vmem = pltpu.SemaphoreType.DMA, pltpu.VMEM
     return pl.pallas_call(
         tile_kernel,
-        grid_spec=pltpu.PrefetchScalarGridSpec(
-            num_scalar_prefetch=0,
-            grid=(1,),
-            in_specs=[any_space] * 8,
-            out_specs=[whole(part_shape), whole(log_shape)],
-            scratch_shapes=[
-                vmem((queries, PLAN_FEATURES, CSIZE), jnp.bfloat16),
-                vmem((keys, 2 * PLAN_FEATURES, CSIZE), jnp.bfloat16),
+        in_specs=[in_vmem] * 8,
+        out_specs=[in_vmem] * 2,
+        scratch_shapes=[
                 pltpu.SMEM((1, LIST_MAX), jnp.int32),
                 pltpu.SMEM((2 * PLAN_HEADS, 1, 128), jnp.float32),
                 pltpu.SMEM((2, RING, RING, 1, 128), jnp.int32),
                 vmem((queries + 1, 8, CSIZE), jnp.float32),
                 vmem((queries + 1, 8, CSIZE), jnp.float32),
                 vmem((queries + 1, PLAN_FEATURES, CSIZE), jnp.float32),
-                dma((2,)), dma((2,)), dma((3,)), dma((2, 3)),
-            ],
-        ),
-        out_shape=[
-            jax.ShapeDtypeStruct(part_shape, jnp.bfloat16),
-            jax.ShapeDtypeStruct(log_shape, jnp.float32),
+            dma((3,)), dma((2, 3)),
         ],
-        compiler_params=pltpu.CompilerParams(vmem_limit_bytes=56 * 2**20),
+        out_shape=[vmem(part_shape, jnp.bfloat16), vmem(log_shape, jnp.float32)],
+        compiler_params=pltpu.CompilerParams(vmem_limit_bytes=16 * 2**20),
         name="tiles",
     )(
         items, bias, table, m, l, acc,
@@ -481,9 +446,8 @@
 
 def tail_kernel(
     part_ref, log_ref, nodes_ref, wo_hbm, up_hbm, down_hbm, out_ref,
-    wo_ref, up_ref, down_ref, rows_ref, part_in, log_in, far_part, far_log, own_part, own_log, near_part, near_log,
-    both_part, both_log, merged, gathered, resid_ref, normed_ref, staged,
-    weight_sem, own_sem, near_sem, back_send, back_recv, x_send, x_recv, out_send, out_recv, out_own,
+    wo_ref, up_ref, down_ref, rows_ref, part_in, log_in, far_part, far_log, both_part, both_log, merged, gathered, resid_ref, normed_ref, staged,
+    weight_sem, back_send, back_recv, x_send, x_recv, out_send, out_recv, out_own,
 ):
     z, y, c = coordinates()
     me = lax.axis_index("owner")
@@ -504,21 +468,6 @@
     ways = ((0, 1), (1, -1))
     ring = [(0, "z", z), (1, "y", y)]
     half = lambda h: pl.ds(h * (RING // 2), RING // 2)
-    near, ready = [], []
-    for plan, axis, at in ring:
-        for way, step in ways:
-            for turn in range(2):
-                near.append(load(
-                    part_ref.at[plan, place(at, step), turn, half(way)], near_part.at[plan, way, turn],
-                    near_sem.at[plan, way, turn, 0],
-                ))
-                near.append(load(
-                    log_ref.at[plan, place(at, step), turn, way], near_log.at[plan, way, turn],
-                    near_sem.at[plan, way, turn, 1],
-                ))
-    for plan, axis, at in ring:
-        ready.append(load(part_ref.at[plan, at], own_part.at[plan], own_sem.at[plan, 0]))
-        ready.append(load(log_ref.at[plan, at], own_log.at[plan], own_sem.at[plan, 1]))
     weights = [
         load(nodes_ref.at[pl.ds(x * 2 * CSIZE, 2 * CSIZE)], rows_ref, weight_sem.at[0]),
         load(wo_hbm, wo_ref, weight_sem.at[1]),
@@ -568,7 +517,7 @@
             for way, step in ways:
                 arrived(far_part.at[plan, way, turn], back_recv.at[plan, way, turn, 0])
                 arrived(far_log.at[plan, way, turn], back_recv.at[plan, way, turn, 1])
-                one, two = near_log[plan, way, turn], far_log[plan, way, turn]
+                one, two = log_ref[plan, place(at, step), turn, way], far_log[plan, way, turn]
                 best = jnp.maximum(one, two)
                 shares = [jnp.exp2(one - best), jnp.exp2(two - best)]
                 total = shares[0] + shares[1]
@@ -579,7 +528,7 @@
                     for h in heads:
                         row = to * PLAN_HEADS + h
                         both_part[plan, way, turn, to, rows(h), :] = (
-                            near_part[plan, way, turn, to, rows(h), :].astype(jnp.float32) * shares[0][row : row + 1]
+                            part_ref[plan, place(at, step), turn, way * 2 + to, rows(h), :].astype(jnp.float32) * shares[0][row : row + 1]
                             + far_part[plan, way, turn, to, rows(h), :].astype(jnp.float32) * shares[1][row : row + 1]
                         ).astype(jnp.bfloat16)
                 to = ring_at(axis, step)
@@ -595,17 +544,17 @@
                 arrived(log_in.at[plan, way, turn, 1 - way], back_recv.at[plan, way, turn, 3])
                 arrived(part_in.at[plan, way, turn, half(way)], back_recv.at[plan, way, turn, 4])
                 arrived(log_in.at[plan, way, turn, way], back_recv.at[plan, way, turn, 5])
-        for plan in range(2):
+        for plan, axis, at in ring:
             for to in range(RING):
                 h0 = to // 2
-                logs = [own_log[plan, turn, h0]] + [log_in[plan, way, turn, h0] for way in range(2)]
+                logs = [log_ref[plan, at, turn, h0]] + [log_in[plan, way, turn, h0] for way in range(2)]
                 best = jnp.maximum(jnp.maximum(logs[0], logs[1]), logs[2])
                 shares = [jnp.exp2(log - best) for log in logs]
                 scale = 1.0 / (shares[0] + shares[1] + shares[2])
                 shares = [share * scale for share in shares]
                 for h in heads:
                     row = to % 2 * PLAN_HEADS + h
-                    total = own_part[plan, turn, to, rows(h), :].astype(jnp.float32) * shares[0][row : row + 1]
+                    total = part_ref[plan, at, turn, to, rows(h), :].astype(jnp.float32) * shares[0][row : row + 1]
                     for way in range(2):
                         total += part_in[plan, way, turn, to, rows(h), :].astype(jnp.float32) * shares[way + 1][row : row + 1]
                     merged[turn, to, rows(h, plan * PLAN_FEATURES), :] = total.astype(jnp.bfloat16)
@@ -656,12 +605,8 @@
         out_copies.append(load(block(x), target, out_own.at[turn]))
 
     send_out(0)
-    for copy in near:
-        copy.wait()
     combine(0)
     send_out(1)
-    for copy in ready:
-        copy.wait()
     merge(0)
     combine(1)
     for copy in weights:
@@ -692,7 +637,7 @@
     return pl.pallas_call(
         tail_kernel,
         out_shape=jax.ShapeDtypeStruct((features, nodes.shape[0]), jnp.bfloat16),
-        in_specs=[any_space] * 6,
+        in_specs=[pl.BlockSpec(memory_space=pltpu.VMEM)] * 2 + [any_space] * 4,
         out_specs=any_space,
         scratch_shapes=[
             vmem(out_weight.shape, jnp.bfloat16),
@@ -703,10 +648,6 @@
             vmem((2, 2, 2, 2, 8, CSIZE), jnp.float32),
             vmem((2, 2, 2, 2, PLAN_FEATURES, CSIZE), jnp.bfloat16),
             vmem((2, 2, 2, 8, CSIZE), jnp.float32),
-            vmem((2, 2, RING, PLAN_FEATURES, CSIZE), jnp.bfloat16),
-            vmem((2, 2, 2, 8, CSIZE), jnp.float32),
-            vmem((2, 2, 2, 2, PLAN_FEATURES, CSIZE), jnp.bfloat16),
-            vmem((2, 2, 2, 8, CSIZE), jnp.float32),
             vmem((2, 2, 2, 2, PLAN_FEATURES, CSIZE), jnp.bfloat16),
             vmem((2, 2, 2, 8, CSIZE), jnp.float32),
             vmem((2, RING, features, CSIZE), jnp.bfloat16),
@@ -714,11 +655,11 @@
             vmem((2 * CSIZE, width), jnp.float32),
             vmem((2 * CSIZE, width), jnp.bfloat16),
             vmem((RING * features, 2 * CSIZE), jnp.bfloat16),
-            dma((4,)), dma((2, 2)), dma((2, 2, 2, 2)), dma((2, 2, 2, 6)), dma((2, 2, 2, 6)),
+            dma((4,)), dma((2, 2, 2, 6)), dma((2, 2, 2, 6)),
             dma((2, 3)), dma((2, 3)), dma((2, 3)), dma((2, 3)), dma((2,)),
         ],
         compiler_params=pltpu.CompilerParams(
-            collective_id=1, has_side_effects=True, vmem_limit_bytes=56 * 2**20
+            collective_id=1, has_side_effects=True, vmem_limit_bytes=32 * 2**20
         ),
         name="tail",
     )(parts, logs, nodes, out_weight, up_weight, down_weight)
@@ -730,12 +671,12 @@
 ):
     lists = [array.reshape(8, 128) for array in (key_owner, key_local, query_owner, query_local)]
     q_all, kv_all, table, items, bias, m, l, acc = gather(
-        nodes, qkv_weight.swapaxes(1, 2), hop_bias.T, hop_bucket.reshape(1, -1), *lists
+        *[pltpu.with_memory_space_constraint(a, pltpu.HBM) for a in (nodes, qkv_weight.swapaxes(1, 2))], hop_bias.T, hop_bucket.reshape(1, -1), *lists
     )
     parts, logs = tiles(items, bias, table, m, l, acc, q_all, kv_all)
     return tail(
         parts.reshape(2, RING, 2, RING, PLAN_FEATURES, CSIZE), logs.reshape(2, RING, 2, 2, 8, CSIZE),
-        nodes, out_weight, up_weight, down_weight,
+        *[pltpu.with_memory_space_constraint(a, pltpu.HBM) for a in (nodes, out_weight, up_weight, down_weight)],
     ).T
 
 

time: 130 us -> 116 us (0.89)
  the two profiles are of different devices: /device:TPU:0 before, /device:TPU:1 now
where the time goes in v5:
time: 116 us
  Pallas kernels  115 us (99%)
    pallas_call x1, Pallas kernels, gather(): pl.pallas_call(gather_kernel, out_shape=[vmem((2, RING, LOCAL) + q_shape,...  52.3 us
    pallas_call x1, Pallas kernels, tail(): pl.pallas_call(tail_kernel, out_shape=jax.ShapeDtypeStruct((features, nod...  37.9 us
    pallas_call x1, Pallas kernels, tiles(): pl.pallas_call(tile_kernel, in_specs=[in_vmem] * 8, out_specs=[in_vmem] *...  24.8 us

profile of v5, /device:TPU:1, one launch (start us, length us, event | category | flops | bytes accessed | tf_op | source)
XLA Modules:
  0.0 115.9 jit_solution(17669738865552950748)
XLA Ops:
  0.0 52.3 %gather.1 = (bf16[2,4,8,96,256]{4,3,2,1,0:T(8,128)(2,1)S(1)}, bf16[2,4,2,8,192,256]{5,4,3,2,1,0:T(8,128)(2,1)S(1)}, s32[2,4,4,1,128]{4,3,2,1,0:T(1,128)S(1)}, s3...) custom-call(bf16[2048,768]{1,0:T(8,128)(2,1)} %nodes_ref.1, ...), custom_call_target="tpu_custom_call" | custom-call | tf_op jit(solution)/shard_map/gather/pallas_call | solution.py:296
  52.3 24.8 %tiles.1 = (bf16[64,96,256]{2,1,0:T(8,128)(2,1)S(1)}, f32[8,2,2,8,256]{4,3,2,1,0:T(8,128)S(1)}) custom-call(s32[1,640]{1,0:T(1,128)S(1)} %get-tuple-element.15.list_hbm, f32[6,1,128]{2,1,0:T(1,128)S(1)} %get-tuple-element.16.bias_hbm, s32[2,4,4,1,128]{4,3,2,1,0:T(1,128)S(1)} %get-tuple-element.17.table_hbm, f32[2,8,8,256]{3,2,1,0:T(8,128)S(1)} %get-tuple-element.18.m_hbm, ...), custom_call_target="tpu_custom_call" | custom-call | tf_op jit(solution)/shard_map/tiles/pallas_call | solution.py:425
  77.1 37.9 %tail.1 = bf16[192,2048]{1,0:T(8,128)(2,1)S(1)} custom-call(bf16[2,4,2,4,96,256]{5,4,3,2,1,0:T(8,128)(2,1)S(1)} %bitcast.15, f32[2,4,2,2,8,256]{5,4,3,2,1,0:T(8,128)S(1)} %bitcast.16, bf16[2048,768]{1,0:T(8,128)(2,1)} %nodes_ref.1, bf16[768,768]{1,0:T(8,128)(2,1)} %wo_hbm.1, bf16[768,3072]{1,0:T(8,128)(2,1)} %up_hbm.1, bf16[3072,768]{1,0:T(8,128)(2,1)} %down_hbm.1), custom_call_target="tpu_custom_call" | custom-call | tf_op jit(solution)/shard_map/tail/pallas_call | solution.py:637
  115.0 0.9 copy.13

commit v6 on v5

--- a/solution.py
+++ b/solution.py
@@ -22,6 +22,8 @@
 NEVER = -1e30
 NOTHING = 64
 PIECES = 4
+BLOCKS = 2
+TURNS = ((0, 0, 256), (1, 0, 128), (1, 128, 128))
 
 
 def norm_rows(values):
@@ -259,7 +261,7 @@
                 before, after = slot(place(at, -1), part(p)), slot(place(at, 1), part(p))
                 arrived(before, ring_recv.at[number, p])
                 arrived(after, ring_recv.at[number, PIECES + p])
-                onward, way = (before, 1) if h == 0 else (after, -1)
+                onward, way = (before, 1) if p % 2 == 0 else (after, -1)
                 far = 2 * PIECES + p
                 send(onward, onward, ring_send.at[number, far], ring_recv.at[number, far], ring_at(axis, way))
         for number, plan, kind, axis, at, slot in ordered:
@@ -495,93 +497,109 @@
         send(src, dst, back_send.at[plan, way, turn, kind], back_recv.at[plan, way, turn, kind], device)
 
     def send_out(turn):
+        t, first, count = TURNS[turn]
+        lanes = pl.ds(first, count)
         for plan, axis, at in ring:
             for way, step in ways:
                 to, far = ring_at(axis, step), place(at, 2)
-                back(plan, way, turn, 0, part_ref.at[plan, far, turn, half(way)], far_part.at[plan, way, turn], to)
-                back(plan, way, turn, 1, log_ref.at[plan, far, turn, way], far_log.at[plan, way, turn], to)
+                back(plan, way, turn, 0, part_ref.at[plan, far, t, half(way), :, lanes], far_part.at[plan, way, t, :, :, lanes], to)
+                back(plan, way, turn, 1, log_ref.at[plan, far, t, way, :, lanes], far_log.at[plan, way, t, :, lanes], to)
         for plan, axis, at in ring:
             for way, step in ways:
                 to, next_at = ring_at(axis, step), place(at, step)
                 back(
-                    plan, way, turn, 2, part_ref.at[plan, next_at, turn, half(1 - way)],
-                    part_in.at[plan, way, turn, half(1 - way)], to,
+                    plan, way, turn, 2, part_ref.at[plan, next_at, t, half(1 - way), :, lanes],
+                    part_in.at[plan, way, t, half(1 - way), :, lanes], to,
                 )
                 back(
-                    plan, way, turn, 3, log_ref.at[plan, next_at, turn, 1 - way],
-                    log_in.at[plan, way, turn, 1 - way], to,
+                    plan, way, turn, 3, log_ref.at[plan, next_at, t, 1 - way, :, lanes],
+                    log_in.at[plan, way, t, 1 - way, :, lanes], to,
                 )
 
     def combine(turn):
+        t, first, count = TURNS[turn]
+        lanes = pl.ds(first, count)
+        span = slice(first, first + count)
         for plan, axis, at in ring:
             for way, step in ways:
-                arrived(far_part.at[plan, way, turn], back_recv.at[plan, way, turn, 0])
-                arrived(far_log.at[plan, way, turn], back_recv.at[plan, way, turn, 1])
-                one, two = log_ref[plan, place(at, step), turn, way], far_log[plan, way, turn]
+                arrived(far_part.at[plan, way, t, :, :, lanes], back_recv.at[plan, way, turn, 0])
+                arrived(far_log.at[plan, way, t, :, lanes], back_recv.at[plan, way, turn, 1])
+                one, two = log_ref[plan, place(at, step), t, way, :, span], far_log[plan, way, t, :, span]
                 best = jnp.maximum(one, two)
                 shares = [jnp.exp2(one - best), jnp.exp2(two - best)]
                 total = shares[0] + shares[1]
-                both_log[plan, way, turn] = best + jnp.log2(total)
+                both_log[plan, way, t, :, span] = best + jnp.log2(total)
                 scale = 1.0 / total
                 shares = [share * scale for share in shares]
                 for to in range(2):
                     for h in heads:
                         row = to * PLAN_HEADS + h
-                        both_part[plan, way, turn, to, rows(h), :] = (
-                            part_ref[plan, place(at, step), turn, way * 2 + to, rows(h), :].astype(jnp.float32) * shares[0][row : row + 1]
-                            + far_part[plan, way, turn, to, rows(h), :].astype(jnp.float32) * shares[1][row : row + 1]
+                        both_part[plan, way, t, to, rows(h), span] = (
+                            part_ref[plan, place(at, step), t, way * 2 + to, rows(h), span].astype(jnp.float32) * shares[0][row : row + 1]
+                            + far_part[plan, way, t, to, rows(h), span].astype(jnp.float32) * shares[1][row : row + 1]
                         ).astype(jnp.bfloat16)
                 to = ring_at(axis, step)
-                back(plan, way, turn, 4, both_part.at[plan, way, turn], part_in.at[plan, way, turn, half(way)], to)
-                back(plan, way, turn, 5, both_log.at[plan, way, turn], log_in.at[plan, way, turn, way], to)
+                back(
+                    plan, way, turn, 4, both_part.at[plan, way, t, :, :, lanes],
+                    part_in.at[plan, way, t, half(way), :, lanes], to,
+                )
+                back(
+                    plan, way, turn, 5, both_log.at[plan, way, t, :, lanes], log_in.at[plan, way, t, way, :, lanes], to
+                )
 
     mine = pl.ds(pl.multiple_of(x * features, 64), features)
 
     def merge(turn):
+        t, first, count = TURNS[turn]
+        lanes = pl.ds(first, count)
+        span = slice(first, first + count)
         for plan in range(2):
             for way in range(2):
-                arrived(part_in.at[plan, way, turn, half(1 - way)], back_recv.at[plan, way, turn, 2])
-                arrived(log_in.at[plan, way, turn, 1 - way], back_recv.at[plan, way, turn, 3])
-                arrived(part_in.at[plan, way, turn, half(way)], back_recv.at[plan, way, turn, 4])
-                arrived(log_in.at[plan, way, turn, way], back_recv.at[plan, way, turn, 5])
+                arrived(part_in.at[plan, way, t, half(1 - way), :, lanes], back_recv.at[plan, way, turn, 2])
+                arrived(log_in.at[plan, way, t, 1 - way, :, lanes], back_recv.at[plan, way, turn, 3])
+                arrived(part_in.at[plan, way, t, half(way), :, lanes], back_recv.at[plan, way, turn, 4])
+                arrived(log_in.at[plan, way, t, way, :, lanes], back_recv.at[plan, way, turn, 5])
         for plan, axis, at in ring:
             for to in range(RING):
                 h0 = to // 2
-                logs = [log_ref[plan, at, turn, h0]] + [log_in[plan, way, turn, h0] for way in range(2)]
+                logs = [log_ref[plan, at, t, h0, :, span]] + [log_in[plan, way, t, h0, :, span] for way in range(2)]
                 best = jnp.maximum(jnp.maximum(logs[0], logs[1]), logs[2])
                 shares = [jnp.exp2(log - best) for log in logs]
                 scale = 1.0 / (shares[0] + shares[1] + shares[2])
                 shares = [share * scale for share in shares]
                 for h in heads:
                     row = to % 2 * PLAN_HEADS + h
-                    total = part_ref[plan, at, turn, to, rows(h), :].astype(jnp.float32) * shares[0][row : row + 1]
+                    total = part_ref[plan, at, t, to, rows(h), span].astype(jnp.float32) * shares[0][row : row + 1]
                     for way in range(2):
-                        total += part_in[plan, way, turn, to, rows(h), :].astype(jnp.float32) * shares[way + 1][row : row + 1]
-                    merged[turn, to, rows(h, plan * PLAN_FEATURES), :] = total.astype(jnp.bfloat16)
+                        total += part_in[plan, way, t, to, rows(h), span].astype(jnp.float32) * shares[way + 1][row : row + 1]
+                    merged[t, to, rows(h, plan * PLAN_FEATURES), span] = total.astype(jnp.bfloat16)
         for step in (2, 1, 3):
             send(
-                merged.at[turn, place(x, step)], gathered.at[turn, mine],
+                merged.at[t, place(x, step), :, lanes], gathered.at[t, mine, lanes],
                 x_send.at[turn, step - 1], x_recv.at[turn, step - 1], across(step),
             )
-        gathered[turn, mine, :] = merged[turn, x]
-
-    wide = up_ref.shape[1] // RING
+        gathered[t, mine, span] = merged[t, x, :, span]
+
+    wide = up_ref.shape[1] // BLOCKS
     out_copies = []
 
     def begin(turn):
-        part = slice(turn * CSIZE, (turn + 1) * CSIZE)
+        t, first, count = TURNS[turn]
+        lanes = pl.ds(first, count)
+        part = slice(t * CSIZE + first, t * CSIZE + first + count)
         for step in (1, 2, 3):
             source = place(x, -step)
-            arrived(gathered.at[turn, pl.ds(pl.multiple_of(source * features, 64), features)], x_recv.at[turn, step - 1])
+            arrived(gathered.at[t, pl.ds(pl.multiple_of(source * features, 64), features), lanes], x_recv.at[turn, step - 1])
         mixed = lax.dot_general(
-            gathered[turn], wo_ref[...], (((0,), (0,)), ((), ())), preferred_element_type=jnp.float32
+            gathered[t, :, first : first + count], wo_ref[...], (((0,), (0,)), ((), ())), preferred_element_type=jnp.float32
         )
         resid = rows_ref[part, :].astype(jnp.float32) + mixed
         resid_ref[part, :] = resid
         normed_ref[part, :] = norm_rows(resid).astype(jnp.bfloat16)
 
-    def feed(turn, first, last):
-        part = slice(turn * CSIZE, (turn + 1) * CSIZE)
+    def feed(turn, start, end):
+        t, first, count = TURNS[turn]
+        part = slice(t * CSIZE + first, t * CSIZE + first + count)
 
         def block(step, carry):
             units = pl.ds(pl.multiple_of(step * wide, 128), wide)
@@ -591,12 +609,13 @@
             resid_ref[part, :] += jnp.dot(hidden, down_ref[units, :], preferred_element_type=jnp.float32)
             return carry
 
-        lax.fori_loop(first, last, block, 0)
+        lax.fori_loop(start, end, block, 0)
 
     def hand_out(turn):
-        part = slice(turn * CSIZE, (turn + 1) * CSIZE)
+        t, first, count = TURNS[turn]
+        part = slice(t * CSIZE + first, t * CSIZE + first + count)
         staged[:, part] = resid_ref[part, :].astype(jnp.bfloat16).T
-        target = out_ref.at[:, pl.ds(pl.multiple_of((x * 2 + turn) * CSIZE, CSIZE), CSIZE)]
+        target = out_ref.at[:, pl.ds(pl.multiple_of((x * 2 + t) * CSIZE + first, 128), count)]
         block = lambda j: staged.at[pl.ds(pl.multiple_of(j * features, 64), features), part]
         for step in (2, 1, 3):
             send(
@@ -607,22 +626,29 @@
     send_out(0)
     combine(0)
     send_out(1)
+    send_out(2)
     merge(0)
     combine(1)
+    combine(2)
+    merge(1)
     for copy in weights:
         copy.wait()
     begin(0)
-    feed(0, 0, 2)
-    merge(1)
-    feed(0, 2, RING)
+    feed(0, 0, BLOCKS // 2)
+    merge(2)
+    feed(0, BLOCKS // 2, BLOCKS)
     hand_out(0)
-    begin(1)
-    feed(1, 0, RING)
-    hand_out(1)
-    for turn in range(2):
+    for turn in (1, 2):
+        begin(turn)
+        feed(turn, 0, BLOCKS)
+        hand_out(turn)
+    for turn, (t, first, count) in enumerate(TURNS):
         for step in (1, 2, 3):
             source = place(x, -step)
-            arrived(out_ref.at[:, pl.ds(pl.multiple_of((source * 2 + turn) * CSIZE, CSIZE), CSIZE)], out_recv.at[turn, step - 1])
+            arrived(
+                out_ref.at[:, pl.ds(pl.multiple_of((source * 2 + t) * CSIZE + first, 128), count)],
+                out_recv.at[turn, step - 1],
+            )
     for copy in out_copies:
         copy.wait()
     for copy in sent:
@@ -655,8 +681,8 @@
             vmem((2 * CSIZE, width), jnp.float32),
             vmem((2 * CSIZE, width), jnp.bfloat16),
             vmem((RING * features, 2 * CSIZE), jnp.bfloat16),
-            dma((4,)), dma((2, 2, 2, 6)), dma((2, 2, 2, 6)),
-            dma((2, 3)), dma((2, 3)), dma((2, 3)), dma((2, 3)), dma((2,)),
+            dma((4,)), dma((2, 2, 3, 6)), dma((2, 2, 3, 6)),
+            dma((3, 3)), dma((3, 3)), dma((3, 3)), dma((3, 3)), dma((3,)),
         ],
         compiler_params=pltpu.CompilerParams(
             collective_id=1, has_side_effects=True, vmem_limit_bytes=32 * 2**20

time: 116 us -> 112 us (0.966)
  the two profiles are of different devices: /device:TPU:1 before, /device:TPU:0 now
where the time goes in v6:
time: 112 us; the launch traced here: 111 us
  Pallas kernels  110 us (98%)
    pallas_call x1, Pallas kernels, gather(): pl.pallas_call(gather_kernel, out_shape=[vmem((2, RING, LOCAL) + q_shape,...  48.5 us
    pallas_call x1, Pallas kernels, tail(): pl.pallas_call(tail_kernel, out_shape=jax.ShapeDtypeStruct((features, nod...  46.3 us
    pallas_call x1, Pallas kernels, tiles(): pl.pallas_call(tile_kernel, in_specs=[in_vmem] * 8, out_specs=[in_vmem] *...  15.4 us

profile of v6, /device:TPU:0, one launch (start us, length us, event | category | flops | bytes accessed | tf_op | source)
XLA Modules:
  0.0 111.1 jit_solution(8562403201341113179)
XLA Ops:
  0.0 48.5 %gather.1 = (bf16[2,4,8,96,256]{4,3,2,1,0:T(8,128)(2,1)S(1)}, bf16[2,4,2,8,192,256]{5,4,3,2,1,0:T(8,128)(2,1)S(1)}, s32[2,4,4,1,128]{4,3,2,1,0:T(1,128)S(1)}, s3...) custom-call(bf16[2048,768]{1,0:T(8,128)(2,1)} %nodes_ref.1, ...), custom_call_target="tpu_custom_call" | custom-call | tf_op jit(solution)/shard_map/gather/pallas_call | solution.py:298
  48.5 15.4 %tiles.1 = (bf16[64,96,256]{2,1,0:T(8,128)(2,1)S(1)}, f32[8,2,2,8,256]{4,3,2,1,0:T(8,128)S(1)}) custom-call(s32[1,640]{1,0:T(1,128)S(1)} %get-tuple-element.15.list_hbm, f32[6,1,128]{2,1,0:T(1,128)S(1)} %get-tuple-element.16.bias_hbm, s32[2,4,4,1,128]{4,3,2,1,0:T(1,128)S(1)} %get-tuple-element.17.table_hbm, f32[2,8,8,256]{3,2,1,0:T(8,128)S(1)} %get-tuple-element.18.m_hbm, ...), custom_call_target="tpu_custom_call" | custom-call | tf_op jit(solution)/shard_map/tiles/pallas_call | solution.py:427
  63.9 46.3 %tail.1 = bf16[192,2048]{1,0:T(8,128)(2,1)S(1)} custom-call(bf16[2,4,2,4,96,256]{5,4,3,2,1,0:T(8,128)(2,1)S(1)} %bitcast.15, f32[2,4,2,2,8,256]{5,4,3,2,1,0:T(8,128)S(1)} %bitcast.16, bf16[2048,768]{1,0:T(8,128)(2,1)} %nodes_ref.1, bf16[768,768]{1,0:T(8,128)(2,1)} %wo_hbm.1, bf16[768,3072]{1,0:T(8,128)(2,1)} %up_hbm.1, bf16[3072,768]{1,0:T(8,128)(2,1)} %down_hbm.1), custom_call_target="tpu_custom_call" | custom-call | tf_op jit(solution)/shard_map/tail/pallas_call | solution.py:663
  110.2 0.9 copy.13

commit v7 on v6

--- a/solution.py
+++ b/solution.py
@@ -97,26 +97,53 @@
     kz, ky, kc = div(key_owner, 8), rem(div(key_owner, 2), 4), rem(key_owner, 2)
     iota = lax.broadcasted_iota
     number = iota(jnp.int32, (8, 128), 0) * 128 + iota(jnp.int32, (8, 128), 1)
-    mine_a = (qy == y) & (qc == c) & (kz == z)
-    mine_b = (qz == z) & (qc == c) & (ky == y)
-    item_a = (qz * 8 + query_local) + (ky * 16 + kc * 8 + key_local) * 128 + number * 16384
-    item_b = (32 + qy * 8 + query_local) + (64 + kz * 16 + kc * 8 + key_local) * 128 + number * 16384
-    zero, one = jnp.zeros((8, 128), jnp.float32), jnp.ones((8, 128), jnp.float32)
-    ones = jnp.concatenate([jnp.where(mine_a, one, zero), jnp.where(mine_b, one, zero)], 0)
-    items = jnp.concatenate([item_a, item_b], 0).astype(jnp.float32)
+
+    def seen(d):
+        d = rem(d + RING, RING)
+        return jnp.where(d == 0, 0, jnp.where(d == RING - 1, 1, d + 1))
+
+    def table(mine, q_seen, k_seen, plan):
+        near = k_seen != RING - 1
+        state = plan * RING * LOCAL + q_seen * LOCAL + query_local
+        item = state + (jnp.where(near, k_seen * 2 * LOCAL, 0) + kc * LOCAL + key_local) * 128 + number * 16384
+        early = mine & near & (q_seen != RING - 1)
+        flag = lambda f: jnp.where(f, jnp.ones((8, 128), jnp.float32), 0.0)
+        return [flag(mine & near), flag(mine & (k_seen == RING - 1)), jnp.where(early, state, -1).astype(jnp.float32), item.astype(jnp.float32)]
+
+    tables = zip(
+        table((qy == y) & (qc == c) & (kz == z), seen(qz - z), seen(ky - y), 0),
+        table((qz == z) & (qc == c) & (ky == y), seen(qy - y), seen(kz - z), 1),
+    )
+    near, far, early, items = [jnp.concatenate(pair, 0) for pair in tables]
+    early, values = early.T, items.T
+    numbers = jnp.concatenate([number, number], 0).astype(jnp.float32).T
+    lane = iota(jnp.int32, (128, 128), 1).astype(jnp.float32)
+    first = jnp.full((128, 128), 4096.0, jnp.float32)
+    for r in range(16):
+        first = jnp.minimum(first, jnp.where(early[:, r : r + 1] == lane, numbers[:, r : r + 1], 4096.0))
+    first = jnp.min(first, axis=0, keepdims=True)
+    slots, chosen = jnp.zeros((128, 128), jnp.float32), jnp.zeros((128, 128), jnp.float32)
+    for r in range(16):
+        hit = jnp.where((early[:, r : r + 1] == lane) & (numbers[:, r : r + 1] == first), 1.0, 0.0)
+        slots += hit * (values[:, r : r + 1] + 1.0)
+        chosen += jnp.where(lane == r, jnp.max(hit, axis=1, keepdims=True), 0.0)
+    slots = (jnp.sum(slots, axis=0, keepdims=True) - 1.0).astype(jnp.int32)
+    near = near * (1.0 - chosen.T[:16])
     before = jnp.where(iota(jnp.int32, (128, 128), 0) < iota(jnp.int32, (128, 128), 1), 1.0, 0.0)
-    inside = jnp.dot(ones, before, preferred_element_type=jnp.float32)
-    counts = jnp.sum(ones, axis=1, keepdims=True)
-    row = iota(jnp.int32, (16, 128), 0)
-    wide = jnp.broadcast_to(counts, (16, 128))
-    first = jnp.sum(jnp.where(row < 8, wide, 0.0), axis=0, keepdims=True)
-    filled = jnp.floor((first + (UNROLL - 1)) * (1.0 / UNROLL)) * UNROLL
-    total = filled + jnp.sum(jnp.where(row >= 8, wide, 0.0), axis=0, keepdims=True)
-    ahead = [jnp.zeros((1, 128), jnp.float32)]
-    for r in range(15):
-        ahead.append(ahead[-1] + wide[r : r + 1] if r != 7 else filled)
-    rank = jnp.where(ones > 0, inside + jnp.concatenate(ahead, 0), -1.0).T
-    values = items.T - NOTHING
+
+    def ranks(ones, start):
+        inside = jnp.dot(ones, before, preferred_element_type=jnp.float32)
+        wide = jnp.broadcast_to(jnp.sum(ones, axis=1, keepdims=True), (16, 128))
+        ahead = [start]
+        for r in range(16):
+            ahead.append(ahead[-1] + wide[r : r + 1])
+        return inside + jnp.concatenate(ahead[:16], 0), ahead[16]
+
+    near_rank, count = ranks(near, jnp.zeros((1, 128), jnp.float32))
+    filled = jnp.floor((count + (UNROLL - 1)) * (1.0 / UNROLL)) * UNROLL
+    far_rank, total = ranks(far, filled)
+    rank = jnp.where(near > 0, near_rank, jnp.where(far > 0, far_rank, -1.0)).T
+    values = values - NOTHING
     place = iota(jnp.int32, (128, LIST_MAX), 1).astype(jnp.float32)
     listed = jnp.zeros((128, LIST_MAX), jnp.float32)
     for r in range(16):
@@ -126,13 +153,13 @@
     repeat = lambda v: jnp.concatenate([v] * (LIST_MAX // 128), 1)
     listed = jnp.where(at == LIST_MAX - 2, repeat(filled), listed)
     listed = jnp.where(at == LIST_MAX - 1, repeat(total), listed)
-    return listed.astype(jnp.int32)
+    return listed.astype(jnp.int32), slots
 
 
 def gather_kernel(
     nodes_hbm, weight_hbm, bias_in, bucket_ref, ko_ref, kl_ref, qo_ref, ql_ref,
-    qg_ref, kvg_ref, table_ref, list_ref, bias_ref, m_ref, l_ref, acc_ref,
-    nodes_ref, weight_ref,
+    qg_ref, kn_ref, kf_ref, table_ref, list_ref, bias_ref, m_ref, l_ref, acc_ref,
+    nodes_ref, weight_ref, slots_ref, slots_s, table_s, bias_s, scalar_sem,
     ring_send, ring_recv, pair_send, pair_recv, table_send, table_recv, load_sem, weight_sem,
 ):
     z, y, c = coordinates()
@@ -172,7 +199,7 @@
             if kind == "q":
                 slot = lambda p, r, plan=plan: qg_ref.at[plan, p, r]
             else:
-                slot = lambda p, r, plan=plan: kvg_ref.at[plan, p, c, r]
+                slot = lambda p, r, plan=plan: kf_ref.at[plan, c, r] if p == 3 else kn_ref.at[plan, p, c, r]
             streams.append((len(streams), plan, kind, axis, at, slot))
 
     def send(src, dst, send_sem, recv_sem, device):
@@ -190,8 +217,6 @@
         ).wait_recv()
 
     weight_load.wait()
-    own_at = ((z, y), (y, z))
-
     def project(cluster, carry):
         normed = norm_rows(nodes_ref[pl.ds(cluster * CSIZE, CSIZE), :].astype(jnp.float32)).astype(jnp.bfloat16)
         for i in range(3):
@@ -204,9 +229,9 @@
             for plan in range(2):
                 block = projected[plan * PLAN_FEATURES : (plan + 1) * PLAN_FEATURES]
                 if i == 0:
-                    qg_ref[plan, own_at[plan][0], cluster] = block
+                    qg_ref[plan, 0, cluster] = block
                 else:
-                    kvg_ref[plan, own_at[plan][1], c, cluster, (i - 1) * PLAN_FEATURES : i * PLAN_FEATURES, :] = block
+                    kn_ref[plan, 0, c, cluster, (i - 1) * PLAN_FEATURES : i * PLAN_FEATURES, :] = block
         return carry
 
     ordered = [s for s in streams if s[2] == "kv"] + [s for s in streams if s[2] == "q"]
@@ -218,17 +243,23 @@
             for step in (1, 2, 3):
                 send(table_ref.at[c, z, y], table_ref.at[c, z, y], table_send.at[step - 1], table_recv.at[step - 1], ring_at("y", step))
         for number, plan, kind, axis, at, slot in ordered:
-            for way, first in ((1, 0), (-1, PIECES)):
+            for way, first, seen in ((1, 0, 1), (-1, PIECES, 2)):
                 send(
-                    slot(at, part(p)), slot(at, part(p)),
+                    slot(0, part(p)), slot(seen, part(p)),
                     ring_send.at[number, first + p], ring_recv.at[number, first + p], ring_at(axis, way),
                 )
         if p % (PIECES // 2) == PIECES // 2 - 1:
             h = p // (PIECES // 2)
             for number, plan, kind, axis, at, slot in ordered:
                 if kind == "kv":
-                    send(slot(at, side(h)), slot(at, side(h)), pair_send.at[plan, h], pair_recv.at[plan, h], sibling())
-    list_ref[...] = make_list(qo_ref[...], ql_ref[...], ko_ref[...], kl_ref[...])
+                    send(slot(0, side(h)), slot(0, side(h)), pair_send.at[plan, h], pair_recv.at[plan, h], sibling())
+    listed, slots = make_list(qo_ref[...], ql_ref[...], ko_ref[...], kl_ref[...])
+    list_ref[...] = listed
+    slots_ref[...] = slots
+    m_ref[...] = jnp.full(m_ref.shape, NEVER, jnp.float32)
+    l_ref[...] = jnp.zeros(l_ref.shape, jnp.float32)
+    acc_ref[...] = jnp.zeros(acc_ref.shape, jnp.float32)
+    scalars = [local_copy(slots_ref, slots_s, scalar_sem.at[0]), local_copy(bias_ref, bias_s, scalar_sem.at[1])]
 
     for plan in range(2):
         bias = [bias_ref[plan * PLAN_HEADS + h, :, 0:1] for h in heads]
@@ -237,9 +268,9 @@
             group = [step * UNROLL + u for u in range(UNROLL)]
             pairs = [
                 (
-                    lambda h, i=i: qg_ref[plan, own_at[plan][0], i, rows(h), :],
-                    lambda h, i=i: kvg_ref[plan, own_at[plan][1], c, i, rows(h), :],
-                    lambda h, i=i: kvg_ref[plan, own_at[plan][1], c, i, rows(h, PLAN_FEATURES), :],
+                    lambda h, i=i: qg_ref[plan, 0, i, rows(h), :],
+                    lambda h, i=i: kn_ref[plan, 0, c, i, rows(h), :],
+                    lambda h, i=i: kn_ref[plan, 0, c, i, rows(h, PLAN_FEATURES), :],
                 )
                 for i in group
             ]
@@ -258,34 +289,76 @@
     for h in range(2):
         for p in range(h * PIECES // 2, (h + 1) * PIECES // 2):
             for number, plan, kind, axis, at, slot in ordered:
-                before, after = slot(place(at, -1), part(p)), slot(place(at, 1), part(p))
+                before, after = slot(1, part(p)), slot(2, part(p))
                 arrived(before, ring_recv.at[number, p])
                 arrived(after, ring_recv.at[number, PIECES + p])
                 onward, way = (before, 1) if p % 2 == 0 else (after, -1)
                 far = 2 * PIECES + p
-                send(onward, onward, ring_send.at[number, far], ring_recv.at[number, far], ring_at(axis, way))
+                send(onward, slot(3, part(p)), ring_send.at[number, far], ring_recv.at[number, far], ring_at(axis, way))
         for number, plan, kind, axis, at, slot in ordered:
             if kind == "kv":
                 for index, step in ((1, -1), (2, 1)):
-                    block, sem = slot(place(at, step), side(h)), 2 * index + h
+                    block, sem = slot(index, side(h)), 2 * index + h
                     send(block, block, pair_send.at[plan, sem], pair_recv.at[plan, sem], sibling())
         if h == 0:
             for step in (1, 2, 3):
                 arrived(table_ref.at[c, place(z, -step)], table_recv.at[2 + step])
             send(table_ref.at[c], table_ref.at[c], table_send.at[6], table_recv.at[6], sibling())
-    for h in range(2):
-        for number, plan, kind, axis, at, slot in ordered:
+    arrived(table_ref.at[1 - c], table_recv.at[6])
+    scalars.append(local_copy(table_ref, table_s, scalar_sem.at[2]))
+    for plan in range(2):
+        for index in range(3):
+            for h in range(2):
+                arrived(kn_ref.at[plan, index, 1 - c, side(h)], pair_recv.at[plan, 2 * index + h])
+    for copy in scalars:
+        copy.wait()
+    for plan in range(2):
+
+        def early_tiles(step, carry):
+            group, pairs = [], []
+            for u in range(UNROLL):
+                i = step * UNROLL + u
+                item = slots_s[0, plan * RING * LOCAL + i]
+                valid = item >= 0
+                item = jnp.maximum(item, 0)
+                key = lax.bitwise_and(lax.shift_right_logical(item, 7), 127)
+                tile = lax.bitwise_and(lax.shift_right_logical(item, 14), 1023)
+                worker = lax.shift_right_logical(tile, 5)
+                bucket = table_s[
+                    lax.bitwise_and(worker, 1), lax.shift_right_logical(worker, 3),
+                    lax.bitwise_and(lax.shift_right_logical(worker, 1), 3), 0, lax.bitwise_and(tile, 31),
+                ]
+                bucket = lax.bitwise_and(bucket, 31)
+                place_of = (jnp.minimum(lax.shift_right_logical(key, 4), 2), lax.bitwise_and(lax.shift_right_logical(key, 3), 1), lax.bitwise_and(key, 7))
+                group.append((i, valid, [bias_s[plan * PLAN_HEADS + h, 0, bucket] for h in heads]))
+                pairs.append((
+                    lambda h, i=i: qg_ref[plan, lax.div(i, LOCAL), lax.rem(i, LOCAL), rows(h), :],
+                    lambda h, k=place_of: kn_ref[plan, k[0], k[1], k[2], rows(h), :],
+                    lambda h, k=place_of: kn_ref[plan, k[0], k[1], k[2], rows(h, PLAN_FEATURES), :],
+                ))
+            for (i, valid, bias), (highest, mixed) in zip(group, attend(pairs)):
+                for h in heads:
+                    top = jnp.where(valid, highest[h] + bias[h], NEVER)
+                    old_m, old_l, old_acc = m_ref[plan, i, h : h + 1, :], l_ref[plan, i, h : h + 1, :], acc_ref[plan, i, rows(h), :]
+                    new_m = jnp.maximum(old_m, top)
+                    keep = jnp.exp2(old_m - new_m)
+                    fresh = jnp.where(valid, jnp.exp2(top - new_m), 0.0)
+                    m_ref[plan, i, h : h + 1, :] = new_m
+                    l_ref[plan, i, h : h + 1, :] = old_l * keep + mixed[h][HEAD_SIZE : HEAD_SIZE + 1] * fresh
+                    acc_ref[plan, i, rows(h), :] = old_acc * keep + mixed[h][:HEAD_SIZE] * fresh
+            return carry
+
+        lax.fori_loop(0, 3 * LOCAL // UNROLL, early_tiles, 0)
+        h = plan
+        for number, kv_plan, kind, axis, at, slot in ordered:
             for p in range(h * PIECES // 2, (h + 1) * PIECES // 2):
-                arrived(slot(place(at, 2), part(p)), ring_recv.at[number, 2 * PIECES + p])
+                arrived(slot(3, part(p)), ring_recv.at[number, 2 * PIECES + p])
             if kind == "kv":
-                far = slot(place(at, 2), side(h))
-                send(far, far, pair_send.at[plan, 6 + h], pair_recv.at[plan, 6 + h], sibling())
-    for number, plan, kind, axis, at, slot in streams:
-        if kind == "kv":
-            for index, step in enumerate((0, -1, 1, 2)):
-                for h in range(2):
-                    arrived(kvg_ref.at[plan, place(at, step), 1 - c, side(h)], pair_recv.at[plan, 2 * index + h])
-    arrived(table_ref.at[1 - c], table_recv.at[6])
+                far = slot(3, side(h))
+                send(far, far, pair_send.at[kv_plan, 6 + h], pair_recv.at[kv_plan, 6 + h], sibling())
+    for plan in range(2):
+        for h in range(2):
+            arrived(kf_ref.at[plan, 1 - c, side(h)], pair_recv.at[plan, 6 + h])
     for copy in sent:
         copy.wait_send()
 
@@ -294,12 +367,13 @@
     any_space, in_vmem = pl.BlockSpec(memory_space=pl.ANY), pl.BlockSpec(memory_space=pltpu.VMEM)
     dma, vmem = pltpu.SemaphoreType.DMA, pltpu.VMEM
     q_shape, kv_shape = (PLAN_FEATURES, CSIZE), (2 * PLAN_FEATURES, CSIZE)
-    m_shape, acc_shape = (2, LOCAL, 8, CSIZE), (2, LOCAL, PLAN_FEATURES, CSIZE)
+    m_shape, acc_shape = (2, 3 * LOCAL, 8, CSIZE), (2, 3 * LOCAL, PLAN_FEATURES, CSIZE)
     return pl.pallas_call(
         gather_kernel,
         out_shape=[
             vmem((2, RING, LOCAL) + q_shape, jnp.bfloat16),
-            vmem((2, RING, 2, LOCAL) + kv_shape, jnp.bfloat16),
+            vmem((2, 3, 2, LOCAL) + kv_shape, jnp.bfloat16),
+            vmem((2, 2, LOCAL) + kv_shape, jnp.bfloat16),
             vmem((2, RING, RING, 1, 128), jnp.int32),
             vmem((1, LIST_MAX), jnp.int32),
             vmem((2 * PLAN_HEADS, 1, 128), jnp.float32),
@@ -308,10 +382,15 @@
             vmem(acc_shape, jnp.float32),
         ],
         in_specs=[any_space] * 2 + [in_vmem] * 6,
-        out_specs=[in_vmem] * 8,
+        out_specs=[in_vmem] * 9,
         scratch_shapes=[
             vmem(nodes.shape, jnp.bfloat16),
             vmem(qkv_weight.shape, jnp.bfloat16),
+            vmem((1, 128), jnp.int32),
+            pltpu.SMEM((1, 128), jnp.int32),
+            pltpu.SMEM((2, RING, RING, 1, 128), jnp.int32),
+            pltpu.SMEM((2 * PLAN_HEADS, 1, 128), jnp.float32),
+            dma((3,)),
             dma((4, 3 * PIECES)), dma((4, 3 * PIECES)), dma((2, 8)), dma((2, 8)), dma((7,)), dma((7,)),
             dma((PIECES,)), dma(()),
         ],
@@ -323,45 +402,20 @@
 
 
 def tile_kernel(
-    list_hbm, bias_hbm, table_hbm, m_hbm, l_hbm, acc_hbm, q_ref, kv_ref, part_ref, log_ref,
-    list_ref, bias_ref, table_ref, m_ref, l_ref, acc_ref, table_sem, state_sem,
+    list_hbm, bias_hbm, table_hbm, m0_ref, l0_ref, acc0_ref, q_ref, kn_ref, kf_ref, part_ref, log_ref,
+    list_ref, bias_ref, table_ref, m_ref, l_ref, acc_ref, table_sem,
 ):
     heads = range(PLAN_HEADS)
-    z, y, c = coordinates()
     queries = part_ref.shape[0]
-    keys = 2 * queries
-    waits = ([], [])
-
-    def load(plan, source, target, sem):
-        copy = pltpu.make_async_copy(source, target, sem)
-        copy.start()
-        waits[plan].append(copy)
-
-    load(0, list_hbm, list_ref, table_sem.at[0])
-    load(0, table_hbm, table_ref, table_sem.at[1])
-    load(0, bias_hbm, bias_ref, table_sem.at[2])
-    for plan in range(2):
-        own = (z if plan == 0 else y) + plan * RING
-
-        def clear(group, carry):
-            @pl.when(group != own)
-            def _():
-                side = pl.ds(group * LOCAL, LOCAL)
-                m_ref[side] = jnp.full((LOCAL, 8, CSIZE), NEVER, jnp.float32)
-                l_ref[side] = jnp.zeros((LOCAL, 8, CSIZE), jnp.float32)
-                acc_ref[side] = jnp.zeros((LOCAL, PLAN_FEATURES, CSIZE), jnp.float32)
-            return carry
-
-        side = pl.ds(own * LOCAL, LOCAL)
-        load(plan, m_hbm.at[plan], m_ref.at[side], state_sem.at[plan, 0])
-        load(plan, l_hbm.at[plan], l_ref.at[side], state_sem.at[plan, 1])
-        load(plan, acc_hbm.at[plan], acc_ref.at[side], state_sem.at[plan, 2])
-        lax.fori_loop(plan * RING, (plan + 1) * RING, clear, 0)
-    m_ref[queries] = jnp.full((8, CSIZE), NEVER, jnp.float32)
-    l_ref[queries] = jnp.zeros((8, CSIZE), jnp.float32)
-    acc_ref[queries] = jnp.zeros((PLAN_FEATURES, CSIZE), jnp.float32)
-
-    def batch(step, carry):
+    waits = []
+    for i, (source, target) in enumerate(((list_hbm, list_ref), (table_hbm, table_ref), (bias_hbm, bias_ref))):
+        waits.append(pltpu.make_async_copy(source, target, table_sem.at[i]))
+        waits[-1].start()
+    m_ref[...] = jnp.full(m_ref.shape, NEVER, jnp.float32)
+    l_ref[...] = jnp.zeros(l_ref.shape, jnp.float32)
+    acc_ref[...] = jnp.zeros(acc_ref.shape, jnp.float32)
+
+    def batch(kv_ref, step, carry):
         items, pairs = [], []
         for u in range(UNROLL):
             item = list_ref[0, step * UNROLL + u]
@@ -369,13 +423,14 @@
             key = lax.bitwise_and(lax.shift_right_logical(item, 7), 127)
             tile = lax.shift_right_logical(item, 14)
             query = jnp.minimum(state, queries - 1)
+            plan = lax.shift_right_logical(query, 5)
+            key = plan * (kv_ref.shape[0] // 2) + key
             worker = lax.shift_right_logical(tile, 5)
             bucket = table_ref[
                 lax.bitwise_and(worker, 1), lax.shift_right_logical(worker, 3),
                 lax.bitwise_and(lax.shift_right_logical(worker, 1), 3), 0, lax.bitwise_and(tile, 31),
             ]
-            first = jnp.where(key >= keys // 2, PLAN_HEADS, 0)
-            items.append((state, [bias_ref[first + h, 0, bucket] for h in heads]))
+            items.append((state, [bias_ref[plan * PLAN_HEADS + h, 0, bucket] for h in heads]))
             pairs.append((
                 lambda h, i=query: q_ref[i, rows(h), :],
                 lambda h, i=key: kv_ref[i, rows(h), :],
@@ -395,38 +450,52 @@
                 acc_ref[state, rows(h), :] = old_acc[h] * keep[h] + mixed[h][:HEAD_SIZE] * fresh[h]
         return carry
 
-    for copy in waits[0]:
+    for copy in waits:
         copy.wait()
     split = lax.div(list_ref[0, LIST_MAX - 2], UNROLL)
-    lax.fori_loop(0, split, batch, 0)
-    for copy in waits[1]:
-        copy.wait()
-    lax.fori_loop(split, lax.div(list_ref[0, LIST_MAX - 1] + UNROLL - 1, UNROLL), batch, 0)
-
-    def finish(group, carry):
+    lax.fori_loop(0, split, functools.partial(batch, kn_ref), 0)
+    lax.fori_loop(
+        split, lax.div(list_ref[0, LIST_MAX - 1] + UNROLL - 1, UNROLL), functools.partial(batch, kf_ref), 0
+    )
+
+    def finish(plan, group, near):
+        base = plan * RING + group
         for local in range(LOCAL):
-            state = group * LOCAL + local
+            state = base * LOCAL + local
             for h in heads:
-                total = l_ref[state, h : h + 1, :]
-                held = total > 0
-                safe = jnp.where(held, total, 1.0)
-                part_ref[group * LOCAL + local % 2 * RING + local // 2, rows(h), :] = (acc_ref[state, rows(h), :] * (1.0 / safe)).astype(jnp.bfloat16)
+                best, total = m_ref[state, h : h + 1, :], l_ref[state, h : h + 1, :]
+                acc = acc_ref[state, rows(h), :]
+                if near:
+                    other = group * LOCAL + local
+                    late, early = best, m0_ref[plan, other, h : h + 1, :]
+                    best = jnp.maximum(late, early)
+                    shares = jnp.exp2(late - best), jnp.exp2(early - best)
+                    total = total * shares[0] + l0_ref[plan, other, h : h + 1, :] * shares[1]
+                    acc = acc * shares[0] + acc0_ref[plan, other, rows(h), :] * shares[1]
+                safe = jnp.where(total > 0, total, 1.0)
+                part_ref[base * LOCAL + local % 2 * RING + local // 2, rows(h), :] = (acc * (1.0 / safe)).astype(jnp.bfloat16)
                 row = local // 2 % 2 * PLAN_HEADS + h
-                log_ref[group, local % 2, local // 4, row : row + 1, :] = m_ref[state, h : h + 1, :] + jnp.log2(safe)
-        return carry
-
-    lax.fori_loop(0, queries // LOCAL, finish, 0)
-
-
-def tiles(items, bias, table, m, l, acc, q_all, kv_all):
-    queries, keys = 2 * RING * LOCAL, 2 * RING * 2 * LOCAL
+                log_ref[base, local % 2, local // 4, row : row + 1, :] = best + jnp.log2(safe)
+
+    for plan in range(2):
+
+        def near_group(group, carry):
+            finish(plan, group, True)
+            return carry
+
+        lax.fori_loop(0, 3, near_group, 0)
+        finish(plan, 3, False)
+
+
+def tiles(items, bias, table, m, l, acc, q_all, kv_near, kv_far):
+    queries, keys = 2 * RING * LOCAL, 2 * 2 * LOCAL
     in_vmem = pl.BlockSpec(memory_space=pltpu.VMEM)
     part_shape = (queries, PLAN_FEATURES, CSIZE)
     log_shape = (2 * RING, 2, 2, 8, CSIZE)
     dma, vmem = pltpu.SemaphoreType.DMA, pltpu.VMEM
     return pl.pallas_call(
         tile_kernel,
-        in_specs=[in_vmem] * 8,
+        in_specs=[in_vmem] * 9,
         out_specs=[in_vmem] * 2,
         scratch_shapes=[
                 pltpu.SMEM((1, LIST_MAX), jnp.int32),
@@ -435,14 +504,15 @@
                 vmem((queries + 1, 8, CSIZE), jnp.float32),
                 vmem((queries + 1, 8, CSIZE), jnp.float32),
                 vmem((queries + 1, PLAN_FEATURES, CSIZE), jnp.float32),
-            dma((3,)), dma((2, 3)),
+            dma((3,)),
         ],
         out_shape=[vmem(part_shape, jnp.bfloat16), vmem(log_shape, jnp.float32)],
         compiler_params=pltpu.CompilerParams(vmem_limit_bytes=16 * 2**20),
         name="tiles",
     )(
         items, bias, table, m, l, acc,
-        q_all.reshape(queries, PLAN_FEATURES, CSIZE), kv_all.reshape(keys, 2 * PLAN_FEATURES, CSIZE),
+        q_all.reshape(queries, PLAN_FEATURES, CSIZE),
+        kv_near.reshape(3 * keys, 2 * PLAN_FEATURES, CSIZE), kv_far.reshape(keys, 2 * PLAN_FEATURES, CSIZE),
     )
 
 
@@ -501,12 +571,12 @@
         lanes = pl.ds(first, count)
         for plan, axis, at in ring:
             for way, step in ways:
-                to, far = ring_at(axis, step), place(at, 2)
+                to, far = ring_at(axis, step), 3
                 back(plan, way, turn, 0, part_ref.at[plan, far, t, half(way), :, lanes], far_part.at[plan, way, t, :, :, lanes], to)
                 back(plan, way, turn, 1, log_ref.at[plan, far, t, way, :, lanes], far_log.at[plan, way, t, :, lanes], to)
         for plan, axis, at in ring:
             for way, step in ways:
-                to, next_at = ring_at(axis, step), place(at, step)
+                to, next_at = ring_at(axis, step), 2 - way
                 back(
                     plan, way, turn, 2, part_ref.at[plan, next_at, t, half(1 - way), :, lanes],
                     part_in.at[plan, way, t, half(1 - way), :, lanes], to,
@@ -524,7 +594,7 @@
             for way, step in ways:
                 arrived(far_part.at[plan, way, t, :, :, lanes], back_recv.at[plan, way, turn, 0])
                 arrived(far_log.at[plan, way, t, :, lanes], back_recv.at[plan, way, turn, 1])
-                one, two = log_ref[plan, place(at, step), t, way, :, span], far_log[plan, way, t, :, span]
+                one, two = log_ref[plan, 2 - way, t, way, :, span], far_log[plan, way, t, :, span]
                 best = jnp.maximum(one, two)
                 shares = [jnp.exp2(one - best), jnp.exp2(two - best)]
                 total = shares[0] + shares[1]
@@ -535,7 +605,7 @@
                     for h in heads:
                         row = to * PLAN_HEADS + h
                         both_part[plan, way, t, to, rows(h), span] = (
-                            part_ref[plan, place(at, step), t, way * 2 + to, rows(h), span].astype(jnp.float32) * shares[0][row : row + 1]
+                            part_ref[plan, 2 - way, t, way * 2 + to, rows(h), span].astype(jnp.float32) * shares[0][row : row + 1]
                             + far_part[plan, way, t, to, rows(h), span].astype(jnp.float32) * shares[1][row : row + 1]
                         ).astype(jnp.bfloat16)
                 to = ring_at(axis, step)
@@ -562,14 +632,14 @@
         for plan, axis, at in ring:
             for to in range(RING):
                 h0 = to // 2
-                logs = [log_ref[plan, at, t, h0, :, span]] + [log_in[plan, way, t, h0, :, span] for way in range(2)]
+                logs = [log_ref[plan, 0, t, h0, :, span]] + [log_in[plan, way, t, h0, :, span] for way in range(2)]
                 best = jnp.maximum(jnp.maximum(logs[0], logs[1]), logs[2])
                 shares = [jnp.exp2(log - best) for log in logs]
                 scale = 1.0 / (shares[0] + shares[1] + shares[2])
                 shares = [share * scale for share in shares]
                 for h in heads:
                     row = to % 2 * PLAN_HEADS + h
-                    total = part_ref[plan, at, t, to, rows(h), span].astype(jnp.float32) * shares[0][row : row + 1]
+                    total = part_ref[plan, 0, t, to, rows(h), span].astype(jnp.float32) * shares[0][row : row + 1]
                     for way in range(2):
                         total += part_in[plan, way, t, to, rows(h), span].astype(jnp.float32) * shares[way + 1][row : row + 1]
                     merged[t, to, rows(h, plan * PLAN_FEATURES), span] = total.astype(jnp.bfloat16)
@@ -696,10 +766,10 @@
     key_owner, key_local, query_owner, query_local, hop_bucket,
 ):
     lists = [array.reshape(8, 128) for array in (key_owner, key_local, query_owner, query_local)]
-    q_all, kv_all, table, items, bias, m, l, acc = gather(
+    q_all, kv_near, kv_far, table, items, bias, m, l, acc = gather(
         *[pltpu.with_memory_space_constraint(a, pltpu.HBM) for a in (nodes, qkv_weight.swapaxes(1, 2))], hop_bias.T, hop_bucket.reshape(1, -1), *lists
     )
-    parts, logs = tiles(items, bias, table, m, l, acc, q_all, kv_all)
+    parts, logs = tiles(items, bias, table, m, l, acc, q_all, kv_near, kv_far)
     return tail(
         parts.reshape(2, RING, 2, RING, PLAN_FEATURES, CSIZE), logs.reshape(2, RING, 2, 2, 8, CSIZE),
         *[pltpu.with_memory_space_constraint(a, pltpu.HBM) for a in (nodes, out_weight, up_weight, down_weight)],

time: 112 us -> 109 us (0.973); the launches traced: 111 us -> 109 us
  Pallas kernels: 110 us -> 108 us
    pallas_call x1, Pallas kernels: 46.3 us -> 38.9 us  [tail(): pl.pallas_call(tail_kernel, out_shape=jax.ShapeDtypeStruct((features, nod...]
    pallas_call x1, Pallas kernels: 48.5 us -> 54.4 us  [gather(): pl.pallas_call(gather_kernel, out_shape=[vmem((2, RING, LOCAL) + q_shape,...]
where the time goes in v7:
time: 109 us
  Pallas kernels  108 us (99%)
    pallas_call x1, Pallas kernels, gather(): pl.pallas_call(gather_kernel, out_shape=[vmem((2, RING, LOCAL) + q_shape,...  54.4 us
    pallas_call x1, Pallas kernels, tail(): pl.pallas_call(tail_kernel, out_shape=jax.ShapeDtypeStruct((features, nod...  38.9 us
    pallas_call x1, Pallas kernels, tiles(): pl.pallas_call(tile_kernel, in_specs=[in_vmem] * 9, out_specs=[in_vmem] *...  15 us

profile of v7, /device:TPU:0, one launch (start us, length us, event | category | flops | bytes accessed | tf_op | source)
XLA Modules:
  0.0 109.3 jit_solution(1826445949429989747)
XLA Ops:
  0.0 54.4 %gather.1 = (bf16[2,4,8,96,256]{4,3,2,1,0:T(8,128)(2,1)S(1)}, bf16[2,3,2,8,192,256]{5,4,3,2,1,0:T(8,128)(2,1)S(1)}, bf16[2,2,8,192,256]{4,3,2,1,0:T(8,128)(2,1)S...) custom-call(bf16[2048,768]{1,0:T(8,128)(2,1)} %nodes_ref.1, ...), custom_call_target="tpu_custom_call" | custom-call | tf_op jit(solution)/shard_map/gather/pallas_call | solution.py:371
  54.5 15.0 %tiles.1 = (bf16[64,96,256]{2,1,0:T(8,128)(2,1)S(1)}, f32[8,2,2,8,256]{4,3,2,1,0:T(8,128)S(1)}) custom-call(s32[1,640]{1,0:T(1,128)S(1)} %get-tuple-element.16.list_hbm, f32[6,1,128]{2,1,0:T(1,128)S(1)} %get-tuple-element.17.bias_hbm, s32[2,4,4,1,128]{4,3,2,1,0:T(1,128)S(1)} %get-tuple-element.18.table_hbm, f32[2,24,8,256]{3,2,1,0:T(8,128)S(1)} %get-tuple-element.19.m0_ref, ...), custom_call_target="tpu_custom_call" | custom-call | tf_op jit(solution)/shard_map/tiles/pallas_call | solution.py:496
  69.4 38.9 %tail.1 = bf16[192,2048]{1,0:T(8,128)(2,1)S(1)} custom-call(bf16[2,4,2,4,96,256]{5,4,3,2,1,0:T(8,128)(2,1)S(1)} %bitcast.17, f32[2,4,2,2,8,256]{5,4,3,2,1,0:T(8,128)S(1)} %bitcast.18, bf16[2048,768]{1,0:T(8,128)(2,1)} %nodes_ref.1, bf16[768,768]{1,0:T(8,128)(2,1)} %wo_hbm.1, bf16[768,3072]{1,0:T(8,128)(2,1)} %up_hbm.1, bf16[3072,768]{1,0:T(8,128)(2,1)} %down_hbm.1), custom_call_target="tpu_custom_call" | custom-call | tf_op jit(solution)/shard_map/tail/pallas_call | solution.py:733
  108.4 0.9 copy.13

commit v8 on v7

--- a/solution.py
+++ b/solution.py
@@ -312,7 +312,7 @@
                 arrived(kn_ref.at[plan, index, 1 - c, side(h)], pair_recv.at[plan, 2 * index + h])
     for copy in scalars:
         copy.wait()
-    for plan in range(2):
+    def early(plan, start, end):
 
         def early_tiles(step, carry):
             group, pairs = [], []
@@ -348,14 +348,23 @@
                     acc_ref[plan, i, rows(h), :] = old_acc * keep + mixed[h][:HEAD_SIZE] * fresh
             return carry
 
-        lax.fori_loop(0, 3 * LOCAL // UNROLL, early_tiles, 0)
-        h = plan
-        for number, kv_plan, kind, axis, at, slot in ordered:
+        lax.fori_loop(start, end, early_tiles, 0)
+
+    def pass_far(h):
+        for number, plan, kind, axis, at, slot in ordered:
             for p in range(h * PIECES // 2, (h + 1) * PIECES // 2):
                 arrived(slot(3, part(p)), ring_recv.at[number, 2 * PIECES + p])
             if kind == "kv":
                 far = slot(3, side(h))
-                send(far, far, pair_send.at[kv_plan, 6 + h], pair_recv.at[kv_plan, 6 + h], sibling())
+                send(far, far, pair_send.at[plan, 6 + h], pair_recv.at[plan, 6 + h], sibling())
+
+    steps = 3 * LOCAL // UNROLL
+    early(0, 0, steps - 1)
+    pass_far(0)
+    early(0, steps - 1, steps)
+    early(1, 0, steps // 2 - 1)
+    pass_far(1)
+    early(1, steps // 2 - 1, steps)
     for plan in range(2):
         for h in range(2):
             arrived(kf_ref.at[plan, 1 - c, side(h)], pair_recv.at[plan, 6 + h])

time: 109 us -> 109 us (level); the launches traced: 109 us -> 107 us
    pallas_call x1, Pallas kernels: 38.9 us -> 42.5 us  [tail(): pl.pallas_call(tail_kernel, out_shape=jax.ShapeDtypeStruct((features, nod...]
    pallas_call x1, Pallas kernels: 15 us -> 11.8 us  [tiles(): pl.pallas_call(tile_kernel, in_specs=[in_vmem] * 9, out_specs=[in_vmem] *...]
    pallas_call x1, Pallas kernels: 54.4 us -> 52.3 us  [gather(): pl.pallas_call(gather_kernel, out_shape=[vmem((2, RING, LOCAL) + q_shape,...]
where the time goes in v8:
time: 109 us; the launch traced here: 107 us
  Pallas kernels  107 us (98%)
    pallas_call x1, Pallas kernels, gather(): pl.pallas_call(gather_kernel, out_shape=[vmem((2, RING, LOCAL) + q_shape,...  52.3 us
    pallas_call x1, Pallas kernels, tail(): pl.pallas_call(tail_kernel, out_shape=jax.ShapeDtypeStruct((features, nod...  42.5 us
    pallas_call x1, Pallas kernels, tiles(): pl.pallas_call(tile_kernel, in_specs=[in_vmem] * 9, out_specs=[in_vmem] *...  11.8 us

profile of v8, /device:TPU:0, one launch (start us, length us, event | category | flops | bytes accessed | tf_op | source)
XLA Modules:
  0.0 107.5 jit_solution(3869609204821233540)
XLA Ops:
  0.0 52.3 %gather.1 = (bf16[2,4,8,96,256]{4,3,2,1,0:T(8,128)(2,1)S(1)}, bf16[2,3,2,8,192,256]{5,4,3,2,1,0:T(8,128)(2,1)S(1)}, bf16[2,2,8,192,256]{4,3,2,1,0:T(8,128)(2,1)S...) custom-call(bf16[2048,768]{1,0:T(8,128)(2,1)} %nodes_ref.1, ...), custom_call_target="tpu_custom_call" | custom-call | tf_op jit(solution)/shard_map/gather/pallas_call | solution.py:380
  52.3 11.8 %tiles.1 = (bf16[64,96,256]{2,1,0:T(8,128)(2,1)S(1)}, f32[8,2,2,8,256]{4,3,2,1,0:T(8,128)S(1)}) custom-call(s32[1,640]{1,0:T(1,128)S(1)} %get-tuple-element.16.list_hbm, f32[6,1,128]{2,1,0:T(1,128)S(1)} %get-tuple-element.17.bias_hbm, s32[2,4,4,1,128]{4,3,2,1,0:T(1,128)S(1)} %get-tuple-element.18.table_hbm, f32[2,24,8,256]{3,2,1,0:T(8,128)S(1)} %get-tuple-element.19.m0_ref, ...), custom_call_target="tpu_custom_call" | custom-call | tf_op jit(solution)/shard_map/tiles/pallas_call | solution.py:505
  64.1 42.5 %tail.1 = bf16[192,2048]{1,0:T(8,128)(2,1)S(1)} custom-call(bf16[2,4,2,4,96,256]{5,4,3,2,1,0:T(8,128)(2,1)S(1)} %bitcast.17, f32[2,4,2,2,8,256]{5,4,3,2,1,0:T(8,128)S(1)} %bitcast.18, bf16[2048,768]{1,0:T(8,128)(2,1)} %nodes_ref.1, bf16[768,768]{1,0:T(8,128)(2,1)} %wo_hbm.1, bf16[768,3072]{1,0:T(8,128)(2,1)} %up_hbm.1, bf16[3072,768]{1,0:T(8,128)(2,1)} %down_hbm.1), custom_call_target="tpu_custom_call" | custom-call | tf_op jit(solution)/shard_map/tail/pallas_call | solution.py:742
  106.6 0.9 copy.13

commit v9 on v8

--- a/solution.py
+++ b/solution.py
@@ -276,9 +276,9 @@
             ]
             for i, (highest, mixed) in zip(group, attend(pairs)):
                 for h in heads:
-                    m_ref[plan, i, h : h + 1, :] = highest[h] + bias[h]
-                    l_ref[plan, i, h : h + 1, :] = mixed[h][HEAD_SIZE : HEAD_SIZE + 1]
-                    acc_ref[plan, i, rows(h), :] = mixed[h][:HEAD_SIZE]
+                    m_ref[plan * RING * LOCAL + i, h : h + 1, :] = highest[h] + bias[h]
+                    l_ref[plan * RING * LOCAL + i, h : h + 1, :] = mixed[h][HEAD_SIZE : HEAD_SIZE + 1]
+                    acc_ref[plan * RING * LOCAL + i, rows(h), :] = mixed[h][:HEAD_SIZE]
             return carry
 
         lax.fori_loop(0, LOCAL // UNROLL, own_tiles, 0)
@@ -339,13 +339,13 @@
             for (i, valid, bias), (highest, mixed) in zip(group, attend(pairs)):
                 for h in heads:
                     top = jnp.where(valid, highest[h] + bias[h], NEVER)
-                    old_m, old_l, old_acc = m_ref[plan, i, h : h + 1, :], l_ref[plan, i, h : h + 1, :], acc_ref[plan, i, rows(h), :]
+                    old_m, old_l, old_acc = m_ref[plan * RING * LOCAL + i, h : h + 1, :], l_ref[plan * RING * LOCAL + i, h : h + 1, :], acc_ref[plan * RING * LOCAL + i, rows(h), :]
                     new_m = jnp.maximum(old_m, top)
                     keep = jnp.exp2(old_m - new_m)
                     fresh = jnp.where(valid, jnp.exp2(top - new_m), 0.0)
-                    m_ref[plan, i, h : h + 1, :] = new_m
-                    l_ref[plan, i, h : h + 1, :] = old_l * keep + mixed[h][HEAD_SIZE : HEAD_SIZE + 1] * fresh
-                    acc_ref[plan, i, rows(h), :] = old_acc * keep + mixed[h][:HEAD_SIZE] * fresh
+                    m_ref[plan * RING * LOCAL + i, h : h + 1, :] = new_m
+                    l_ref[plan * RING * LOCAL + i, h : h + 1, :] = old_l * keep + mixed[h][HEAD_SIZE : HEAD_SIZE + 1] * fresh
+                    acc_ref[plan * RING * LOCAL + i, rows(h), :] = old_acc * keep + mixed[h][:HEAD_SIZE] * fresh
             return carry
 
         lax.fori_loop(start, end, early_tiles, 0)
@@ -376,7 +376,8 @@
     any_space, in_vmem = pl.BlockSpec(memory_space=pl.ANY), pl.BlockSpec(memory_space=pltpu.VMEM)
     dma, vmem = pltpu.SemaphoreType.DMA, pltpu.VMEM
     q_shape, kv_shape = (PLAN_FEATURES, CSIZE), (2 * PLAN_FEATURES, CSIZE)
-    m_shape, acc_shape = (2, 3 * LOCAL, 8, CSIZE), (2, 3 * LOCAL, PLAN_FEATURES, CSIZE)
+    states = 2 * RING * LOCAL + 1
+    m_shape, acc_shape = (states, 8, CSIZE), (states, PLAN_FEATURES, CSIZE)
     return pl.pallas_call(
         gather_kernel,
         out_shape=[
@@ -404,15 +405,15 @@
             dma((PIECES,)), dma(()),
         ],
         compiler_params=pltpu.CompilerParams(
-            collective_id=0, has_side_effects=True, vmem_limit_bytes=42 * 2**20
+            collective_id=0, has_side_effects=True, vmem_limit_bytes=36 * 2**20
         ),
         name="gather",
     )(nodes, qkv_weight, bias, bucket, key_owner, key_local, query_owner, query_local)
 
 
 def tile_kernel(
-    list_hbm, bias_hbm, table_hbm, m0_ref, l0_ref, acc0_ref, q_ref, kn_ref, kf_ref, part_ref, log_ref,
-    list_ref, bias_ref, table_ref, m_ref, l_ref, acc_ref, table_sem,
+    list_hbm, bias_hbm, table_hbm, m_in, l_in, acc_in, q_ref, kn_ref, kf_ref,
+    part_ref, log_ref, m_ref, l_ref, acc_ref, list_ref, bias_ref, table_ref, table_sem,
 ):
     heads = range(PLAN_HEADS)
     queries = part_ref.shape[0]
@@ -420,9 +421,6 @@
     for i, (source, target) in enumerate(((list_hbm, list_ref), (table_hbm, table_ref), (bias_hbm, bias_ref))):
         waits.append(pltpu.make_async_copy(source, target, table_sem.at[i]))
         waits[-1].start()
-    m_ref[...] = jnp.full(m_ref.shape, NEVER, jnp.float32)
-    l_ref[...] = jnp.zeros(l_ref.shape, jnp.float32)
-    acc_ref[...] = jnp.zeros(acc_ref.shape, jnp.float32)
 
     def batch(kv_ref, step, carry):
         items, pairs = [], []
@@ -467,33 +465,20 @@
         split, lax.div(list_ref[0, LIST_MAX - 1] + UNROLL - 1, UNROLL), functools.partial(batch, kf_ref), 0
     )
 
-    def finish(plan, group, near):
-        base = plan * RING + group
+    def finish(group, carry):
         for local in range(LOCAL):
-            state = base * LOCAL + local
+            state = group * LOCAL + local
             for h in heads:
-                best, total = m_ref[state, h : h + 1, :], l_ref[state, h : h + 1, :]
-                acc = acc_ref[state, rows(h), :]
-                if near:
-                    other = group * LOCAL + local
-                    late, early = best, m0_ref[plan, other, h : h + 1, :]
-                    best = jnp.maximum(late, early)
-                    shares = jnp.exp2(late - best), jnp.exp2(early - best)
-                    total = total * shares[0] + l0_ref[plan, other, h : h + 1, :] * shares[1]
-                    acc = acc * shares[0] + acc0_ref[plan, other, rows(h), :] * shares[1]
+                total = l_ref[state, h : h + 1, :]
                 safe = jnp.where(total > 0, total, 1.0)
-                part_ref[base * LOCAL + local % 2 * RING + local // 2, rows(h), :] = (acc * (1.0 / safe)).astype(jnp.bfloat16)
+                part_ref[group * LOCAL + local % 2 * RING + local // 2, rows(h), :] = (
+                    acc_ref[state, rows(h), :] * (1.0 / safe)
+                ).astype(jnp.bfloat16)
                 row = local // 2 % 2 * PLAN_HEADS + h
-                log_ref[base, local % 2, local // 4, row : row + 1, :] = best + jnp.log2(safe)
-
-    for plan in range(2):
-
-        def near_group(group, carry):
-            finish(plan, group, True)
-            return carry
-
-        lax.fori_loop(0, 3, near_group, 0)
-        finish(plan, 3, False)
+                log_ref[group, local % 2, local // 4, row : row + 1, :] = m_ref[state, h : h + 1, :] + jnp.log2(safe)
+        return carry
+
+    lax.fori_loop(0, queries // LOCAL, finish, 0)
 
 
 def tiles(items, bias, table, m, l, acc, q_all, kv_near, kv_far):
@@ -505,18 +490,17 @@
     return pl.pallas_call(
         tile_kernel,
         in_specs=[in_vmem] * 9,
-        out_specs=[in_vmem] * 2,
+        out_specs=[in_vmem] * 5,
+        input_output_aliases={3: 2, 4: 3, 5: 4},
         scratch_shapes=[
-                pltpu.SMEM((1, LIST_MAX), jnp.int32),
-                pltpu.SMEM((2 * PLAN_HEADS, 1, 128), jnp.float32),
-                pltpu.SMEM((2, RING, RING, 1, 128), jnp.int32),
-                vmem((queries + 1, 8, CSIZE), jnp.float32),
-                vmem((queries + 1, 8, CSIZE), jnp.float32),
-                vmem((queries + 1, PLAN_FEATURES, CSIZE), jnp.float32),
+            pltpu.SMEM((1, LIST_MAX), jnp.int32),
+            pltpu.SMEM((2 * PLAN_HEADS, 1, 128), jnp.float32),
+            pltpu.SMEM((2, RING, RING, 1, 128), jnp.int32),
             dma((3,)),
         ],
-        out_shape=[vmem(part_shape, jnp.bfloat16), vmem(log_shape, jnp.float32)],
-        compiler_params=pltpu.CompilerParams(vmem_limit_bytes=16 * 2**20),
+        out_shape=[vmem(part_shape, jnp.bfloat16), vmem(log_shape, jnp.float32)]
+        + [vmem(state.shape, jnp.float32) for state in (m, l, acc)],
+        compiler_params=pltpu.CompilerParams(vmem_limit_bytes=8 * 2**20),
         name="tiles",
     )(
         items, bias, table, m, l, acc,
@@ -764,7 +748,7 @@
             dma((3, 3)), dma((3, 3)), dma((3, 3)), dma((3, 3)), dma((3,)),
         ],
         compiler_params=pltpu.CompilerParams(
-            collective_id=1, has_side_effects=True, vmem_limit_bytes=32 * 2**20
+            collective_id=1, has_side_effects=True, vmem_limit_bytes=36 * 2**20
         ),
         name="tail",
     )(parts, logs, nodes, out_weight, up_weight, down_weight)
@@ -778,7 +762,7 @@
     q_all, kv_near, kv_far, table, items, bias, m, l, acc = gather(
         *[pltpu.with_memory_space_constraint(a, pltpu.HBM) for a in (nodes, qkv_weight.swapaxes(1, 2))], hop_bias.T, hop_bucket.reshape(1, -1), *lists
     )
-    parts, logs = tiles(items, bias, table, m, l, acc, q_all, kv_near, kv_far)
+    parts, logs, *_ = tiles(items, bias, table, m, l, acc, q_all, kv_near, kv_far)
     return tail(
         parts.reshape(2, RING, 2, RING, PLAN_FEATURES, CSIZE), logs.reshape(2, RING, 2, 2, 8, CSIZE),
         *[pltpu.with_memory_space_constraint(a, pltpu.HBM) for a in (nodes, out_weight, up_weight, down_weight)],

time: 109 us -> 107 us (0.982)
  the two profiles are of different devices: /device:TPU:0 before, /device:TPU:1 now
where the time goes in v9:
time: 107 us; the launch traced here: 106 us
  Pallas kernels  106 us (99%)
    pallas_call x1, Pallas kernels, gather(): pl.pallas_call(gather_kernel, out_shape=[vmem((2, RING, LOCAL) + q_shape,...  53.6 us
    pallas_call x1, Pallas kernels, tail(): pl.pallas_call(tail_kernel, out_shape=jax.ShapeDtypeStruct((features, nod...  39.7 us
    pallas_call x1, Pallas kernels, tiles(): pl.pallas_call(tile_kernel, in_specs=[in_vmem] * 9, out_specs=[in_vmem] *...  12.2 us

profile of v9, /device:TPU:1, one launch (start us, length us, event | category | flops | bytes accessed | tf_op | source)
XLA Modules:
  0.0 106.5 jit_solution(4684222841525739016)
XLA Ops:
  0.0 53.6 %gather.1 = (bf16[2,4,8,96,256]{4,3,2,1,0:T(8,128)(2,1)S(1)}, bf16[2,3,2,8,192,256]{5,4,3,2,1,0:T(8,128)(2,1)S(1)}, bf16[2,2,8,192,256]{4,3,2,1,0:T(8,128)(2,1)S...) custom-call(bf16[2048,768]{1,0:T(8,128)(2,1)} %nodes_ref.1, ...), custom_call_target="tpu_custom_call" | custom-call | tf_op jit(solution)/shard_map/gather/pallas_call | solution.py:381
  53.6 12.2 %tiles.1 = (bf16[64,96,256]{2,1,0:T(8,128)(2,1)S(1)}, f32[8,2,2,8,256]{4,3,2,1,0:T(8,128)S(1)}, f32[65,8,256]{2,1,0:T(8,128)S(1)}, f32[65,8,256]{2,1,0:T(8,128)S(1)}, f32[65,96,256]{2,1,0:T(8,128)S(1)}) custom-call(s32[1,640]{1,0:T(1,128)S(1)} %get-tuple-element.16.list_hbm, ...), custom_call_target="tpu_custom_call", output_to_operand_aliasing={{2}: (3, {}), {3}: (4, {}), {4}: (5, {})} | custom-call | tf_op jit(solution)/shard_map/tiles/pallas_call | solution.py:490
  65.9 39.7 %tail.1 = bf16[192,2048]{1,0:T(8,128)(2,1)S(1)} custom-call(bf16[2,4,2,4,96,256]{5,4,3,2,1,0:T(8,128)(2,1)S(1)} %bitcast.17, f32[2,4,2,2,8,256]{5,4,3,2,1,0:T(8,128)S(1)} %bitcast.18, bf16[2048,768]{1,0:T(8,128)(2,1)} %nodes_ref.1, bf16[768,768]{1,0:T(8,128)(2,1)} %wo_hbm.1, bf16[768,3072]{1,0:T(8,128)(2,1)} %up_hbm.1, bf16[3072,768]{1,0:T(8,128)(2,1)} %down_hbm.1), custom_call_target="tpu_custom_call" | custom-call | tf_op jit(solution)/shard_map/tail/pallas_call | solution.py:726
  105.6 0.9 copy.19

commit v10 on v9

--- a/solution.py
+++ b/solution.py
@@ -295,11 +295,10 @@
                 onward, way = (before, 1) if p % 2 == 0 else (after, -1)
                 far = 2 * PIECES + p
                 send(onward, slot(3, part(p)), ring_send.at[number, far], ring_recv.at[number, far], ring_at(axis, way))
-        for number, plan, kind, axis, at, slot in ordered:
-            if kind == "kv":
-                for index, step in ((1, -1), (2, 1)):
-                    block, sem = slot(index, side(h)), 2 * index + h
-                    send(block, block, pair_send.at[plan, sem], pair_recv.at[plan, sem], sibling())
+                if kind == "kv" and p % (PIECES // 2) == PIECES // 2 - 1:
+                    for index in (1, 2):
+                        block, sem = slot(index, side(h)), 2 * index + h
+                        send(block, block, pair_send.at[plan, sem], pair_recv.at[plan, sem], sibling())
         if h == 0:
             for step in (1, 2, 3):
                 arrived(table_ref.at[c, place(z, -step)], table_recv.at[2 + step])

time: 107 us -> 108 us (level)
  the two profiles are of different devices: /device:TPU:1 before, /device:TPU:0 now
where the time goes in v10:
time: 108 us; the launch traced here: 107 us
  Pallas kernels  106 us (98%)
    pallas_call x1, Pallas kernels, gather(): pl.pallas_call(gather_kernel, out_shape=[vmem((2, RING, LOCAL) + q_shape,...  52.3 us
    pallas_call x1, Pallas kernels, tail(): pl.pallas_call(tail_kernel, out_shape=jax.ShapeDtypeStruct((features, nod...  43.3 us
    pallas_call x1, Pallas kernels, tiles(): pl.pallas_call(tile_kernel, in_specs=[in_vmem] * 9, out_specs=[in_vmem] *...  10.1 us

profile of v10, /device:TPU:0, one launch (start us, length us, event | category | flops | bytes accessed | tf_op | source)
XLA Modules:
  0.0 106.6 jit_solution(14711246009104733067)
XLA Ops:
  0.0 52.3 %gather.1 = (bf16[2,4,8,96,256]{4,3,2,1,0:T(8,128)(2,1)S(1)}, bf16[2,3,2,8,192,256]{5,4,3,2,1,0:T(8,128)(2,1)S(1)}, bf16[2,2,8,192,256]{4,3,2,1,0:T(8,128)(2,1)S...) custom-call(bf16[2048,768]{1,0:T(8,128)(2,1)} %nodes_ref.1, ...), custom_call_target="tpu_custom_call" | custom-call | tf_op jit(solution)/shard_map/gather/pallas_call | solution.py:380
  52.3 10.1 %tiles.1 = (bf16[64,96,256]{2,1,0:T(8,128)(2,1)S(1)}, f32[8,2,2,8,256]{4,3,2,1,0:T(8,128)S(1)}, f32[65,8,256]{2,1,0:T(8,128)S(1)}, f32[65,8,256]{2,1,0:T(8,128)S(1)}, f32[65,96,256]{2,1,0:T(8,128)S(1)}) custom-call(s32[1,640]{1,0:T(1,128)S(1)} %get-tuple-element.16.list_hbm, ...), custom_call_target="tpu_custom_call", output_to_operand_aliasing={{2}: (3, {}), {3}: (4, {}), {4}: (5, {})} | custom-call | tf_op jit(solution)/shard_map/tiles/pallas_call | solution.py:489
  62.4 43.3 %tail.1 = bf16[192,2048]{1,0:T(8,128)(2,1)S(1)} custom-call(bf16[2,4,2,4,96,256]{5,4,3,2,1,0:T(8,128)(2,1)S(1)} %bitcast.17, f32[2,4,2,2,8,256]{5,4,3,2,1,0:T(8,128)S(1)} %bitcast.18, bf16[2048,768]{1,0:T(8,128)(2,1)} %nodes_ref.1, bf16[768,768]{1,0:T(8,128)(2,1)} %wo_hbm.1, bf16[768,3072]{1,0:T(8,128)(2,1)} %up_hbm.1, bf16[3072,768]{1,0:T(8,128)(2,1)} %down_hbm.1), custom_call_target="tpu_custom_call" | custom-call | tf_op jit(solution)/shard_map/tail/pallas_call | solution.py:725
  105.7 0.9 copy.19
